TPU v7x, 256 devices: a whole 4x4x8 slice. The times are simulated.
256 devices in a mesh: queue: 32 (over z_hi, y, core), head: 8 (over z_lo, x).
Axes of the slice: x: 4, y: 4, z: 8 (z_hi: 4, z_lo: 2; z = z_hi * 2 + z_lo), core: 2. Of those that a mesh axis runs over, the one named last changes fastest.
Arguments:
- latents: bfloat16 [9216, 3072], P('queue'), may hold values from -6 to 6
- levels: int32 [32], P('queue'), may hold values from 0 to 15
- counts: int32 [32], replicated, may hold values from 72 to 288, as said below
- window_mask: int32 [32, 2], replicated, may hold values 0 or 1
- modulation: float32 [16, 9216], replicated, may hold values from -1 to 25, as said below
- qkv_weight: bfloat16 [3072, 3, 3072], P(None, None, 'head'), may hold values from -0.109375 to 0.109375
- out_weight: bfloat16 [3072, 3072], P('head'), may hold values from -0.109375 to 0.109375
Outputs:
- queue_next: bfloat16 [9216, 3072], P('queue')
Inputs may be any that keep to these rules, and one draw needn't show every extreme that they name: `counts`: at least one span has exactly 288 valid tokens and at least one has 72. `modulation`: gates and shifts lie in -1 to 1.5; scales of some levels may be large.
All inputs are finite; a program needn't handle non-finite values.
Results may differ from a plain program's by a relative error of at most 0.03.
The roundings to bfloat16 on the way count: a program that leaves them out, or rounds other values in their place, can miss the bound.
Values may be sent and summed in bfloat16 or wider, within the bound.
No kernel may reach another device: no remote copies, remote signals or barrier semaphores. Data moves between devices by JAX's collectives and lax.ppermute only.
A program may use at most 128 MiB of HBM per device.

v0:
```python
import math

import jax
import jax.numpy as jnp
from jax import lax
from jax.sharding import PartitionSpec as P

HD = 128


def padded_2(cells, sides, width):
    for axis, dim in sides:
        count = lax.axis_size(axis)
        ends = count - 1
        head = lax.slice_in_dim(cells, 0, width, axis=dim)
        tail = lax.slice_in_dim(cells, cells.shape[dim] - width, cells.shape[dim], axis=dim)
        cells = jnp.concatenate(
            [
                lax.ppermute(tail, axis, [(i, (i + 1) % count) for i in range(ends)]),
                cells,
                lax.ppermute(head, axis, [((i + 1) % count, i) for i in range(ends)]),
            ],
            axis=dim,
        )
    return cells


def shifted(block, axis, distance):
    devices = range(lax.axis_size(axis))
    route = [((i - distance) % len(devices), i) for i in devices]
    return lax.ppermute(block, axis, route)


def normalize(rows, shift, scale):
    mean = jnp.mean(rows, axis=-1, keepdims=True)
    centered = rows - mean
    variance = jnp.mean(centered * centered, axis=-1, keepdims=True)
    return centered / jnp.sqrt(variance + 1e-06) * (1.0 + scale) + shift


def pick_value(table, spot):
    places = jnp.arange(table.shape[0])
    return jnp.sum(jnp.where(places == spot, table, 0))


def body(latents, levels, counts, window_mask, modulation, qkv_weight, out_weight):
    rows, width = latents.shape
    widthq = qkv_weight.shape[2]
    local_heads = widthq // HD
    place = lax.axis_index("queue")
    onehot = (jnp.arange(modulation.shape[0]) == levels[0]).astype(jnp.float32)
    table = jnp.dot(onehot[None, :], modulation, precision=lax.Precision.HIGHEST)
    shift = table[:, :width]
    scale = table[:, width : 2 * width]
    gate = table[:, 2 * width :]
    latent_rows = latents.astype(jnp.float32)
    normed = normalize(latent_rows, shift, scale).astype(jnp.bfloat16)
    qkv = jnp.dot(normed, qkv_weight.reshape(width, 3 * widthq), preferred_element_type=jnp.float32)
    qkv = qkv.astype(jnp.bfloat16).reshape(rows, 3, widthq)
    query = qkv[:, 0]
    padded = padded_2(qkv[:, 1:3], (("queue", 0),), rows)
    keys = padded[:, 0]
    values = padded[:, 1]
    self_limit = pick_value(counts, place)
    prev_limit = pick_value(counts, place - 1) * pick_value(window_mask[:, 0], place)
    next_limit = pick_value(counts, place + 1) * pick_value(window_mask[:, 1], place)
    scores = jnp.einsum(
        "thd,shd->hts",
        query.reshape(rows, local_heads, HD),
        keys.reshape(3 * rows, local_heads, HD),
        preferred_element_type=jnp.float32,
    ) / math.sqrt(HD)
    spots = jnp.arange(3 * rows)
    limit = jnp.where(
        spots // rows == 0, prev_limit, jnp.where(spots // rows == 1, self_limit, next_limit)
    )
    valid = spots % rows < limit
    scores = jnp.where(valid[None, None, :], scores, -jnp.inf)
    top = jnp.max(scores, axis=-1, keepdims=True)
    expo = jnp.exp(scores - top)
    weights = (expo / jnp.sum(expo, axis=-1, keepdims=True)).astype(jnp.bfloat16)
    attended = jnp.einsum(
        "hts,shd->thd",
        weights,
        values.reshape(3 * rows, local_heads, HD),
        preferred_element_type=jnp.float32,
    )
    attended = attended.astype(jnp.bfloat16).reshape(rows, widthq)
    partial_sum = jnp.dot(attended, out_weight, preferred_element_type=jnp.float32)
    partial_sum = partial_sum.astype(jnp.bfloat16).astype(jnp.float32)
    projected = lax.psum(partial_sum.astype(jnp.bfloat16), "head").astype(jnp.float32)
    updated = (latent_rows + gate * projected).astype(jnp.bfloat16)
    return shifted(updated, "queue", -1)


def solution(mesh):
    in_specs = (P("queue", None), P("queue"), P(), P(), P(), P(None, None, "head"), P("head", None))
    out_specs = P("queue", None)
    return jax.shard_map(body, mesh=mesh, in_specs=in_specs, out_specs=out_specs, check_vma=False)
```

profile of v0, /device:TPU:89, one launch (start us, length us, event | category | flops | bytes accessed | tf_op | source)
XLA Modules:
  0.0 214.9 jit_solution(12551029663866733434)
XLA Ops:
  6.5 0.0 copy-start
  6.5 0.0 copy-start.2
  6.5 0.0 all-reduce.2.cloned.1.call-start
  6.5 10.4 %copy.8 = bf16[3072,3,384]{0,2,1:T(8,128)(2,1)} copy(bf16[3072,3,384]{2,0,1:T(8,128)(2,1)} %param.12) | data formatting | bytes 14155776 | tf_op args[5]
  17.0 0.0 copy-start.1
  17.8 0.0 copy-done.2
  17.8 0.3 fusion.41
  18.1 1.8 convert_reduce_fusion
  19.9 0.0 copy-done.1
  19.9 0.6 fusion.3
  20.6 0.0 copy-start.3
  20.6 0.0 copy-start.4
  20.6 6.6 %convolution_convert_fusion.1 = bf16[288,1152]{1,0:T(8,128)(2,1)} fusion(bf16[3072,1152]{0,1:T(8,128)(2,1)} %bitcast.53, bf16[288,3072]{1,0:T(8,128)(2,1)S(1)} %copy-done.1, f32[3072]{0:T(1024)S(1)} %bitcast.58, f32[3072]{0:T(1024)S(1)} %bitcast.57, f32[288]{0:T(512)S(1)} %add_sqrt_fusion, f32[288]{0:T(512)S(1)} %broadcast_multiply_fusion), kind=kOutput, calls=%fused_computation.15 | convolution fusion | flops 2044071936 | bytes 9537792 | tf_op jit(solution)/shard_map/dot_general | solution.py:58
  27.2 2.2 %reshape.50 = bf16[288,3,384]{2,1,0:T(4,128)(2,1)S(1)} reshape(bf16[288,1152]{1,0:T(8,128)(2,1)} %convolution_convert_fusion.1) | data formatting | bytes 1327104 | tf_op jit(solution)/shard_map/reshape | solution.py:59
  29.5 1.2 slice.39
  30.7 2.6 %collective-permute-start.1 = (bf16[288,2,384]{2,1,0:T(2,128)(2,1)}, bf16[288,2,384]{2,1,0:T(2,128)(2,1)}, u32[]{:S(2)}, u32[]{:S(2)}) collective-permute-start(bf16[288,2,384]{2,1,0:T(2,128)(2,1)} %slice.39), channel_id=1, source_target_pairs={{8,0},{16,8},{24,16},{32,24},{40,32},{48,40},{56,48},{64,56},{72,6... | collective-permute-start | bytes 1327112 | tf_op jit(solution)/shard_map/ppermute | solution.py:21
  33.3 7.4 %collective-permute-start = (bf16[288,2,384]{2,1,0:T(2,128)(2,1)}, bf16[288,2,384]{2,1,0:T(2,128)(2,1)}, u32[]{:S(2)}, u32[]{:S(2)}) collective-permute-start(bf16[288,2,384]{2,1,0:T(2,128)(2,1)} %slice.39), channel_id=1, source_target_pairs={{0,8},{8,16},{16,24},{24,32},{32,40},{40,48},{48,56},{56,64},{64,7... | collective-permute-start | bytes 1327112 | tf_op jit(solution)/shard_map/ppermute | solution.py:19
  40.7 0.0 copy-done.3
  40.7 0.0 copy-done.4
  40.7 0.8 fusion.44
  44.0 0.6 fusion.35
  44.6 1.3 slice_reduce_fusion
  45.9 3.7 %collective-permute-done.1 = bf16[288,2,384]{2,1,0:T(2,128)(2,1)} collective-permute-done((bf16[288,2,384]{2,1,0:T(2,128)(2,1)}, bf16[288,2,384]{2,1,0:T(2,128)(2,1)}, u32[]{:S(2)}, u32[]{:S(2)}) %collective-permute-start.1) | collective-permute-done | bytes 442400 | tf_op jit(solution)/shard_map/ppermute | solution.py:21
  49.6 1.2 collective-permute-done
  50.7 3.4 %pad_maximum_fusion = bf16[864,2,384]{2,1,0:T(2,128)(2,1)S(1)} fusion(bf16[288,2,384]{2,1,0:T(2,128)(2,1)} %collective-permute-done.1, bf16[288,2,384]{2,1,0:T(2,128)(2,1)} %slice.39, bf16[288,2,384]{2,1,0:T(2,128)(2,1)} %collective-permute-done), kind=kLoop, calls=%fused_computation.25 | loop fusion | flops 1327104 | bytes 2654208 | tf_op jit(solution)/shard_map/concatenate | solution.py:17
  54.1 3.3 %fusion.52 = (bf16[864,1,384]{2,1,0:T(2,128)(2,1)}, bf16[864,1,384]{2,1,0:T(2,128)(2,1)}) fusion(bf16[864,2,384]{2,1,0:T(2,128)(2,1)S(1)} %pad_maximum_fusion), kind=kLoop, calls=%fused_computation.68 | loop fusion | bytes 2654208 | tf_op jit(solution)/shard_map/slice | solution.py:62
  57.5 3.6 %copy.9 = bf16[864,1,384]{0,2,1:T(8,128)(2,1)S(1)} copy(bf16[864,1,384]{2,1,0:T(2,128)(2,1)} %get-tuple-element.11) | data formatting | bytes 1327104 | tf_op jit(solution)/shard_map/slice | solution.py:63
  61.0 4.6 %copy.10 = bf16[864,1,384]{0,2,1:T(8,128)(2,1)} copy(bf16[864,1,384]{2,1,0:T(2,128)(2,1)} %get-tuple-element.10) | data formatting | bytes 1327104 | tf_op jit(solution)/shard_map/slice | solution.py:62
  65.6 3.8 %fusion.54 = (f32[3,288]{1,0:T(4,128)S(1)}, f32[3,288,864]{2,1,0:T(8,128)}) fusion(pred[864]{0:T(1024)(128)(4,1)S(1)} %fusion.35, bf16[864,3,128]{0,2,1:T(8,128)(2,1)} %bitcast.55, bf16[288,384]{1,0:T(8,128)(2,1)S(1)} %slice_reduce_fusion), kind=kOutput, calls=%fused_computation.70 | convolution fusion | flops 194089824 | bytes 3875040 | tf_op jit(solution)/shard_map/sub | solution.py:80
  69.5 2.5 %fusion.19 = bf16[3,36,8,128]{3,2,1,0:T(8,128)(2,1)S(1)} fusion(bf16[864,3,128]{0,2,1:T(8,128)(2,1)S(1)} %bitcast.54, f32[3,288,864]{2,1,0:T(8,128)} %get-tuple-element.16, f32[3,288]{1,0:T(4,128)S(1)} %get-tuple-element.15), kind=kOutput, calls=%fused_computation.27 | convolution fusion | flops 192706560 | bytes 3874176 | tf_op jit(solution)/shard_map/hts,shd->thd/dot_general | solution.py:82
  72.0 0.0 copy-done
  72.0 2.3 %convolution_convert_fusion = bf16[288,3072]{1,0:T(8,128)(2,1)} fusion(bf16[384,3072]{1,0:T(8,128)(2,1)S(1)} %copy-done, bf16[3,36,8,128]{3,2,1,0:T(8,128)(2,1)S(1)} %fusion.19), kind=kOutput, calls=%fused_computation.6 | convolution fusion | flops 680361984 | bytes 4349952 | tf_op jit(solution)/shard_map/dot_general | solution.py:89
  74.3 0.0 all-reduce.2.cloned.1.call-update
  74.3 83.3 %all-reduce.2.cloned.1.call-done = bf16[288,3072]{1,0:T(8,128)(2,1)} async-done(((bf16[288,3072]{1,0:T(8,128)(2,1)}), bf16[288,3072]{1,0:T(8,128)(2,1)}) %all-reduce.2.cloned.1.call-update) | async-done | bytes 1769488 | tf_op jit(solution)/shard_map/psum | solution.py:91
  157.7 2.6 %fusion.7 = bf16[288,3072]{1,0:T(8,128)(2,1)S(1)} fusion(bf16[288,3072]{1,0:T(8,128)(2,1)} %param.7, bf16[288,3072]{1,0:T(8,128)(2,1)} %all-reduce.2.cloned.1.call-done, f32[3072]{0:T(1024)S(1)} %bitcast.56), kind=kLoop, calls=%fused_computation.11 | loop fusion | flops 4423680 | bytes 5320704 | tf_op jit(solution)/shard_map/convert_element_type | solution.py:92
  160.3 5.0 %collective-permute-start.2 = (bf16[288,3072]{1,0:T(8,128)(2,1)S(1)}, bf16[288,3072]{1,0:T(8,128)(2,1)S(1)}, u32[]{:S(2)}, u32[]{:S(2)}) collective-permute-start(bf16[288,3072]{1,0:T(8,128)(2,1)S(1)} %fusion.7), channel_id=1, source_target_pairs={{8,0},{16,8},{24,16},{32,24},{40,32},{48,40},{56,48},{64,56},{72,6... | collective-permute-start | bytes 5308424 | tf_op jit(solution)/shard_map/ppermute | solution.py:31
  165.3 41.6 %collective-permute-done.2 = bf16[288,3072]{1,0:T(8,128)(2,1)S(1)} collective-permute-done((bf16[288,3072]{1,0:T(8,128)(2,1)S(1)}, bf16[288,3072]{1,0:T(8,128)(2,1)S(1)}, u32[]{:S(2)}, u32[]{:S(2)}) %collective-permute-start.2) | collective-permute-done | bytes 1769504 | tf_op jit(solution)/shard_map/ppermute | solution.py:31
  206.9 1.2 copy.42
  (3 shorter events, 0.0 us)
Async XLA Ops:
  6.5 65.5 %copy-start = (bf16[384,3072]{1,0:T(8,128)(2,1)S(1)}, bf16[384,3072]{1,0:T(8,128)(2,1)}, u32[]{:S(2)}) copy-start(bf16[384,3072]{1,0:T(8,128)(2,1)} %param.13) | copy-start | bytes 7077892
  6.5 11.2 %copy-start.2 = (f32[16,9216]{1,0:T(8,128)S(1)}, f32[16,9216]{1,0:T(8,128)}, u32[]{:S(2)}) copy-start(f32[16,9216]{1,0:T(8,128)} %param.11) | copy-start | bytes 1769476
  6.5 151.1 %all-reduce.2.cloned.1.call-start = ((), (), s32[]{:S(2)}) async-start(), calls=%async_computation | async-start | bytes 3538944 | tf_op jit(solution)/shard_map/psum | solution.py:91
  17.0 2.9 %copy-start.1 = (bf16[288,3072]{1,0:T(8,128)(2,1)S(1)}, bf16[288,3072]{1,0:T(8,128)(2,1)}, u32[]{:S(2)}) copy-start(bf16[288,3072]{1,0:T(8,128)(2,1)} %param.7) | copy-start | bytes 5308420
  20.6 20.1 %copy-start.3 = (s32[32,2]{0,1:T(2,128)S(1)}, s32[32,2]{0,1:T(2,128)}, u32[]{:S(2)}) copy-start(s32[32,2]{0,1:T(2,128)} %param.10) | copy-start | bytes 772
  20.6 20.1 %copy-start.4 = (s32[32]{0:T(128)S(1)}, s32[32]{0:T(128)}, u32[]{:S(2)}) copy-start(s32[32]{0:T(128)} %param.9) | copy-start | bytes 388
  30.7 18.9 %collective-permute-start.1 = (bf16[288,2,384]{2,1,0:T(2,128)(2,1)}, bf16[288,2,384]{2,1,0:T(2,128)(2,1)}, u32[]{:S(2)}, u32[]{:S(2)}) collective-permute-start(bf16[288,2,384]{2,1,0:T(2,128)(2,1)} %slice.39), channel_id=1, source_target_pairs={{8,0},{16,8},{24,16},{32,24},{40,32},{48,40},{56,48},{64,56},{72,6... | collective-permute-start | bytes 1327112 | tf_op jit(solution)/shard_map/ppermute | solution.py:21
  33.3 17.5 %collective-permute-start = (bf16[288,2,384]{2,1,0:T(2,128)(2,1)}, bf16[288,2,384]{2,1,0:T(2,128)(2,1)}, u32[]{:S(2)}, u32[]{:S(2)}) collective-permute-start(bf16[288,2,384]{2,1,0:T(2,128)(2,1)} %slice.39), channel_id=1, source_target_pairs={{0,8},{8,16},{16,24},{24,32},{32,40},{40,48},{48,56},{56,64},{64,7... | collective-permute-start | bytes 1327112 | tf_op jit(solution)/shard_map/ppermute | solution.py:19
  160.3 46.6 %collective-permute-start.2 = (bf16[288,3072]{1,0:T(8,128)(2,1)S(1)}, bf16[288,3072]{1,0:T(8,128)(2,1)S(1)}, u32[]{:S(2)}, u32[]{:S(2)}) collective-permute-start(bf16[288,3072]{1,0:T(8,128)(2,1)S(1)} %fusion.7), channel_id=1, source_target_pairs={{8,0},{16,8},{24,16},{32,24},{40,32},{48,40},{56,48},{64,56},{72,6... | collective-permute-start | bytes 5308424 | tf_op jit(solution)/shard_map/ppermute | solution.py:31
Sparse Core Ops, SparseCore 0:
  74.5 83.1 all-reduce.1
where the time goes:
time: 216 us; the launch traced here: 215 us
  waiting for transfers between devices  130 us (60%)
  local copies, waits for them, and re-layouts  27.9 us (13%)
  between operations  16.9 us (8%)
  matrix products  15.6 us (7%)
  starting transfers between devices  15 us (7%)
  other arithmetic  9.81 us (5%)
    psum x1, waiting for transfers between devices, body(): lax.psum(partial_sum.astype(jnp.bfloat16), 'head').astype(jnp.float32)  83.3 us
    ppermute x1, waiting for transfers between devices, shifted(): return lax.ppermute(block, axis, route)  41.6 us
    unnamed x12, local copies, waits for them, and re-layouts  11.7 us
    slice x2, local copies, waits for them, and re-layouts, body(): keys = padded[:, 0]  7.96 us
    ppermute x1, starting transfers between devices, padded_2(): lax.ppermute(tail, axis, [(i, (i + 1) % count) for i in range(ends)])  7.38 us
    dot_general x1, matrix products, body(): jnp.dot(normed, qkv_weight.reshape(width, 3 * widthq), preferred_element_...  6.63 us
    ppermute x1, starting transfers between devices, shifted(): return lax.ppermute(block, axis, route)  5.01 us
  transfers between devices with their start and end apart: 4, of which 4 were waited for; matrix products, arithmetic and copies ran while one was open for 1% of the time, Pallas kernels for 0%

commit v1 on v0

v1 whole, which is shorter than its diff:
```python
import functools
import math

import jax
import jax.numpy as jnp
from jax import lax
from jax.experimental import pallas as pl
from jax.experimental.pallas import tpu as pltpu
from jax.sharding import PartitionSpec as P

HD = 128
ORDERS = ((4, 1, 3), (1, 3, 4), (3, 4, 1))
CHUNK = 16
F32, BF16 = jnp.float32, jnp.bfloat16


def vmem(n=1):
    return [pl.BlockSpec(memory_space=pltpu.VMEM)] * n


def smem(n=1):
    return [pl.BlockSpec(memory_space=pltpu.SMEM)] * n


def hbm(n=1):
    return [pl.BlockSpec(memory_space=pltpu.HBM)] * n


def params(mib):
    return pltpu.CompilerParams(vmem_limit_bytes=mib * 1024 * 1024)


def cost(flops, size):
    return pl.CostEstimate(flops=flops, bytes_accessed=size, transcendentals=0)


def dot(a, b):
    return jnp.dot(a, b, preferred_element_type=F32)


def dot_t(a, b):
    return lax.dot_general(a, b, (((1,), (1,)), ((), ())), preferred_element_type=F32)


def combos(dims):
    found = [0]
    for d in dims:
        found = [f ^ e for f in found for e in (0, d)]
    return found


def columns(target, size):
    return pl.ds(pl.multiple_of(target * size, size), size)


def keys_kernel(level_ref, x_hbm, mod_hbm, w_hbm, kv_ref, normed_ref, x_ref, mod_ref, w_ref, sems):
    rows, width = x_ref.shape
    level = level_ref[0]
    first = pl.multiple_of(level // 8 * 8, 8)
    copy_x = pltpu.make_async_copy(x_hbm, x_ref, sems.at[0])
    copy_mod = pltpu.make_async_copy(mod_hbm.at[pl.ds(first, 8), pl.ds(0, 2 * width)], mod_ref, sems.at[1])
    copy_k = pltpu.make_async_copy(w_hbm.at[1], w_ref.at[0], sems.at[2])
    copy_v = pltpu.make_async_copy(w_hbm.at[2], w_ref.at[1], sems.at[3])
    copy_x.start()
    copy_mod.start()
    copy_k.start()
    copy_v.start()
    copy_x.wait()
    copy_mod.wait()
    row = pl.ds(level % 8, 1)

    def step(i, carry):
        at = pl.ds(pl.multiple_of(i * CHUNK, CHUNK), CHUNK)
        x = x_ref[at, :].astype(F32)
        mean = jnp.mean(x, axis=-1, keepdims=True)
        centered = x - mean
        variance = jnp.mean(centered * centered, axis=-1, keepdims=True)
        scaled = centered * lax.rsqrt(variance + 1e-06)
        normed = scaled * (1.0 + mod_ref[row, width:]) + mod_ref[row, :width]
        normed_ref[at, :] = normed.astype(BF16)
        return carry

    lax.fori_loop(0, rows // CHUNK, step, 0, unroll=3)
    copy_k.wait()
    kv_ref[0] = dot(normed_ref[...], w_ref[0]).astype(BF16)
    copy_v.wait()
    kv_ref[1] = dot(normed_ref[...], w_ref[1]).astype(BF16)


def masked(scores, limit):
    spots = lax.broadcasted_iota(jnp.int32, scores.shape, 1)
    return jnp.where(spots < limit, scores * (1.0 / math.sqrt(HD)), -jnp.inf)


def self_kernel(
    meta_ref, level_ref, counts_ref, normed_ref, w_hbm, mod_hbm, kv_ref, q_ref, o_ref, m_ref, l_ref, gate_ref, w_ref, mod_ref, sems
):
    rows, width = normed_ref.shape
    level = level_ref[0]
    first = pl.multiple_of(level // 8 * 8, 8)
    copy = pltpu.make_async_copy(w_hbm.at[0], w_ref, sems.at[0])
    copy_mod = pltpu.make_async_copy(
        mod_hbm.at[pl.ds(first, 8), pl.ds(2 * width, width)], mod_ref, sems.at[1]
    )
    copy.start()
    copy_mod.start()
    copy_mod.wait()
    gate_ref[...] = mod_ref[pl.ds(level % 8, 1), :]
    copy.wait()
    q_ref[...] = dot(normed_ref[...], w_ref[...]).astype(BF16)
    limit = counts_ref[meta_ref[0]]
    for head in range(q_ref.shape[1] // HD):
        at = slice(head * HD, (head + 1) * HD)
        scores = masked(dot_t(q_ref[:, at], kv_ref[0, :, at]), limit)
        top = jnp.max(scores, axis=-1, keepdims=True)
        expo = jnp.exp(scores - top)
        m_ref[:, at] = jnp.broadcast_to(top, (rows, HD))
        l_ref[:, at] = jnp.broadcast_to(jnp.sum(expo, axis=-1, keepdims=True), (rows, HD))
        o_ref[:, at] = dot(expo.astype(BF16), kv_ref[1, :, at])


def join_kernel(meta_ref, counts_ref, mask_ref, q_ref, o_ref, m_ref, l_ref, cross_ref, chip_ref, w_ref, *refs):
    outs, att_ref = refs[:-1], refs[-1]
    places = counts_ref.shape[0]
    place, h = meta_ref[0], meta_ref[1]
    before = jnp.where(place > 0, counts_ref[jnp.maximum(place - 1, 0)] * mask_ref[0, place], 0)
    after = jnp.where(
        place < places - 1, counts_ref[jnp.minimum(place + 1, places - 1)] * mask_ref[1, place], 0
    )
    odd = place % 2 == 1
    cross = jnp.where(odd, after, before)
    chip = jnp.where(odd, before, after)
    for head in range(q_ref.shape[1] // HD):
        at = slice(head * HD, (head + 1) * HD)
        query = q_ref[:, at]
        left = masked(dot_t(query, cross_ref[0, :, at]), cross)
        right = masked(dot_t(query, chip_ref[0, :, at]), chip)
        old = m_ref[:, at][:, :1]
        top = jnp.maximum(old, jnp.max(jnp.maximum(left, right), axis=-1, keepdims=True))
        left = jnp.exp(left - top)
        right = jnp.exp(right - top)
        keep = jnp.exp(old - top)
        total = l_ref[:, at][:, :1] * keep + jnp.sum(left + right, axis=-1, keepdims=True)
        acc = o_ref[:, at] * keep
        acc = acc + dot(left.astype(BF16), cross_ref[1, :, at])
        acc = acc + dot(right.astype(BF16), chip_ref[1, :, at])
        att_ref[:, at] = (acc / total).astype(BF16)
    rows, size = q_ref.shape
    part = rows // len(ORDERS)
    for k in range(w_ref.shape[1] // size):
        result = dot(att_ref[...], w_ref[:, columns(h ^ k, size)]).astype(BF16)
        for c, dims in enumerate(ORDERS):
            spot = combos(dims).index(k)
            outs[2 * c + spot // 4][spot % 4] = result[c * part : (c + 1) * part]


def add_kernel(keep_ref, got_ref, *outs):
    total = (keep_ref[...].astype(F32) + got_ref[...].astype(F32)).astype(BF16)
    if len(outs) == 1:
        outs[0][...] = total
    else:
        half = total.shape[0] // 2
        outs[0][...] = total[:half]
        outs[1][...] = total[half:]


def update_kernel(chain, meta_ref, x_ref, gate_ref, keep_ref, got_ref, out_ref):
    part, size = out_ref.shape[1:]
    for c, step in enumerate((0, ORDERS[chain][2])):
        at = columns(meta_ref[1] ^ step, size)
        total = keep_ref[c].astype(F32) + got_ref[1 - c].astype(F32)
        x = x_ref[chain * part : (chain + 1) * part, at].astype(F32)
        out_ref[c] = (x + gate_ref[:, at] * total).astype(BF16)


def concat_kernel(a_ref, b_ref, out_ref):
    half = a_ref.shape[0]
    out_ref[:half] = a_ref[...]
    out_ref[half:] = b_ref[...]


def place_kernel(chain, meta_ref, *refs):
    own_ref, got_ref, out, sems = refs[-4:]
    part, size = own_ref.shape[1:]
    d1, d2, d3 = ORDERS[chain]
    copies = []
    for i, step in enumerate(combos((d1, d2, d3))):
        piece = (own_ref if i < 4 else got_ref).at[i % 4]
        to = out.at[pl.ds(chain * part, part), columns(meta_ref[1] ^ step, size)]
        copies.append(pltpu.make_async_copy(piece, to, sems.at[i]))
        copies[-1].start()
    for copy in copies:
        copy.wait()


def body(latents, levels, counts, window_mask, modulation, qkv_weight, out_weight):
    rows, width = latents.shape
    size = qkv_weight.shape[2]
    part = rows // len(ORDERS)
    weight = jnp.transpose(qkv_weight, (1, 0, 2))
    n_head = lax.axis_size("head")
    n_queue = lax.axis_size("queue")
    meta = jnp.stack([lax.axis_index("queue"), lax.axis_index("head")]).astype(jnp.int32)
    shape = jax.ShapeDtypeStruct

    def swap(array, step):
        return lax.ppermute(array, "head", [(i, i ^ step) for i in range(n_head)])

    kv, normed = pl.pallas_call(
        keys_kernel,
        out_shape=(shape((2, rows, size), BF16), shape((rows, width), BF16)),
        in_specs=smem() + hbm(3),
        out_specs=vmem(2),
        scratch_shapes=[
            pltpu.VMEM((rows, width), BF16),
            pltpu.VMEM((8, 2 * width), F32),
            pltpu.VMEM((2, width, size), BF16),
            pltpu.SemaphoreType.DMA((4,)),
        ],
        compiler_params=params(32),
        cost_estimate=cost(4 * rows * width * size, 4 * width * size),
    )(levels, latents, modulation, weight)

    pairs = [(i, i + 1) for i in range(1, n_queue - 1, 2)]
    cross = lax.ppermute(kv, "queue", pairs + [(j, i) for i, j in pairs])
    pairs = [(i, i + 1) for i in range(0, n_queue, 2)]
    chip = lax.ppermute(kv, "queue", pairs + [(j, i) for i, j in pairs])

    query, acc, top, total, gate = pl.pallas_call(
        self_kernel,
        out_shape=(shape((rows, size), BF16),) + (shape((rows, size), F32),) * 3 + (shape((1, width), F32),),
        in_specs=smem(3) + vmem() + hbm(2) + vmem(),
        out_specs=vmem(5),
        scratch_shapes=[
            pltpu.VMEM((width, size), BF16),
            pltpu.VMEM((8, width), F32),
            pltpu.SemaphoreType.DMA((2,)),
        ],
        compiler_params=params(32),
        cost_estimate=cost(4 * rows * width * size, 2 * width * size),
    )(meta, levels, counts, normed, weight, modulation, kv)

    parts = pl.pallas_call(
        join_kernel,
        out_shape=(shape((n_head // 2, part, size), BF16),) * 6,
        in_specs=smem(3) + vmem(7),
        out_specs=vmem(6),
        scratch_shapes=[pltpu.VMEM((rows, size), BF16)],
        compiler_params=params(32),
        cost_estimate=cost(4 * rows * width * size, 2 * width * size),
    )(meta, counts, window_mask.T, query, acc, top, total, cross, chip, out_weight)

    pair = shape((2, part, size), BF16)
    small = dict(compiler_params=params(16), cost_estimate=cost(4 * part * size, 8 * part * size))
    ready = []
    for c, (d1, d2, d3) in enumerate(ORDERS):
        keep, give = parts[2 * c : 2 * c + 2]
        got = swap(give, d1)
        keep, give = pl.pallas_call(
            add_kernel, out_shape=(pair, pair), in_specs=vmem(2), out_specs=vmem(2), **small
        )(keep, got)
        got = swap(give, d2)
        keep = pl.pallas_call(
            add_kernel, out_shape=(pair,), in_specs=vmem(2), out_specs=vmem(1), **small
        )(keep, got)[0]
        got = swap(keep, d3)
        fresh = pl.pallas_call(
            functools.partial(update_kernel, c),
            out_shape=pair,
            in_specs=smem() + vmem(4),
            out_specs=vmem()[0],
            **small,
        )(meta, latents, gate, keep, got)
        moved = lax.ppermute(fresh, "queue", [(i, (i - 1) % n_queue) for i in range(n_queue)])
        got = swap(moved, d2)
        four = pl.pallas_call(
            concat_kernel,
            out_shape=shape((4, part, size), BF16),
            in_specs=vmem(2),
            out_specs=vmem()[0],
            **small,
        )(moved, got)
        ready.append((four, swap(four, d1)))

    out = None
    for c, pieces in enumerate(ready):
        out = pl.pallas_call(
            functools.partial(place_kernel, c),
            out_shape=shape((rows, width), BF16),
            in_specs=smem() + hbm(c > 0) + vmem(2),
            out_specs=hbm()[0],
            scratch_shapes=[pltpu.SemaphoreType.DMA((8,))],
            input_output_aliases={1: 0} if c else {},
            **small,
        )(meta, *([out] if c else []), *pieces)
    return out


def solution(mesh):
    in_specs = (P("queue", None), P("queue"), P(), P(), P(), P(None, None, "head"), P("head", None))
    out_specs = P("queue", None)
    return jax.shard_map(body, mesh=mesh, in_specs=in_specs, out_specs=out_specs, check_vma=False)
```

time: 216 us -> 83.9 us (0.39)
  waiting for transfers between devices: 130 us -> 31.2 us
  local copies, waits for them, and re-layouts: 27.9 us -> 8.57 us
  Pallas kernels: 0 us -> 18.4 us
  between operations: 16.9 us -> 1 us
  matrix products: 15.6 us -> 0 us
  other arithmetic: 9.81 us -> 0.08 us
  starting transfers between devices: 15 us -> 24.1 us
    psum x1 -> x0, waiting for transfers between devices: 83.3 us -> none  [body(): lax.psum(partial_sum.astype(jnp.bfloat16), 'head').astype(jnp.float32)]
    pallas_call x0 -> x18, Pallas kernels: none -> 18.4 us  [the longest x1 5.01 us: body(): pl.pallas_call(keys_kernel, out_shape=(shape((2, rows, size), BF16), shap...]
    ppermute x3 -> x20, waiting for transfers between devices: 46.4 us -> 31.2 us  [the longest x3 13.9 us: body(): lax.ppermute(fresh, 'queue', [(i, (i - 1) % n_queue) for i in range(n_que...]
    slice x5 -> x0, local copies, waits for them, and re-layouts: 14 us -> none  [the longest x2 7.96 us: body(): keys = padded[:, 0]]
    dot_general x4 -> x0, matrix products: 11.8 us -> none  [the longest x1 6.63 us: body(): jnp.dot(normed, qkv_weight.reshape(width, 3 * widthq), preferred_element_...]
    ppermute x3 -> x20, starting transfers between devices: 15 us -> 24.1 us  [the longest x15 17.5 us: swap(): return lax.ppermute(array, 'head', [(i, i ^ step) for i in range(n_head)])]
    sub x1 -> x0, matrix products: 3.84 us -> none  [body(): expo = jnp.exp(scores - top)]
    concatenate x1 -> x0, other arithmetic: 3.35 us -> none  [padded_2(): jnp.concatenate([lax.ppermute(tail, axis, [(i, (i + 1) % count) for i in...]
  transfers between devices with their start and end apart: 4 -> 20, of which waited for: 4 -> 15; matrix products, arithmetic and copies ran while one was open for 1% -> 0% of each run, Pallas kernels for 0% -> 10%
where the time goes in v1:
time: 83.9 us; the launch traced here: 83.4 us
  waiting for transfers between devices  31.2 us (37%)
  starting transfers between devices  24.1 us (29%)
  Pallas kernels  18.4 us (22%)
  local copies, waits for them, and re-layouts  8.57 us (10%)
  between operations  1 us (1%)
    ppermute x15, starting transfers between devices, swap(): return lax.ppermute(array, 'head', [(i, i ^ step) for i in range(n_head)])  17.5 us
    ppermute x3, waiting for transfers between devices, body(): lax.ppermute(fresh, 'queue', [(i, (i - 1) % n_queue) for i in range(n_que...  13.9 us
    ppermute x15, waiting for transfers between devices, swap(): return lax.ppermute(array, 'head', [(i, i ^ step) for i in range(n_head)])  10.2 us
    unnamed x18, local copies, waits for them, and re-layouts  8.57 us
    ppermute x1, waiting for transfers between devices, body(): cross = lax.ppermute(kv, 'queue', pairs + [(j, i) for i, j in pairs])  7.08 us
    ppermute x1, starting transfers between devices, body(): cross = lax.ppermute(kv, 'queue', pairs + [(j, i) for i, j in pairs])  5.67 us
    pallas_call x1, Pallas kernels, body(): pl.pallas_call(keys_kernel, out_shape=(shape((2, rows, size), BF16), shap...  5.01 us
    pallas_call x3, Pallas kernels, body(): pl.pallas_call(functools.partial(place_kernel, c), out_shape=shape((rows,...  4.25 us
  transfers between devices with their start and end apart: 20, of which 15 were waited for; matrix products, arithmetic and copies ran while one was open for 0% of the time, Pallas kernels for 10%

profile of v1, /device:TPU:89, one launch (start us, length us, event | category | flops | bytes accessed | tf_op | source)
XLA Modules:
  0.0 83.4 jit_solution(6147829072102210259)
XLA Ops:
  0.7 1.5 %copy-done = bf16[288,3072]{1,0:T(8,128)(2,1)S(1)} copy-done((bf16[288,3072]{1,0:T(8,128)(2,1)S(1)}, bf16[288,3072]{1,0:T(8,128)(2,1)}, u32[]{:S(2)}) %copy-start) | copy-done | bytes 1769496
  2.1 3.0 %copy-done.2 = bf16[3072,3,384]{2,0,1:T(8,128)(2,1)S(1)} copy-done((bf16[3072,3,384]{2,0,1:T(8,128)(2,1)S(1)}, bf16[3072,3,384]{2,0,1:T(8,128)(2,1)}, u32[]{:S(2)}) %copy-start.2) | copy-done | bytes 7077912
  5.1 1.1 %copy-done.4 = f32[16,9216]{1,0:T(8,128)S(1)} copy-done((f32[16,9216]{1,0:T(8,128)S(1)}, f32[16,9216]{1,0:T(8,128)}, u32[]{:S(2)}) %copy-start.4) | copy-done | bytes 589848
  6.2 5.0 %shard_map.73 = (bf16[2,288,384]{2,1,0:T(8,128)(2,1)S(1)}, bf16[288,3072]{1,0:T(8,128)(2,1)S(1)}) custom-call(s32[1]{0:T(128)S(6)} %copy.12.level_ref, bf16[288,3072]{1,0:T(8,128)(2,1)S(1)} %copy-done, f32[16,9216]{1,0:T(8,128)S(1)} %copy-done.4, bf16[3,3072,384]{2,1,0:T(8,128)(2,1)S(1)} %bitcast.4), custom_call_target="tpu_custom_call" | custom-call | flops 1358954496 | bytes 4718592 | tf_op jit(solution)/shard_map/pallas_call | solution.py:209
  11.2 0.8 collective-permute-start.1
  12.0 5.7 %collective-permute-start = (bf16[2,288,384]{2,1,0:T(8,128)(2,1)S(1)}, bf16[2,288,384]{2,1,0:T(8,128)(2,1)}, u32[]{:S(2)}, u32[]{:S(2)}) collective-permute-start(bf16[2,288,384]{2,1,0:T(8,128)(2,1)S(1)} %get-tuple-element.25.kv_ref), channel_id=1, source_target_pairs={{8,16},{24,32},{40,48},{56,64},{72,80},{88,96},{104,112},{120,128}... | collective-permute-start | bytes 1327112 | tf_op jit(solution)/shard_map/ppermute | solution.py:225
  17.7 0.1 pad_add_fusion.meta_ref
  17.8 3.0 %copy-done.3 = bf16[3072,3,384]{2,0,1:T(8,128)(2,1)S(1)} copy-done((bf16[3072,3,384]{2,0,1:T(8,128)(2,1)S(1)}, bf16[3072,3,384]{2,0,1:T(8,128)(2,1)}, u32[]{:S(2)}) %copy-start.3) | copy-done | bytes 7077912
  20.8 2.9 %shard_map.74 = (bf16[288,384]{1,0:T(8,128)(2,1)S(1)}, f32[288,384]{1,0:T(8,128)S(1)}, f32[288,384]{1,0:T(8,128)S(1)}, f32[288,384]{1,0:T(8,128)S(1)}, f32[1,3072]{1,0:T(1,128)S(1)}) custom-call(s32[2]{0:T(128)S(1)} %pad_add_fusion.meta_ref, s32[1]{0:T(128)S(6)} %copy.12.level_ref, s32[32]{0:T(128)S(1)} %copy-done.6, ...), custom_call_target="tpu_custom_call" | custom-call | flops 1358954496 | bytes 2359296 | tf_op jit(solution)/shard_map/pallas_call | solution.py:229
  23.7 7.1 %collective-permute-done.cross_ref = bf16[2,288,384]{2,1,0:T(8,128)(2,1)} collective-permute-done((bf16[2,288,384]{2,1,0:T(8,128)(2,1)S(1)}, bf16[2,288,384]{2,1,0:T(8,128)(2,1)}, u32[]{:S(2)}, u32[]{:S(2)}) %collective-permute-start) | collective-permute-done | bytes 442400 | tf_op jit(solution)/shard_map/ppermute | solution.py:225
  30.8 4.0 %shard_map.75 = (bf16[4,96,384]{2,1,0:T(8,128)(2,1)S(1)}, bf16[4,96,384]{2,1,0:T(8,128)(2,1)S(1)}, bf16[4,96,384]{2,1,0:T(8,128)(2,1)S(1)}, bf16[4,96,384]{2,1,0...) custom-call(s32[2]{0:T(128)S(1)} %pad_add_fusion.meta_ref, s32[32]{0:T(128)S(1)} %copy-done.6, ...), custom_call_target="tpu_custom_call" | custom-call | flops 1358954496 | bytes 2359296 | tf_op jit(solution)/shard_map/pallas_call | solution.py:243
  34.8 0.1 collective-permute-start.2
  34.9 1.3 %collective-permute-start.8 = (bf16[4,96,384]{2,1,0:T(8,128)(2,1)S(1)}, bf16[4,96,384]{2,1,0:T(8,128)(2,1)S(1)}, u32[]{:S(2)}, u32[]{:S(2)}) collective-permute-start(bf16[4,96,384]{2,1,0:T(8,128)(2,1)S(1)} %get-tuple-element.36), channel_id=1, source_target_pairs={{0,1},{1,0},{2,3},{3,2},{4,5},{5,4},{6,7},{7,6},{8,9},{9,8},{10,11... | collective-permute-start | bytes 884744 | tf_op jit(solution)/shard_map/ppermute | solution.py:207
  36.2 1.8 %collective-permute-start.14 = (bf16[4,96,384]{2,1,0:T(8,128)(2,1)S(1)}, bf16[4,96,384]{2,1,0:T(8,128)(2,1)S(1)}, u32[]{:S(2)}, u32[]{:S(2)}) collective-permute-start(bf16[4,96,384]{2,1,0:T(8,128)(2,1)S(1)} %get-tuple-element.40), channel_id=1, source_target_pairs={{0,3},{1,2},{2,1},{3,0},{4,7},{5,6},{6,5},{7,4},{8,11},{9,10},{10,... | collective-permute-start | bytes 884744 | tf_op jit(solution)/shard_map/ppermute | solution.py:207
  38.0 2.7 %collective-permute-done.2.got_ref = bf16[4,96,384]{2,1,0:T(8,128)(2,1)S(1)} collective-permute-done((bf16[4,96,384]{2,1,0:T(8,128)(2,1)S(1)}, bf16[4,96,384]{2,1,0:T(8,128)(2,1)S(1)}, u32[]{:S(2)}, u32[]{:S(2)}) %collective-permute-start.2) | collective-permute-done | bytes 294944 | tf_op jit(solution)/shard_map/ppermute | solution.py:207
  40.8 0.1 shard_map.76
  40.8 2.5 %collective-permute-start.3 = (bf16[2,96,384]{2,1,0:T(8,128)(2,1)S(1)}, bf16[2,96,384]{2,1,0:T(8,128)(2,1)S(1)}, u32[]{:S(2)}, u32[]{:S(2)}) collective-permute-start(bf16[2,96,384]{2,1,0:T(8,128)(2,1)S(1)} %get-tuple-element.34), channel_id=1, source_target_pairs={{0,1},{1,0},{2,3},{3,2},{4,5},{5,4},{6,7},{7,6},{8,9},{9,8},{10,11... | collective-permute-start | bytes 442376 | tf_op jit(solution)/shard_map/ppermute | solution.py:207
  43.3 0.1 shard_map.81
  43.4 2.3 %collective-permute-start.9 = (bf16[2,96,384]{2,1,0:T(8,128)(2,1)S(1)}, bf16[2,96,384]{2,1,0:T(8,128)(2,1)S(1)}, u32[]{:S(2)}, u32[]{:S(2)}) collective-permute-start(bf16[2,96,384]{2,1,0:T(8,128)(2,1)S(1)} %get-tuple-element.38), channel_id=1, source_target_pairs={{0,3},{1,2},{2,1},{3,0},{4,7},{5,6},{6,5},{7,4},{8,11},{9,10},{10,... | collective-permute-start | bytes 442376 | tf_op jit(solution)/shard_map/ppermute | solution.py:207
  45.8 0.6 collective-permute-start.15
  46.4 2.2 %collective-permute-start.4 = (bf16[2,96,384]{2,1,0:T(8,128)(2,1)S(1)}, bf16[2,96,384]{2,1,0:T(8,128)(2,1)S(1)}, u32[]{:S(2)}, u32[]{:S(2)}) collective-permute-start(bf16[2,96,384]{2,1,0:T(8,128)(2,1)S(1)} %shard_map.77.keep_ref), channel_id=1, source_target_pairs={{0,3},{1,2},{2,1},{3,0},{4,7},{5,6},{6,5},{7,4},{8,11},{9,10},{10,... | collective-permute-start | bytes 442376 | tf_op jit(solution)/shard_map/ppermute | solution.py:207
  48.8 0.7 collective-permute-start.10
  49.5 0.4 collective-permute-done.15.got_ref
  49.9 0.6 collective-permute-start.16
  50.5 1.2 %collective-permute-done.4.got_ref = bf16[2,96,384]{2,1,0:T(8,128)(2,1)S(1)} collective-permute-done((bf16[2,96,384]{2,1,0:T(8,128)(2,1)S(1)}, bf16[2,96,384]{2,1,0:T(8,128)(2,1)S(1)}, u32[]{:S(2)}, u32[]{:S(2)}) %collective-permute-start.4) | collective-permute-done | bytes 147488 | tf_op jit(solution)/shard_map/ppermute | solution.py:207
  51.7 0.6 shard_map.78
  52.4 0.1 collective-permute-start.5
  52.4 0.4 collective-permute-done.10.got_ref
  52.8 0.6 shard_map.83
  53.5 0.1 collective-permute-start.11
  53.5 0.6 collective-permute-done.16.got_ref
  54.2 0.6 shard_map.88
  54.8 0.1 collective-permute-start.17
  54.9 12.2 %collective-permute-done.5.a_ref = bf16[2,96,384]{2,1,0:T(8,128)(2,1)S(1)} collective-permute-done((bf16[2,96,384]{2,1,0:T(8,128)(2,1)S(1)}, bf16[2,96,384]{2,1,0:T(8,128)(2,1)S(1)}, u32[]{:S(2)}, u32[]{:S(2)}) %collective-permute-start.5) | collective-permute-done | bytes 147488 | tf_op jit(solution)/shard_map/ppermute | solution.py:274
  67.1 1.7 %collective-permute-done.11.a_ref = bf16[2,96,384]{2,1,0:T(8,128)(2,1)S(1)} collective-permute-done((bf16[2,96,384]{2,1,0:T(8,128)(2,1)S(1)}, bf16[2,96,384]{2,1,0:T(8,128)(2,1)S(1)}, u32[]{:S(2)}, u32[]{:S(2)}) %collective-permute-start.11) | collective-permute-done | bytes 147488 | tf_op jit(solution)/shard_map/ppermute | solution.py:274
  68.8 2.1 %collective-permute-start.12 = (bf16[2,96,384]{2,1,0:T(8,128)(2,1)S(1)}, bf16[2,96,384]{2,1,0:T(8,128)(2,1)S(1)}, u32[]{:S(2)}, u32[]{:S(2)}) collective-permute-start(bf16[2,96,384]{2,1,0:T(8,128)(2,1)S(1)} %collective-permute-done.11.a_ref), channel_id=1, source_target_pairs={{0,3},{1,2},{2,1},{3,0},{4,7},{5,6},{6,5},{7,4},{8,11},{9,10},{10,... | collective-permute-start | bytes 442376 | tf_op jit(solution)/shard_map/ppermute | solution.py:207
  70.9 0.2 collective-permute-done.6.b_ref
  71.1 1.4 %collective-permute-start.7 = (bf16[4,96,384]{2,1,0:T(8,128)(2,1)S(1)}, bf16[4,96,384]{2,1,0:T(8,128)(2,1)S(1)}, u32[]{:S(2)}, u32[]{:S(2)}) collective-permute-start(bf16[4,96,384]{2,1,0:T(8,128)(2,1)S(1)} %shard_map.79.refs_0_), channel_id=1, source_target_pairs={{0,4},{1,5},{2,6},{3,7},{4,0},{5,1},{6,2},{7,3},{8,12},{9,13},{10,... | collective-permute-start | bytes 884744 | tf_op jit(solution)/shard_map/ppermute | solution.py:207
  72.5 1.5 %collective-permute-done.12.b_ref = bf16[2,96,384]{2,1,0:T(8,128)(2,1)S(1)} collective-permute-done((bf16[2,96,384]{2,1,0:T(8,128)(2,1)S(1)}, bf16[2,96,384]{2,1,0:T(8,128)(2,1)S(1)}, u32[]{:S(2)}, u32[]{:S(2)}) %collective-permute-start.12) | collective-permute-done | bytes 147488 | tf_op jit(solution)/shard_map/ppermute | solution.py:207
  74.0 0.1 collective-permute-start.13
  74.1 0.8 collective-permute-done.18.b_ref
  75.0 1.7 %collective-permute-start.19 = (bf16[4,96,384]{2,1,0:T(8,128)(2,1)S(1)}, bf16[4,96,384]{2,1,0:T(8,128)(2,1)S(1)}, u32[]{:S(2)}, u32[]{:S(2)}) collective-permute-start(bf16[4,96,384]{2,1,0:T(8,128)(2,1)S(1)} %shard_map.89.refs_1_), channel_id=1, source_target_pairs={{0,3},{1,2},{2,1},{3,0},{4,7},{5,6},{6,5},{7,4},{8,11},{9,10},{10,... | collective-permute-start | bytes 884744 | tf_op jit(solution)/shard_map/ppermute | solution.py:207
  76.6 1.5 %collective-permute-done.7.refs_1_ = bf16[4,96,384]{2,1,0:T(8,128)(2,1)S(1)} collective-permute-done((bf16[4,96,384]{2,1,0:T(8,128)(2,1)S(1)}, bf16[4,96,384]{2,1,0:T(8,128)(2,1)S(1)}, u32[]{:S(2)}, u32[]{:S(2)}) %collective-permute-start.7) | collective-permute-done | bytes 294944 | tf_op jit(solution)/shard_map/ppermute | solution.py:207
  78.1 1.4 %shard_map.80.refs_0_ = bf16[288,3072]{1,0:T(8,128)(2,1)} custom-call(s32[2]{0:T(128)S(1)} %pad_add_fusion.meta_ref, bf16[4,96,384]{2,1,0:T(8,128)(2,1)S(1)} %shard_map.79.refs_0_, bf16[4,96,384]{2,1,0:T(8,128)(2,1)S(1)} %collective-permute-done.7.refs_1_), custom_call_target="tpu_custom_call" | custom-call | flops 147456 | bytes 294912 | tf_op jit(solution)/shard_map/pallas_call | solution.py:287
  79.5 0.2 collective-permute-done.13.refs_2_
  79.7 1.4 %shard_map.85.refs_0_ = bf16[288,3072]{1,0:T(8,128)(2,1)} custom-call(s32[2]{0:T(128)S(1)} %pad_add_fusion.meta_ref, bf16[288,3072]{1,0:T(8,128)(2,1)} %shard_map.80.refs_0_, bf16[4,96,384]{2,1,0:T(8,128)(2,1)S(1)} %shard_map.84.refs_1_, bf16[4,96,384]{2,1,0:T(8,128)(2,1)S(1)} %collective-permute-done.13.refs_2_), custom_call_target="tpu_custom_call", output_to_operand_aliasing={{}: (1, {})} | custom-call | flops 147456 | bytes 294912 | tf_op jit(solution)/shard_map/pallas_call | solution.py:287
  81.1 0.7 collective-permute-done.19.refs_2_
  81.8 1.4 %shard_map.90 = bf16[288,3072]{1,0:T(8,128)(2,1)} custom-call(s32[2]{0:T(128)S(1)} %pad_add_fusion.meta_ref, bf16[288,3072]{1,0:T(8,128)(2,1)} %shard_map.85.refs_0_, bf16[4,96,384]{2,1,0:T(8,128)(2,1)S(1)} %shard_map.89.refs_1_, bf16[4,96,384]{2,1,0:T(8,128)(2,1)S(1)} %collective-permute-done.19.refs_2_), custom_call_target="tpu_custom_call", output_to_operand_aliasing={{}: (1, {})} | custom-call | flops 147456 | bytes 294912 | tf_op jit(solution)/shard_map/pallas_call | solution.py:287
  (29 shorter events, 0.4 us)
Async XLA Ops:
  0.7 1.5 %copy-start = (bf16[288,3072]{1,0:T(8,128)(2,1)S(1)}, bf16[288,3072]{1,0:T(8,128)(2,1)}, u32[]{:S(2)}) copy-start(bf16[288,3072]{1,0:T(8,128)(2,1)} %x_ref.5) | copy-start | bytes 5308420
  2.1 3.0 %copy-start.2 = (bf16[3072,3,384]{2,0,1:T(8,128)(2,1)S(1)}, bf16[3072,3,384]{2,0,1:T(8,128)(2,1)}, u32[]{:S(2)}) copy-start(bf16[3072,3,384]{2,0,1:T(8,128)(2,1)} %param.12) | copy-start | bytes 21233668
  5.1 1.1 %copy-start.4 = (f32[16,9216]{1,0:T(8,128)S(1)}, f32[16,9216]{1,0:T(8,128)}, u32[]{:S(2)}) copy-start(f32[16,9216]{1,0:T(8,128)} %mod_hbm.3) | copy-start | bytes 1769476
  6.2 11.5 %copy-start.5 = (f32[16,9216]{1,0:T(8,128)S(1)}, f32[16,9216]{1,0:T(8,128)}, u32[]{:S(2)}) copy-start(f32[16,9216]{1,0:T(8,128)} %mod_hbm.3) | copy-start | bytes 1769476
  6.2 11.5 %copy-start.6 = (s32[32]{0:T(128)S(1)}, s32[32]{0:T(128)}, u32[]{:S(2)}) copy-start(s32[32]{0:T(128)} %counts_ref.3) | copy-start | bytes 388
  11.2 12.5 %collective-permute-start.1 = (bf16[2,288,384]{2,1,0:T(8,128)(2,1)S(1)}, bf16[2,288,384]{2,1,0:T(8,128)(2,1)S(1)}, u32[]{:S(2)}, u32[]{:S(2)}) collective-permute-start(bf16[2,288,384]{2,1,0:T(8,128)(2,1)S(1)} %get-tuple-element.25.kv_ref), channel_id=1, source_target_pairs={{0,8},{16,24},{32,40},{48,56},{64,72},{80,88},{96,104},{112,120},{... | collective-permute-start | bytes 1327112 | tf_op jit(solution)/shard_map/ppermute | solution.py:227
  12.0 18.8 %collective-permute-start = (bf16[2,288,384]{2,1,0:T(8,128)(2,1)S(1)}, bf16[2,288,384]{2,1,0:T(8,128)(2,1)}, u32[]{:S(2)}, u32[]{:S(2)}) collective-permute-start(bf16[2,288,384]{2,1,0:T(8,128)(2,1)S(1)} %get-tuple-element.25.kv_ref), channel_id=1, source_target_pairs={{8,16},{24,32},{40,48},{56,64},{72,80},{88,96},{104,112},{120,128}... | collective-permute-start | bytes 1327112 | tf_op jit(solution)/shard_map/ppermute | solution.py:225
  17.8 3.0 %copy-start.3 = (bf16[3072,3,384]{2,0,1:T(8,128)(2,1)S(1)}, bf16[3072,3,384]{2,0,1:T(8,128)(2,1)}, u32[]{:S(2)}) copy-start(bf16[3072,3,384]{2,0,1:T(8,128)(2,1)} %param.12) | copy-start | bytes 21233668
  20.8 10.0 %copy-start.7 = (bf16[384,3072]{1,0:T(8,128)(2,1)S(1)}, bf16[384,3072]{1,0:T(8,128)(2,1)}, u32[]{:S(2)}) copy-start(bf16[384,3072]{1,0:T(8,128)(2,1)} %w_ref.1) | copy-start | bytes 7077892
  20.8 10.0 %copy-start.8 = (s32[32,2]{0,1:T(2,128)S(1)}, s32[32,2]{0,1:T(2,128)}, u32[]{:S(2)}) copy-start(s32[32,2]{0,1:T(2,128)} %param.10) | copy-start | bytes 772
  34.8 17.0 %copy-start.1 = (bf16[288,3072]{1,0:T(8,128)(2,1)S(1)}, bf16[288,3072]{1,0:T(8,128)(2,1)}, u32[]{:S(2)}) copy-start(bf16[288,3072]{1,0:T(8,128)(2,1)} %x_ref.5) | copy-start | bytes 5308420
  34.8 6.0 %collective-permute-start.2 = (bf16[4,96,384]{2,1,0:T(8,128)(2,1)S(1)}, bf16[4,96,384]{2,1,0:T(8,128)(2,1)S(1)}, u32[]{:S(2)}, u32[]{:S(2)}) collective-permute-start(bf16[4,96,384]{2,1,0:T(8,128)(2,1)S(1)} %get-tuple-element.32), channel_id=1, source_target_pairs={{0,4},{1,5},{2,6},{3,7},{4,0},{5,1},{6,2},{7,3},{8,12},{9,13},{10,... | collective-permute-start | bytes 884744 | tf_op jit(solution)/shard_map/ppermute | solution.py:207
  34.9 8.4 %collective-permute-start.8 = (bf16[4,96,384]{2,1,0:T(8,128)(2,1)S(1)}, bf16[4,96,384]{2,1,0:T(8,128)(2,1)S(1)}, u32[]{:S(2)}, u32[]{:S(2)}) collective-permute-start(bf16[4,96,384]{2,1,0:T(8,128)(2,1)S(1)} %get-tuple-element.36), channel_id=1, source_target_pairs={{0,1},{1,0},{2,3},{3,2},{4,5},{5,4},{6,7},{7,6},{8,9},{9,8},{10,11... | collective-permute-start | bytes 884744 | tf_op jit(solution)/shard_map/ppermute | solution.py:207
  36.2 9.5 %collective-permute-start.14 = (bf16[4,96,384]{2,1,0:T(8,128)(2,1)S(1)}, bf16[4,96,384]{2,1,0:T(8,128)(2,1)S(1)}, u32[]{:S(2)}, u32[]{:S(2)}) collective-permute-start(bf16[4,96,384]{2,1,0:T(8,128)(2,1)S(1)} %get-tuple-element.40), channel_id=1, source_target_pairs={{0,3},{1,2},{2,1},{3,0},{4,7},{5,6},{6,5},{7,4},{8,11},{9,10},{10,... | collective-permute-start | bytes 884744 | tf_op jit(solution)/shard_map/ppermute | solution.py:207
  40.8 5.6 %collective-permute-start.3 = (bf16[2,96,384]{2,1,0:T(8,128)(2,1)S(1)}, bf16[2,96,384]{2,1,0:T(8,128)(2,1)S(1)}, u32[]{:S(2)}, u32[]{:S(2)}) collective-permute-start(bf16[2,96,384]{2,1,0:T(8,128)(2,1)S(1)} %get-tuple-element.34), channel_id=1, source_target_pairs={{0,1},{1,0},{2,3},{3,2},{4,5},{5,4},{6,7},{7,6},{8,9},{9,8},{10,11... | collective-permute-start | bytes 442376 | tf_op jit(solution)/shard_map/ppermute | solution.py:207
  43.4 5.3 %collective-permute-start.9 = (bf16[2,96,384]{2,1,0:T(8,128)(2,1)S(1)}, bf16[2,96,384]{2,1,0:T(8,128)(2,1)S(1)}, u32[]{:S(2)}, u32[]{:S(2)}) collective-permute-start(bf16[2,96,384]{2,1,0:T(8,128)(2,1)S(1)} %get-tuple-element.38), channel_id=1, source_target_pairs={{0,3},{1,2},{2,1},{3,0},{4,7},{5,6},{6,5},{7,4},{8,11},{9,10},{10,... | collective-permute-start | bytes 442376 | tf_op jit(solution)/shard_map/ppermute | solution.py:207
  45.8 4.1 %collective-permute-start.15 = (bf16[2,96,384]{2,1,0:T(8,128)(2,1)S(1)}, bf16[2,96,384]{2,1,0:T(8,128)(2,1)S(1)}, u32[]{:S(2)}, u32[]{:S(2)}) collective-permute-start(bf16[2,96,384]{2,1,0:T(8,128)(2,1)S(1)} %get-tuple-element.42), channel_id=1, source_target_pairs={{0,4},{1,5},{2,6},{3,7},{4,0},{5,1},{6,2},{7,3},{8,12},{9,13},{10,... | collective-permute-start | bytes 442376 | tf_op jit(solution)/shard_map/ppermute | solution.py:207
  46.4 5.3 %collective-permute-start.4 = (bf16[2,96,384]{2,1,0:T(8,128)(2,1)S(1)}, bf16[2,96,384]{2,1,0:T(8,128)(2,1)S(1)}, u32[]{:S(2)}, u32[]{:S(2)}) collective-permute-start(bf16[2,96,384]{2,1,0:T(8,128)(2,1)S(1)} %shard_map.77.keep_ref), channel_id=1, source_target_pairs={{0,3},{1,2},{2,1},{3,0},{4,7},{5,6},{6,5},{7,4},{8,11},{9,10},{10,... | collective-permute-start | bytes 442376 | tf_op jit(solution)/shard_map/ppermute | solution.py:207
  48.8 4.1 %collective-permute-start.10 = (bf16[2,96,384]{2,1,0:T(8,128)(2,1)S(1)}, bf16[2,96,384]{2,1,0:T(8,128)(2,1)S(1)}, u32[]{:S(2)}, u32[]{:S(2)}) collective-permute-start(bf16[2,96,384]{2,1,0:T(8,128)(2,1)S(1)} %shard_map.82.keep_ref), channel_id=1, source_target_pairs={{0,4},{1,5},{2,6},{3,7},{4,0},{5,1},{6,2},{7,3},{8,12},{9,13},{10,... | collective-permute-start | bytes 442376 | tf_op jit(solution)/shard_map/ppermute | solution.py:207
  49.9 4.3 %collective-permute-start.16 = (bf16[2,96,384]{2,1,0:T(8,128)(2,1)S(1)}, bf16[2,96,384]{2,1,0:T(8,128)(2,1)S(1)}, u32[]{:S(2)}, u32[]{:S(2)}) collective-permute-start(bf16[2,96,384]{2,1,0:T(8,128)(2,1)S(1)} %shard_map.87.keep_ref), channel_id=1, source_target_pairs={{0,1},{1,0},{2,3},{3,2},{4,5},{5,4},{6,7},{7,6},{8,9},{9,8},{10,11... | collective-permute-start | bytes 442376 | tf_op jit(solution)/shard_map/ppermute | solution.py:207
  52.4 14.8 %collective-permute-start.5 = (bf16[2,96,384]{2,1,0:T(8,128)(2,1)S(1)}, bf16[2,96,384]{2,1,0:T(8,128)(2,1)S(1)}, u32[]{:S(2)}, u32[]{:S(2)}) collective-permute-start(bf16[2,96,384]{2,1,0:T(8,128)(2,1)S(1)} %shard_map.78), channel_id=1, source_target_pairs={{0,248},{8,0},{16,8},{24,16},{32,24},{40,32},{48,40},{56,48},{64,5... | collective-permute-start | bytes 442376 | tf_op jit(solution)/shard_map/ppermute | solution.py:274
  53.5 15.3 %collective-permute-start.11 = (bf16[2,96,384]{2,1,0:T(8,128)(2,1)S(1)}, bf16[2,96,384]{2,1,0:T(8,128)(2,1)S(1)}, u32[]{:S(2)}, u32[]{:S(2)}) collective-permute-start(bf16[2,96,384]{2,1,0:T(8,128)(2,1)S(1)} %shard_map.83), channel_id=1, source_target_pairs={{0,248},{8,0},{16,8},{24,16},{32,24},{40,32},{48,40},{56,48},{64,5... | collective-permute-start | bytes 442376 | tf_op jit(solution)/shard_map/ppermute | solution.py:274
  54.8 16.1 %collective-permute-start.17 = (bf16[2,96,384]{2,1,0:T(8,128)(2,1)S(1)}, bf16[2,96,384]{2,1,0:T(8,128)(2,1)S(1)}, u32[]{:S(2)}, u32[]{:S(2)}) collective-permute-start(bf16[2,96,384]{2,1,0:T(8,128)(2,1)S(1)} %shard_map.88), channel_id=1, source_target_pairs={{0,248},{8,0},{16,8},{24,16},{32,24},{40,32},{48,40},{56,48},{64,5... | collective-permute-start | bytes 442376 | tf_op jit(solution)/shard_map/ppermute | solution.py:274
  67.1 4.0 %collective-permute-start.6 = (bf16[2,96,384]{2,1,0:T(8,128)(2,1)S(1)}, bf16[2,96,384]{2,1,0:T(8,128)(2,1)S(1)}, u32[]{:S(2)}, u32[]{:S(2)}) collective-permute-start(bf16[2,96,384]{2,1,0:T(8,128)(2,1)S(1)} %collective-permute-done.5.a_ref), channel_id=1, source_target_pairs={{0,1},{1,0},{2,3},{3,2},{4,5},{5,4},{6,7},{7,6},{8,9},{9,8},{10,11... | collective-permute-start | bytes 442376 | tf_op jit(solution)/shard_map/ppermute | solution.py:207
  68.8 5.2 %collective-permute-start.12 = (bf16[2,96,384]{2,1,0:T(8,128)(2,1)S(1)}, bf16[2,96,384]{2,1,0:T(8,128)(2,1)S(1)}, u32[]{:S(2)}, u32[]{:S(2)}) collective-permute-start(bf16[2,96,384]{2,1,0:T(8,128)(2,1)S(1)} %collective-permute-done.11.a_ref), channel_id=1, source_target_pairs={{0,3},{1,2},{2,1},{3,0},{4,7},{5,6},{6,5},{7,4},{8,11},{9,10},{10,... | collective-permute-start | bytes 442376 | tf_op jit(solution)/shard_map/ppermute | solution.py:207
  70.9 4.0 %collective-permute-start.18 = (bf16[2,96,384]{2,1,0:T(8,128)(2,1)S(1)}, bf16[2,96,384]{2,1,0:T(8,128)(2,1)S(1)}, u32[]{:S(2)}, u32[]{:S(2)}) collective-permute-start(bf16[2,96,384]{2,1,0:T(8,128)(2,1)S(1)} %collective-permute-done.17.a_ref), channel_id=1, source_target_pairs={{0,4},{1,5},{2,6},{3,7},{4,0},{5,1},{6,2},{7,3},{8,12},{9,13},{10,... | collective-permute-start | bytes 442376 | tf_op jit(solution)/shard_map/ppermute | solution.py:207
  71.1 7.0 %collective-permute-start.7 = (bf16[4,96,384]{2,1,0:T(8,128)(2,1)S(1)}, bf16[4,96,384]{2,1,0:T(8,128)(2,1)S(1)}, u32[]{:S(2)}, u32[]{:S(2)}) collective-permute-start(bf16[4,96,384]{2,1,0:T(8,128)(2,1)S(1)} %shard_map.79.refs_0_), channel_id=1, source_target_pairs={{0,4},{1,5},{2,6},{3,7},{4,0},{5,1},{6,2},{7,3},{8,12},{9,13},{10,... | collective-permute-start | bytes 884744 | tf_op jit(solution)/shard_map/ppermute | solution.py:207
  74.0 5.7 %collective-permute-start.13 = (bf16[4,96,384]{2,1,0:T(8,128)(2,1)S(1)}, bf16[4,96,384]{2,1,0:T(8,128)(2,1)S(1)}, u32[]{:S(2)}, u32[]{:S(2)}) collective-permute-start(bf16[4,96,384]{2,1,0:T(8,128)(2,1)S(1)} %shard_map.84.refs_1_), channel_id=1, source_target_pairs={{0,1},{1,0},{2,3},{3,2},{4,5},{5,4},{6,7},{7,6},{8,9},{9,8},{10,11... | collective-permute-start | bytes 884744 | tf_op jit(solution)/shard_map/ppermute | solution.py:207
  75.0 6.9 %collective-permute-start.19 = (bf16[4,96,384]{2,1,0:T(8,128)(2,1)S(1)}, bf16[4,96,384]{2,1,0:T(8,128)(2,1)S(1)}, u32[]{:S(2)}, u32[]{:S(2)}) collective-permute-start(bf16[4,96,384]{2,1,0:T(8,128)(2,1)S(1)} %shard_map.89.refs_1_), channel_id=1, source_target_pairs={{0,3},{1,2},{2,1},{3,0},{4,7},{5,6},{6,5},{7,4},{8,11},{9,10},{10,... | collective-permute-start | bytes 884744 | tf_op jit(solution)/shard_map/ppermute | solution.py:207

commit v2 on v1

--- a/solution.py
+++ b/solution.py
@@ -11,6 +11,7 @@
 HD = 128
 ORDERS = ((4, 1, 3), (1, 3, 4), (3, 4, 1))
 CHUNK = 16
+LOADS = 3
 F32, BF16 = jnp.float32, jnp.bfloat16
 
 
@@ -53,19 +54,25 @@
     return pl.ds(pl.multiple_of(target * size, size), size)
 
 
-def keys_kernel(level_ref, x_hbm, mod_hbm, w_hbm, kv_ref, normed_ref, x_ref, mod_ref, w_ref, sems):
+def keys_kernel(level_ref, x_hbm, mod_hbm, w_hbm, kv_ref, q_ref, gate_ref, x_ref, normed_ref, mod_ref, w_ref, sems):
     rows, width = x_ref.shape
     level = level_ref[0]
     first = pl.multiple_of(level // 8 * 8, 8)
-    copy_x = pltpu.make_async_copy(x_hbm, x_ref, sems.at[0])
-    copy_mod = pltpu.make_async_copy(mod_hbm.at[pl.ds(first, 8), pl.ds(0, 2 * width)], mod_ref, sems.at[1])
-    copy_k = pltpu.make_async_copy(w_hbm.at[1], w_ref.at[0], sems.at[2])
-    copy_v = pltpu.make_async_copy(w_hbm.at[2], w_ref.at[1], sems.at[3])
-    copy_x.start()
+    copy_mod = pltpu.make_async_copy(mod_hbm.at[pl.ds(first, 8)], mod_ref, sems.at[0])
+    copy_k = pltpu.make_async_copy(w_hbm.at[1], w_ref.at[0], sems.at[1])
+    copy_v = pltpu.make_async_copy(w_hbm.at[2], w_ref.at[1], sems.at[2])
+    copy_q = pltpu.make_async_copy(w_hbm.at[0], w_ref.at[2], sems.at[3])
+    part = rows // LOADS
+    copy_x = []
+    for i in range(LOADS):
+        at = pl.ds(i * part, part)
+        copy_x.append(pltpu.make_async_copy(x_hbm.at[at], x_ref.at[at], sems.at[4 + i]))
     copy_mod.start()
+    for copy in copy_x:
+        copy.start()
     copy_k.start()
     copy_v.start()
-    copy_x.wait()
+    copy_q.start()
     copy_mod.wait()
     row = pl.ds(level % 8, 1)
 
@@ -76,15 +83,21 @@
         centered = x - mean
         variance = jnp.mean(centered * centered, axis=-1, keepdims=True)
         scaled = centered * lax.rsqrt(variance + 1e-06)
-        normed = scaled * (1.0 + mod_ref[row, width:]) + mod_ref[row, :width]
+        normed = scaled * (1.0 + mod_ref[row, width : 2 * width]) + mod_ref[row, :width]
         normed_ref[at, :] = normed.astype(BF16)
         return carry
 
-    lax.fori_loop(0, rows // CHUNK, step, 0, unroll=3)
+    steps = part // CHUNK
+    for i, copy in enumerate(copy_x):
+        copy.wait()
+        lax.fori_loop(i * steps, (i + 1) * steps, step, 0, unroll=steps)
+    gate_ref[...] = mod_ref[row, 2 * width :]
     copy_k.wait()
     kv_ref[0] = dot(normed_ref[...], w_ref[0]).astype(BF16)
     copy_v.wait()
     kv_ref[1] = dot(normed_ref[...], w_ref[1]).astype(BF16)
+    copy_q.wait()
+    q_ref[...] = dot(normed_ref[...], w_ref[2]).astype(BF16)
 
 
 def masked(scores, limit):
@@ -92,22 +105,8 @@
     return jnp.where(spots < limit, scores * (1.0 / math.sqrt(HD)), -jnp.inf)
 
 
-def self_kernel(
-    meta_ref, level_ref, counts_ref, normed_ref, w_hbm, mod_hbm, kv_ref, q_ref, o_ref, m_ref, l_ref, gate_ref, w_ref, mod_ref, sems
-):
-    rows, width = normed_ref.shape
-    level = level_ref[0]
-    first = pl.multiple_of(level // 8 * 8, 8)
-    copy = pltpu.make_async_copy(w_hbm.at[0], w_ref, sems.at[0])
-    copy_mod = pltpu.make_async_copy(
-        mod_hbm.at[pl.ds(first, 8), pl.ds(2 * width, width)], mod_ref, sems.at[1]
-    )
-    copy.start()
-    copy_mod.start()
-    copy_mod.wait()
-    gate_ref[...] = mod_ref[pl.ds(level % 8, 1), :]
-    copy.wait()
-    q_ref[...] = dot(normed_ref[...], w_ref[...]).astype(BF16)
+def self_kernel(meta_ref, counts_ref, q_ref, kv_ref, o_ref, m_ref, l_ref):
+    rows = q_ref.shape[0]
     limit = counts_ref[meta_ref[0]]
     for head in range(q_ref.shape[1] // HD):
         at = slice(head * HD, (head + 1) * HD)
@@ -179,16 +178,16 @@
     out_ref[half:] = b_ref[...]
 
 
-def place_kernel(chain, meta_ref, *refs):
-    own_ref, got_ref, out, sems = refs[-4:]
-    part, size = own_ref.shape[1:]
-    d1, d2, d3 = ORDERS[chain]
+def place_kernel(meta_ref, *refs):
+    pieces, out, sems = refs[:-2], refs[-2], refs[-1]
+    part, size = pieces[0].shape[1:]
     copies = []
-    for i, step in enumerate(combos((d1, d2, d3))):
-        piece = (own_ref if i < 4 else got_ref).at[i % 4]
-        to = out.at[pl.ds(chain * part, part), columns(meta_ref[1] ^ step, size)]
-        copies.append(pltpu.make_async_copy(piece, to, sems.at[i]))
-        copies[-1].start()
+    for c, dims in enumerate(ORDERS):
+        for i, step in enumerate(combos(dims)):
+            piece = pieces[2 * c + i // 4].at[i % 4]
+            to = out.at[pl.ds(c * part, part), columns(meta_ref[1] ^ step, size)]
+            copies.append(pltpu.make_async_copy(piece, to, sems.at[len(copies)]))
+            copies[-1].start()
     for copy in copies:
         copy.wait()
 
@@ -206,39 +205,39 @@
     def swap(array, step):
         return lax.ppermute(array, "head", [(i, i ^ step) for i in range(n_head)])
 
-    kv, normed = pl.pallas_call(
+    kv, query, gate = pl.pallas_call(
         keys_kernel,
-        out_shape=(shape((2, rows, size), BF16), shape((rows, width), BF16)),
+        out_shape=(shape((2, rows, size), BF16), shape((rows, size), BF16), shape((1, width), F32)),
         in_specs=smem() + hbm(3),
-        out_specs=vmem(2),
+        out_specs=vmem(3),
         scratch_shapes=[
             pltpu.VMEM((rows, width), BF16),
-            pltpu.VMEM((8, 2 * width), F32),
-            pltpu.VMEM((2, width, size), BF16),
-            pltpu.SemaphoreType.DMA((4,)),
+            pltpu.VMEM((rows, width), BF16),
+            pltpu.VMEM((8, 3 * width), F32),
+            pltpu.VMEM((3, width, size), BF16),
+            pltpu.SemaphoreType.DMA((4 + LOADS,)),
         ],
-        compiler_params=params(32),
+        compiler_params=params(53),
         cost_estimate=cost(4 * rows * width * size, 4 * width * size),
     )(levels, latents, modulation, weight)
 
-    pairs = [(i, i + 1) for i in range(1, n_queue - 1, 2)]
-    cross = lax.ppermute(kv, "queue", pairs + [(j, i) for i, j in pairs])
-    pairs = [(i, i + 1) for i in range(0, n_queue, 2)]
-    chip = lax.ppermute(kv, "queue", pairs + [(j, i) for i, j in pairs])
-
-    query, acc, top, total, gate = pl.pallas_call(
+    chip = lax.ppermute(kv, "queue", [(i, i ^ 1) for i in range(n_queue)])
+    route = []
+    for i in range(n_queue):
+        j = i - 1 + i % 2 * 2
+        for k in range(n_head):
+            there = j * n_head + k if 0 <= j < n_queue else i * n_head + (k ^ 1)
+            route.append((i * n_head + k, there))
+    cross = lax.ppermute(kv, ("queue", "head"), route)
+
+    acc, top, total = pl.pallas_call(
         self_kernel,
-        out_shape=(shape((rows, size), BF16),) + (shape((rows, size), F32),) * 3 + (shape((1, width), F32),),
-        in_specs=smem(3) + vmem() + hbm(2) + vmem(),
-        out_specs=vmem(5),
-        scratch_shapes=[
-            pltpu.VMEM((width, size), BF16),
-            pltpu.VMEM((8, width), F32),
-            pltpu.SemaphoreType.DMA((2,)),
-        ],
-        compiler_params=params(32),
-        cost_estimate=cost(4 * rows * width * size, 2 * width * size),
-    )(meta, levels, counts, normed, weight, modulation, kv)
+        out_shape=(shape((rows, size), F32),) * 3,
+        in_specs=smem(2) + vmem(2),
+        out_specs=vmem(3),
+        compiler_params=params(24),
+        cost_estimate=cost(1, 1),
+    )(meta, counts, query, kv)
 
     parts = pl.pallas_call(
         join_kernel,
@@ -280,20 +279,16 @@
             out_specs=vmem()[0],
             **small,
         )(moved, got)
-        ready.append((four, swap(four, d1)))
-
-    out = None
-    for c, pieces in enumerate(ready):
-        out = pl.pallas_call(
-            functools.partial(place_kernel, c),
-            out_shape=shape((rows, width), BF16),
-            in_specs=smem() + hbm(c > 0) + vmem(2),
-            out_specs=hbm()[0],
-            scratch_shapes=[pltpu.SemaphoreType.DMA((8,))],
-            input_output_aliases={1: 0} if c else {},
-            **small,
-        )(meta, *([out] if c else []), *pieces)
-    return out
+        ready += [four, swap(four, d1)]
+
+    return pl.pallas_call(
+        place_kernel,
+        out_shape=shape((rows, width), BF16),
+        in_specs=smem() + vmem(len(ready)),
+        out_specs=hbm()[0],
+        scratch_shapes=[pltpu.SemaphoreType.DMA((4 * len(ready),))],
+        **small,
+    )(meta, *ready)
 
 
 def solution(mesh):

time: 83.9 us -> 77.8 us (0.927)
  local copies, waits for them, and re-layouts: 8.57 us -> 0.02 us
  waiting for transfers between devices: 31.2 us -> 34.6 us
  Pallas kernels: 18.4 us -> 15.8 us
  starting transfers between devices: 24.1 us -> 26.2 us
    unnamed x18 -> x8, local copies, waits for them, and re-layouts: 8.57 us -> 0.02 us
    ppermute x2, waiting for transfers between devices: 7.09 us -> 11.3 us  [the longest x1 11.3 us: body(): cross = lax.ppermute(kv, ('queue', 'head'), route)]
    ppermute x15, starting transfers between devices: 17.5 us -> 21.3 us  [swap(): return lax.ppermute(array, 'head', [(i, i ^ step) for i in range(n_head)])]
    pallas_call x4 -> x2, Pallas kernels: 7.15 us -> 3.57 us  [the longest x1 1.95 us: body(): pl.pallas_call(place_kernel, out_shape=shape((rows, width), BF16), in_spe...]
    ppermute x3, waiting for transfers between devices: 13.9 us -> 10.8 us  [body(): lax.ppermute(fresh, 'queue', [(i, (i - 1) % n_queue) for i in range(n_que...]
    ppermute x15, waiting for transfers between devices: 10.2 us -> 12.5 us  [swap(): return lax.ppermute(array, 'head', [(i, i ^ step) for i in range(n_head)])]
    ppermute x2, starting transfers between devices: 6.43 us -> 4.61 us  [the longest x1 3.85 us: body(): cross = lax.ppermute(kv, ('queue', 'head'), route)]
    pallas_call x1, Pallas kernels: 5.01 us -> 5.91 us  [body(): pl.pallas_call(keys_kernel, out_shape=(shape((2, rows, size), BF16), shap...]
  transfers between devices with their start and end apart: 20 -> 20, of which waited for: 15 -> 13; matrix products, arithmetic and copies ran while one was open for 0% -> 0% of each run, Pallas kernels for 10% -> 5%
where the time goes in v2:
time: 77.8 us; the launch traced here: 77.6 us
  waiting for transfers between devices  34.6 us (44%)
  starting transfers between devices  26.2 us (34%)
  Pallas kernels  15.8 us (20%)
  between operations  0.99 us (1%)
    ppermute x15, starting transfers between devices, swap(): return lax.ppermute(array, 'head', [(i, i ^ step) for i in range(n_head)])  21.3 us
    ppermute x15, waiting for transfers between devices, swap(): return lax.ppermute(array, 'head', [(i, i ^ step) for i in range(n_head)])  12.5 us
    ppermute x1, waiting for transfers between devices, body(): cross = lax.ppermute(kv, ('queue', 'head'), route)  11.3 us
    ppermute x3, waiting for transfers between devices, body(): lax.ppermute(fresh, 'queue', [(i, (i - 1) % n_queue) for i in range(n_que...  10.8 us
    pallas_call x1, Pallas kernels, body(): pl.pallas_call(keys_kernel, out_shape=(shape((2, rows, size), BF16), shap...  5.91 us
    pallas_call x1, Pallas kernels, body(): pl.pallas_call(join_kernel, out_shape=(shape((n_head // 2, part, size), B...  4.05 us
    ppermute x1, starting transfers between devices, body(): cross = lax.ppermute(kv, ('queue', 'head'), route)  3.85 us
    pallas_call x1, Pallas kernels, body(): pl.pallas_call(place_kernel, out_shape=shape((rows, width), BF16), in_spe...  1.95 us
  transfers between devices with their start and end apart: 20, of which 13 were waited for; matrix products, arithmetic and copies ran while one was open for 0% of the time, Pallas kernels for 5%

profile of v2, /device:TPU:89, one launch (start us, length us, event | category | flops | bytes accessed | tf_op | source)
XLA Modules:
  0.0 77.6 jit_solution(18121363332070430700)
XLA Ops:
  0.7 5.9 %shard_map.73 = (bf16[2,288,384]{2,1,0:T(8,128)(2,1)S(1)}, bf16[288,384]{1,0:T(8,128)(2,1)S(1)}, f32[1,3072]{1,0:T(1,128)S(1)}) custom-call(s32[1]{0:T(128)S(6)} %copy.8.level_ref, bf16[288,3072]{1,0:T(8,128)(2,1)} %x_ref.5, f32[16,9216]{1,0:T(8,128)} %mod_hbm.1, bf16[3,3072,384]{2,1,0:T(8,128)(2,1)} %bitcast.5), custom_call_target="tpu_custom_call" | custom-call | flops 1358954496 | bytes 4718592 | tf_op jit(solution)/shard_map/pallas_call | solution.py:208
  6.6 0.8 collective-permute-start.1
  7.4 3.8 %collective-permute-start = (bf16[2,288,384]{2,1,0:T(8,128)(2,1)S(1)}, bf16[2,288,384]{2,1,0:T(8,128)(2,1)}, u32[]{:S(2)}, u32[]{:S(2)}) collective-permute-start(bf16[2,288,384]{2,1,0:T(8,128)(2,1)S(1)} %get-tuple-element.25.kv_ref), channel_id=1, source_target_pairs={{0,1},{1,0},{2,3},{3,2},{4,5},{5,4},{6,7},{7,6},{8,16},{9,17},{10,... | collective-permute-start | bytes 1327112 | tf_op jit(solution)/shard_map/ppermute | solution.py:231
  11.2 0.1 pad_add_fusion.meta_ref
  11.3 1.6 %shard_map.74 = (f32[288,384]{1,0:T(8,128)S(1)}, f32[288,384]{1,0:T(8,128)S(1)}, f32[288,384]{1,0:T(8,128)S(1)}) custom-call(s32[2]{0:T(128)S(1)} %pad_add_fusion.meta_ref, s32[32]{0:T(128)S(1)} %copy-done.1, bf16[288,384]{1,0:T(8,128)(2,1)S(1)} %get-tuple-element.24.q_ref, bf16[2,288,384]{2,1,0:T(8,128)(2,1)S(1)} %get-tuple-element.25.kv_ref), custom_call_target="tpu_custom_call" | custom-call | flops 1 | bytes 1 | tf_op jit(solution)/shard_map/pallas_call | solution.py:233
  12.9 11.3 %collective-permute-done.cross_ref = bf16[2,288,384]{2,1,0:T(8,128)(2,1)} collective-permute-done((bf16[2,288,384]{2,1,0:T(8,128)(2,1)S(1)}, bf16[2,288,384]{2,1,0:T(8,128)(2,1)}, u32[]{:S(2)}, u32[]{:S(2)}) %collective-permute-start) | collective-permute-done | bytes 442400 | tf_op jit(solution)/shard_map/ppermute | solution.py:231
  24.3 4.1 %shard_map.75 = (bf16[4,96,384]{2,1,0:T(8,128)(2,1)S(1)}, bf16[4,96,384]{2,1,0:T(8,128)(2,1)S(1)}, bf16[4,96,384]{2,1,0:T(8,128)(2,1)S(1)}, bf16[4,96,384]{2,1,0...) custom-call(s32[2]{0:T(128)S(1)} %pad_add_fusion.meta_ref, s32[32]{0:T(128)S(1)} %copy-done.1, ...), custom_call_target="tpu_custom_call" | custom-call | flops 1358954496 | bytes 2359296 | tf_op jit(solution)/shard_map/pallas_call | solution.py:242
  28.3 0.0 copy-start
  28.3 0.1 collective-permute-start.2
  28.4 1.3 %collective-permute-start.8 = (bf16[4,96,384]{2,1,0:T(8,128)(2,1)S(1)}, bf16[4,96,384]{2,1,0:T(8,128)(2,1)S(1)}, u32[]{:S(2)}, u32[]{:S(2)}) collective-permute-start(bf16[4,96,384]{2,1,0:T(8,128)(2,1)S(1)} %get-tuple-element.34), channel_id=1, source_target_pairs={{0,1},{1,0},{2,3},{3,2},{4,5},{5,4},{6,7},{7,6},{8,9},{9,8},{10,11... | collective-permute-start | bytes 884744 | tf_op jit(solution)/shard_map/ppermute | solution.py:206
  29.7 1.8 %collective-permute-start.14 = (bf16[4,96,384]{2,1,0:T(8,128)(2,1)S(1)}, bf16[4,96,384]{2,1,0:T(8,128)(2,1)S(1)}, u32[]{:S(2)}, u32[]{:S(2)}) collective-permute-start(bf16[4,96,384]{2,1,0:T(8,128)(2,1)S(1)} %get-tuple-element.38), channel_id=1, source_target_pairs={{0,3},{1,2},{2,1},{3,0},{4,7},{5,6},{6,5},{7,4},{8,11},{9,10},{10,... | collective-permute-start | bytes 884744 | tf_op jit(solution)/shard_map/ppermute | solution.py:206
  31.6 2.7 %collective-permute-done.2.got_ref = bf16[4,96,384]{2,1,0:T(8,128)(2,1)S(1)} collective-permute-done((bf16[4,96,384]{2,1,0:T(8,128)(2,1)S(1)}, bf16[4,96,384]{2,1,0:T(8,128)(2,1)S(1)}, u32[]{:S(2)}, u32[]{:S(2)}) %collective-permute-start.2) | collective-permute-done | bytes 294944 | tf_op jit(solution)/shard_map/ppermute | solution.py:206
  34.3 0.1 shard_map.76
  34.4 2.4 %collective-permute-start.3 = (bf16[2,96,384]{2,1,0:T(8,128)(2,1)S(1)}, bf16[2,96,384]{2,1,0:T(8,128)(2,1)S(1)}, u32[]{:S(2)}, u32[]{:S(2)}) collective-permute-start(bf16[2,96,384]{2,1,0:T(8,128)(2,1)S(1)} %get-tuple-element.32), channel_id=1, source_target_pairs={{0,1},{1,0},{2,3},{3,2},{4,5},{5,4},{6,7},{7,6},{8,9},{9,8},{10,11... | collective-permute-start | bytes 442376 | tf_op jit(solution)/shard_map/ppermute | solution.py:206
  36.8 0.0 collective-permute-done.8.got_ref
  36.8 0.1 shard_map.80
  36.9 2.4 %collective-permute-start.9 = (bf16[2,96,384]{2,1,0:T(8,128)(2,1)S(1)}, bf16[2,96,384]{2,1,0:T(8,128)(2,1)S(1)}, u32[]{:S(2)}, u32[]{:S(2)}) collective-permute-start(bf16[2,96,384]{2,1,0:T(8,128)(2,1)S(1)} %get-tuple-element.36), channel_id=1, source_target_pairs={{0,3},{1,2},{2,1},{3,0},{4,7},{5,6},{6,5},{7,4},{8,11},{9,10},{10,... | collective-permute-start | bytes 442376 | tf_op jit(solution)/shard_map/ppermute | solution.py:206
  39.2 0.0 collective-permute-done.14.got_ref
  39.2 0.1 shard_map.84
  39.3 0.5 collective-permute-start.15
  39.8 2.5 %collective-permute-start.4 = (bf16[2,96,384]{2,1,0:T(8,128)(2,1)S(1)}, bf16[2,96,384]{2,1,0:T(8,128)(2,1)S(1)}, u32[]{:S(2)}, u32[]{:S(2)}) collective-permute-start(bf16[2,96,384]{2,1,0:T(8,128)(2,1)S(1)} %shard_map.77.keep_ref), channel_id=1, source_target_pairs={{0,3},{1,2},{2,1},{3,0},{4,7},{5,6},{6,5},{7,4},{8,11},{9,10},{10,... | collective-permute-start | bytes 442376 | tf_op jit(solution)/shard_map/ppermute | solution.py:206
  42.3 0.0 collective-permute-done.9.got_ref
  42.3 0.7 collective-permute-start.10
  43.1 0.3 collective-permute-done.15.got_ref
  43.4 0.7 collective-permute-start.16
  44.2 1.1 %collective-permute-done.4.got_ref = bf16[2,96,384]{2,1,0:T(8,128)(2,1)S(1)} collective-permute-done((bf16[2,96,384]{2,1,0:T(8,128)(2,1)S(1)}, bf16[2,96,384]{2,1,0:T(8,128)(2,1)S(1)}, u32[]{:S(2)}, u32[]{:S(2)}) %collective-permute-start.4) | collective-permute-done | bytes 147488 | tf_op jit(solution)/shard_map/ppermute | solution.py:206
  45.3 0.6 shard_map.78
  45.9 0.1 collective-permute-start.5
  46.0 0.4 collective-permute-done.10.got_ref
  46.4 0.6 shard_map.82
  47.0 0.1 collective-permute-start.11
  47.1 0.4 collective-permute-done.16.got_ref
  47.5 0.6 shard_map.86
  48.1 0.1 collective-permute-start.17
  48.2 8.6 %collective-permute-done.5.a_ref = bf16[2,96,384]{2,1,0:T(8,128)(2,1)S(1)} collective-permute-done((bf16[2,96,384]{2,1,0:T(8,128)(2,1)S(1)}, bf16[2,96,384]{2,1,0:T(8,128)(2,1)S(1)}, u32[]{:S(2)}, u32[]{:S(2)}) %collective-permute-start.5) | collective-permute-done | bytes 147488 | tf_op jit(solution)/shard_map/ppermute | solution.py:273
  56.8 3.4 %collective-permute-start.6 = (bf16[2,96,384]{2,1,0:T(8,128)(2,1)S(1)}, bf16[2,96,384]{2,1,0:T(8,128)(2,1)S(1)}, u32[]{:S(2)}, u32[]{:S(2)}) collective-permute-start(bf16[2,96,384]{2,1,0:T(8,128)(2,1)S(1)} %collective-permute-done.5.a_ref), channel_id=1, source_target_pairs={{0,1},{1,0},{2,3},{3,2},{4,5},{5,4},{6,7},{7,6},{8,9},{9,8},{10,11... | collective-permute-start | bytes 442376 | tf_op jit(solution)/shard_map/ppermute | solution.py:206
  60.2 2.1 %collective-permute-done.11.a_ref = bf16[2,96,384]{2,1,0:T(8,128)(2,1)S(1)} collective-permute-done((bf16[2,96,384]{2,1,0:T(8,128)(2,1)S(1)}, bf16[2,96,384]{2,1,0:T(8,128)(2,1)S(1)}, u32[]{:S(2)}, u32[]{:S(2)}) %collective-permute-start.11) | collective-permute-done | bytes 147488 | tf_op jit(solution)/shard_map/ppermute | solution.py:273
  62.4 2.2 %collective-permute-start.12 = (bf16[2,96,384]{2,1,0:T(8,128)(2,1)S(1)}, bf16[2,96,384]{2,1,0:T(8,128)(2,1)S(1)}, u32[]{:S(2)}, u32[]{:S(2)}) collective-permute-start(bf16[2,96,384]{2,1,0:T(8,128)(2,1)S(1)} %collective-permute-done.11.a_ref), channel_id=1, source_target_pairs={{0,3},{1,2},{2,1},{3,0},{4,7},{5,6},{6,5},{7,4},{8,11},{9,10},{10,... | collective-permute-start | bytes 442376 | tf_op jit(solution)/shard_map/ppermute | solution.py:206
  64.6 0.0 collective-permute-done.17.a_ref
  64.7 1.5 %collective-permute-start.7 = (bf16[4,96,384]{2,1,0:T(8,128)(2,1)S(1)}, bf16[4,96,384]{2,1,0:T(8,128)(2,1)S(1)}, u32[]{:S(2)}, u32[]{:S(2)}) collective-permute-start(bf16[4,96,384]{2,1,0:T(8,128)(2,1)S(1)} %shard_map.79.refs_0_), channel_id=1, source_target_pairs={{0,4},{1,5},{2,6},{3,7},{4,0},{5,1},{6,2},{7,3},{8,12},{9,13},{10,... | collective-permute-start | bytes 884744 | tf_op jit(solution)/shard_map/ppermute | solution.py:206
  66.2 1.4 %collective-permute-done.12.b_ref = bf16[2,96,384]{2,1,0:T(8,128)(2,1)S(1)} collective-permute-done((bf16[2,96,384]{2,1,0:T(8,128)(2,1)S(1)}, bf16[2,96,384]{2,1,0:T(8,128)(2,1)S(1)}, u32[]{:S(2)}, u32[]{:S(2)}) %collective-permute-start.12) | collective-permute-done | bytes 147488 | tf_op jit(solution)/shard_map/ppermute | solution.py:206
  67.6 0.1 collective-permute-start.13
  67.7 0.9 %collective-permute-done.18.b_ref = bf16[2,96,384]{2,1,0:T(8,128)(2,1)S(1)} collective-permute-done((bf16[2,96,384]{2,1,0:T(8,128)(2,1)S(1)}, bf16[2,96,384]{2,1,0:T(8,128)(2,1)S(1)}, u32[]{:S(2)}, u32[]{:S(2)}) %collective-permute-start.18) | collective-permute-done | bytes 147488 | tf_op jit(solution)/shard_map/ppermute | solution.py:206
  68.6 1.7 %collective-permute-start.19 = (bf16[4,96,384]{2,1,0:T(8,128)(2,1)S(1)}, bf16[4,96,384]{2,1,0:T(8,128)(2,1)S(1)}, u32[]{:S(2)}, u32[]{:S(2)}) collective-permute-start(bf16[4,96,384]{2,1,0:T(8,128)(2,1)S(1)} %shard_map.87.refs_4_), channel_id=1, source_target_pairs={{0,3},{1,2},{2,1},{3,0},{4,7},{5,6},{6,5},{7,4},{8,11},{9,10},{10,... | collective-permute-start | bytes 884744 | tf_op jit(solution)/shard_map/ppermute | solution.py:206
  70.3 1.5 %collective-permute-done.7.refs_1_ = bf16[4,96,384]{2,1,0:T(8,128)(2,1)S(1)} collective-permute-done((bf16[4,96,384]{2,1,0:T(8,128)(2,1)S(1)}, bf16[4,96,384]{2,1,0:T(8,128)(2,1)S(1)}, u32[]{:S(2)}, u32[]{:S(2)}) %collective-permute-start.7) | collective-permute-done | bytes 294944 | tf_op jit(solution)/shard_map/ppermute | solution.py:206
  71.8 1.5 %collective-permute-done.13.refs_3_ = bf16[4,96,384]{2,1,0:T(8,128)(2,1)S(1)} collective-permute-done((bf16[4,96,384]{2,1,0:T(8,128)(2,1)S(1)}, bf16[4,96,384]{2,1,0:T(8,128)(2,1)S(1)}, u32[]{:S(2)}, u32[]{:S(2)}) %collective-permute-start.13) | collective-permute-done | bytes 294944 | tf_op jit(solution)/shard_map/ppermute | solution.py:206
  73.3 2.2 %collective-permute-done.19.refs_5_ = bf16[4,96,384]{2,1,0:T(8,128)(2,1)S(1)} collective-permute-done((bf16[4,96,384]{2,1,0:T(8,128)(2,1)S(1)}, bf16[4,96,384]{2,1,0:T(8,128)(2,1)S(1)}, u32[]{:S(2)}, u32[]{:S(2)}) %collective-permute-start.19) | collective-permute-done | bytes 294944 | tf_op jit(solution)/shard_map/ppermute | solution.py:206
  75.5 1.9 %shard_map.88 = bf16[288,3072]{1,0:T(8,128)(2,1)} custom-call(s32[2]{0:T(128)S(1)} %pad_add_fusion.meta_ref, bf16[4,96,384]{2,1,0:T(8,128)(2,1)S(1)} %shard_map.79.refs_0_, bf16[4,96,384]{2,1,0:T(8,128)(2,1)S(1)} %collective-permute-done.7.refs_1_, bf16[4,96,384]{2,1,0:T(8,128)(2,1)S(1)} %shard_map.83.refs_2_, ...), custom_call_target="tpu_custom_call" | custom-call | flops 147456 | bytes 294912 | tf_op jit(solution)/shard_map/pallas_call | solution.py:284
  (17 shorter events, 0.2 us)
Async XLA Ops:
  0.7 10.6 %copy-start.1 = (s32[32]{0:T(128)S(1)}, s32[32]{0:T(128)}, u32[]{:S(2)}) copy-start(s32[32]{0:T(128)} %counts_ref.3) | copy-start | bytes 388
  0.7 23.6 %copy-start.2 = (bf16[384,3072]{1,0:T(8,128)(2,1)S(1)}, bf16[384,3072]{1,0:T(8,128)(2,1)}, u32[]{:S(2)}) copy-start(bf16[384,3072]{1,0:T(8,128)(2,1)} %w_ref.1) | copy-start | bytes 7077892
  0.7 23.6 %copy-start.3 = (s32[32,2]{0,1:T(2,128)S(1)}, s32[32,2]{0,1:T(2,128)}, u32[]{:S(2)}) copy-start(s32[32,2]{0,1:T(2,128)} %param.10) | copy-start | bytes 772
  6.6 6.3 %collective-permute-start.1 = (bf16[2,288,384]{2,1,0:T(8,128)(2,1)S(1)}, bf16[2,288,384]{2,1,0:T(8,128)(2,1)S(1)}, u32[]{:S(2)}, u32[]{:S(2)}) collective-permute-start(bf16[2,288,384]{2,1,0:T(8,128)(2,1)S(1)} %get-tuple-element.25.kv_ref), channel_id=1, source_target_pairs={{0,8},{8,0},{16,24},{24,16},{32,40},{40,32},{48,56},{56,48},{64,72... | collective-permute-start | bytes 1327112 | tf_op jit(solution)/shard_map/ppermute | solution.py:224
  7.4 16.9 %collective-permute-start = (bf16[2,288,384]{2,1,0:T(8,128)(2,1)S(1)}, bf16[2,288,384]{2,1,0:T(8,128)(2,1)}, u32[]{:S(2)}, u32[]{:S(2)}) collective-permute-start(bf16[2,288,384]{2,1,0:T(8,128)(2,1)S(1)} %get-tuple-element.25.kv_ref), channel_id=1, source_target_pairs={{0,1},{1,0},{2,3},{3,2},{4,5},{5,4},{6,7},{7,6},{8,16},{9,17},{10,... | collective-permute-start | bytes 1327112 | tf_op jit(solution)/shard_map/ppermute | solution.py:231
  28.3 17.0 %copy-start = (bf16[288,3072]{1,0:T(8,128)(2,1)S(1)}, bf16[288,3072]{1,0:T(8,128)(2,1)}, u32[]{:S(2)}) copy-start(bf16[288,3072]{1,0:T(8,128)(2,1)} %x_ref.5) | copy-start | bytes 5308420
  28.3 6.0 %collective-permute-start.2 = (bf16[4,96,384]{2,1,0:T(8,128)(2,1)S(1)}, bf16[4,96,384]{2,1,0:T(8,128)(2,1)S(1)}, u32[]{:S(2)}, u32[]{:S(2)}) collective-permute-start(bf16[4,96,384]{2,1,0:T(8,128)(2,1)S(1)} %get-tuple-element.30), channel_id=1, source_target_pairs={{0,4},{1,5},{2,6},{3,7},{4,0},{5,1},{6,2},{7,3},{8,12},{9,13},{10,... | collective-permute-start | bytes 884744 | tf_op jit(solution)/shard_map/ppermute | solution.py:206
  28.4 8.3 %collective-permute-start.8 = (bf16[4,96,384]{2,1,0:T(8,128)(2,1)S(1)}, bf16[4,96,384]{2,1,0:T(8,128)(2,1)S(1)}, u32[]{:S(2)}, u32[]{:S(2)}) collective-permute-start(bf16[4,96,384]{2,1,0:T(8,128)(2,1)S(1)} %get-tuple-element.34), channel_id=1, source_target_pairs={{0,1},{1,0},{2,3},{3,2},{4,5},{5,4},{6,7},{7,6},{8,9},{9,8},{10,11... | collective-permute-start | bytes 884744 | tf_op jit(solution)/shard_map/ppermute | solution.py:206
  29.7 9.5 %collective-permute-start.14 = (bf16[4,96,384]{2,1,0:T(8,128)(2,1)S(1)}, bf16[4,96,384]{2,1,0:T(8,128)(2,1)S(1)}, u32[]{:S(2)}, u32[]{:S(2)}) collective-permute-start(bf16[4,96,384]{2,1,0:T(8,128)(2,1)S(1)} %get-tuple-element.38), channel_id=1, source_target_pairs={{0,3},{1,2},{2,1},{3,0},{4,7},{5,6},{6,5},{7,4},{8,11},{9,10},{10,... | collective-permute-start | bytes 884744 | tf_op jit(solution)/shard_map/ppermute | solution.py:206
  34.4 5.4 %collective-permute-start.3 = (bf16[2,96,384]{2,1,0:T(8,128)(2,1)S(1)}, bf16[2,96,384]{2,1,0:T(8,128)(2,1)S(1)}, u32[]{:S(2)}, u32[]{:S(2)}) collective-permute-start(bf16[2,96,384]{2,1,0:T(8,128)(2,1)S(1)} %get-tuple-element.32), channel_id=1, source_target_pairs={{0,1},{1,0},{2,3},{3,2},{4,5},{5,4},{6,7},{7,6},{8,9},{9,8},{10,11... | collective-permute-start | bytes 442376 | tf_op jit(solution)/shard_map/ppermute | solution.py:206
  36.9 5.4 %collective-permute-start.9 = (bf16[2,96,384]{2,1,0:T(8,128)(2,1)S(1)}, bf16[2,96,384]{2,1,0:T(8,128)(2,1)S(1)}, u32[]{:S(2)}, u32[]{:S(2)}) collective-permute-start(bf16[2,96,384]{2,1,0:T(8,128)(2,1)S(1)} %get-tuple-element.36), channel_id=1, source_target_pairs={{0,3},{1,2},{2,1},{3,0},{4,7},{5,6},{6,5},{7,4},{8,11},{9,10},{10,... | collective-permute-start | bytes 442376 | tf_op jit(solution)/shard_map/ppermute | solution.py:206
  39.3 4.1 %collective-permute-start.15 = (bf16[2,96,384]{2,1,0:T(8,128)(2,1)S(1)}, bf16[2,96,384]{2,1,0:T(8,128)(2,1)S(1)}, u32[]{:S(2)}, u32[]{:S(2)}) collective-permute-start(bf16[2,96,384]{2,1,0:T(8,128)(2,1)S(1)} %get-tuple-element.40), channel_id=1, source_target_pairs={{0,4},{1,5},{2,6},{3,7},{4,0},{5,1},{6,2},{7,3},{8,12},{9,13},{10,... | collective-permute-start | bytes 442376 | tf_op jit(solution)/shard_map/ppermute | solution.py:206
  39.8 5.5 %collective-permute-start.4 = (bf16[2,96,384]{2,1,0:T(8,128)(2,1)S(1)}, bf16[2,96,384]{2,1,0:T(8,128)(2,1)S(1)}, u32[]{:S(2)}, u32[]{:S(2)}) collective-permute-start(bf16[2,96,384]{2,1,0:T(8,128)(2,1)S(1)} %shard_map.77.keep_ref), channel_id=1, source_target_pairs={{0,3},{1,2},{2,1},{3,0},{4,7},{5,6},{6,5},{7,4},{8,11},{9,10},{10,... | collective-permute-start | bytes 442376 | tf_op jit(solution)/shard_map/ppermute | solution.py:206
  42.3 4.1 %collective-permute-start.10 = (bf16[2,96,384]{2,1,0:T(8,128)(2,1)S(1)}, bf16[2,96,384]{2,1,0:T(8,128)(2,1)S(1)}, u32[]{:S(2)}, u32[]{:S(2)}) collective-permute-start(bf16[2,96,384]{2,1,0:T(8,128)(2,1)S(1)} %shard_map.81.keep_ref), channel_id=1, source_target_pairs={{0,4},{1,5},{2,6},{3,7},{4,0},{5,1},{6,2},{7,3},{8,12},{9,13},{10,... | collective-permute-start | bytes 442376 | tf_op jit(solution)/shard_map/ppermute | solution.py:206
  43.4 4.1 %collective-permute-start.16 = (bf16[2,96,384]{2,1,0:T(8,128)(2,1)S(1)}, bf16[2,96,384]{2,1,0:T(8,128)(2,1)S(1)}, u32[]{:S(2)}, u32[]{:S(2)}) collective-permute-start(bf16[2,96,384]{2,1,0:T(8,128)(2,1)S(1)} %shard_map.85.keep_ref), channel_id=1, source_target_pairs={{0,1},{1,0},{2,3},{3,2},{4,5},{5,4},{6,7},{7,6},{8,9},{9,8},{10,11... | collective-permute-start | bytes 442376 | tf_op jit(solution)/shard_map/ppermute | solution.py:206
  45.9 10.9 %collective-permute-start.5 = (bf16[2,96,384]{2,1,0:T(8,128)(2,1)S(1)}, bf16[2,96,384]{2,1,0:T(8,128)(2,1)S(1)}, u32[]{:S(2)}, u32[]{:S(2)}) collective-permute-start(bf16[2,96,384]{2,1,0:T(8,128)(2,1)S(1)} %shard_map.78), channel_id=1, source_target_pairs={{0,248},{8,0},{16,8},{24,16},{32,24},{40,32},{48,40},{56,48},{64,5... | collective-permute-start | bytes 442376 | tf_op jit(solution)/shard_map/ppermute | solution.py:273
  47.0 15.3 %collective-permute-start.11 = (bf16[2,96,384]{2,1,0:T(8,128)(2,1)S(1)}, bf16[2,96,384]{2,1,0:T(8,128)(2,1)S(1)}, u32[]{:S(2)}, u32[]{:S(2)}) collective-permute-start(bf16[2,96,384]{2,1,0:T(8,128)(2,1)S(1)} %shard_map.82), channel_id=1, source_target_pairs={{0,248},{8,0},{16,8},{24,16},{32,24},{40,32},{48,40},{56,48},{64,5... | collective-permute-start | bytes 442376 | tf_op jit(solution)/shard_map/ppermute | solution.py:273
  48.1 16.5 %collective-permute-start.17 = (bf16[2,96,384]{2,1,0:T(8,128)(2,1)S(1)}, bf16[2,96,384]{2,1,0:T(8,128)(2,1)S(1)}, u32[]{:S(2)}, u32[]{:S(2)}) collective-permute-start(bf16[2,96,384]{2,1,0:T(8,128)(2,1)S(1)} %shard_map.86), channel_id=1, source_target_pairs={{0,248},{8,0},{16,8},{24,16},{32,24},{40,32},{48,40},{56,48},{64,5... | collective-permute-start | bytes 442376 | tf_op jit(solution)/shard_map/ppermute | solution.py:273
  56.8 7.8 %collective-permute-start.6 = (bf16[2,96,384]{2,1,0:T(8,128)(2,1)S(1)}, bf16[2,96,384]{2,1,0:T(8,128)(2,1)S(1)}, u32[]{:S(2)}, u32[]{:S(2)}) collective-permute-start(bf16[2,96,384]{2,1,0:T(8,128)(2,1)S(1)} %collective-permute-done.5.a_ref), channel_id=1, source_target_pairs={{0,1},{1,0},{2,3},{3,2},{4,5},{5,4},{6,7},{7,6},{8,9},{9,8},{10,11... | collective-permute-start | bytes 442376 | tf_op jit(solution)/shard_map/ppermute | solution.py:206
  62.4 5.2 %collective-permute-start.12 = (bf16[2,96,384]{2,1,0:T(8,128)(2,1)S(1)}, bf16[2,96,384]{2,1,0:T(8,128)(2,1)S(1)}, u32[]{:S(2)}, u32[]{:S(2)}) collective-permute-start(bf16[2,96,384]{2,1,0:T(8,128)(2,1)S(1)} %collective-permute-done.11.a_ref), channel_id=1, source_target_pairs={{0,3},{1,2},{2,1},{3,0},{4,7},{5,6},{6,5},{7,4},{8,11},{9,10},{10,... | collective-permute-start | bytes 442376 | tf_op jit(solution)/shard_map/ppermute | solution.py:206
  64.6 4.0 %collective-permute-start.18 = (bf16[2,96,384]{2,1,0:T(8,128)(2,1)S(1)}, bf16[2,96,384]{2,1,0:T(8,128)(2,1)S(1)}, u32[]{:S(2)}, u32[]{:S(2)}) collective-permute-start(bf16[2,96,384]{2,1,0:T(8,128)(2,1)S(1)} %collective-permute-done.17.a_ref), channel_id=1, source_target_pairs={{0,4},{1,5},{2,6},{3,7},{4,0},{5,1},{6,2},{7,3},{8,12},{9,13},{10,... | collective-permute-start | bytes 442376 | tf_op jit(solution)/shard_map/ppermute | solution.py:206
  64.7 7.1 %collective-permute-start.7 = (bf16[4,96,384]{2,1,0:T(8,128)(2,1)S(1)}, bf16[4,96,384]{2,1,0:T(8,128)(2,1)S(1)}, u32[]{:S(2)}, u32[]{:S(2)}) collective-permute-start(bf16[4,96,384]{2,1,0:T(8,128)(2,1)S(1)} %shard_map.79.refs_0_), channel_id=1, source_target_pairs={{0,4},{1,5},{2,6},{3,7},{4,0},{5,1},{6,2},{7,3},{8,12},{9,13},{10,... | collective-permute-start | bytes 884744 | tf_op jit(solution)/shard_map/ppermute | solution.py:206
  67.6 5.7 %collective-permute-start.13 = (bf16[4,96,384]{2,1,0:T(8,128)(2,1)S(1)}, bf16[4,96,384]{2,1,0:T(8,128)(2,1)S(1)}, u32[]{:S(2)}, u32[]{:S(2)}) collective-permute-start(bf16[4,96,384]{2,1,0:T(8,128)(2,1)S(1)} %shard_map.83.refs_2_), channel_id=1, source_target_pairs={{0,1},{1,0},{2,3},{3,2},{4,5},{5,4},{6,7},{7,6},{8,9},{9,8},{10,11... | collective-permute-start | bytes 884744 | tf_op jit(solution)/shard_map/ppermute | solution.py:206
  68.6 6.9 %collective-permute-start.19 = (bf16[4,96,384]{2,1,0:T(8,128)(2,1)S(1)}, bf16[4,96,384]{2,1,0:T(8,128)(2,1)S(1)}, u32[]{:S(2)}, u32[]{:S(2)}) collective-permute-start(bf16[4,96,384]{2,1,0:T(8,128)(2,1)S(1)} %shard_map.87.refs_4_), channel_id=1, source_target_pairs={{0,3},{1,2},{2,1},{3,0},{4,7},{5,6},{6,5},{7,4},{8,11},{9,10},{10,... | collective-permute-start | bytes 884744 | tf_op jit(solution)/shard_map/ppermute | solution.py:206

commit v3 on v2

v3 whole, which is shorter than its diff:
```python
import functools
import math

import jax
import jax.numpy as jnp
from jax import lax
from jax.experimental import pallas as pl
from jax.experimental.pallas import tpu as pltpu
from jax.sharding import PartitionSpec as P

HD = 128
ROWS = (96, 96, 96)
ORDERS = ((4, 1, 3), (1, 3, 4), (3, 4, 1))
HALVES = (True, True, True)
GATHER = (False, False, False)
CHUNK = 16
LOADS = 3
NEAR = 48
F32, BF16 = jnp.float32, jnp.bfloat16


def vmem(n=1):
    return [pl.BlockSpec(memory_space=pltpu.VMEM)] * n


def smem(n=1):
    return [pl.BlockSpec(memory_space=pltpu.SMEM)] * n


def hbm(n=1):
    return [pl.BlockSpec(memory_space=pltpu.HBM)] * n


def params(mib):
    return pltpu.CompilerParams(vmem_limit_bytes=mib * 1024 * 1024)


def cost(flops, size):
    return pl.CostEstimate(flops=flops, bytes_accessed=size, transcendentals=0)


def dot(a, b):
    return jnp.dot(a, b, preferred_element_type=F32)


def dot_t(a, b):
    return lax.dot_general(a, b, (((1,), (1,)), ((), ())), preferred_element_type=F32)


def combos(dims):
    found = [0]
    for d in dims:
        found = [f ^ e for f in found for e in (0, d)]
    return found


def rows_of(chain):
    start = sum(ROWS[:chain])
    return slice(start, start + ROWS[chain])


def columns(target, size):
    return pl.ds(pl.multiple_of(target * size, size), size)


def load(pieces, target, sems, first):
    part = target.shape[0] // LOADS
    copies = []
    for i in range(LOADS):
        at = pl.ds(i * part, part)
        copies.append(pltpu.make_async_copy(pieces.at[at], target.at[at], sems.at[first + i]))
        copies[-1].start()
    return copies


def normalize(copies, x_ref, mod_ref, row, normed_ref):
    rows, width = x_ref.shape

    def step(i, carry):
        at = pl.ds(pl.multiple_of(i * CHUNK, CHUNK), CHUNK)
        x = x_ref[at, :].astype(F32)
        mean = jnp.mean(x, axis=-1, keepdims=True)
        centered = x - mean
        variance = jnp.mean(centered * centered, axis=-1, keepdims=True)
        scaled = centered * lax.rsqrt(variance + 1e-06)
        normed = scaled * (1.0 + mod_ref[row, width : 2 * width]) + mod_ref[row, :width]
        normed_ref[at, :] = normed.astype(BF16)
        return carry

    steps = rows // LOADS // CHUNK
    for i, copy in enumerate(copies):
        copy.wait()
        lax.fori_loop(i * steps, (i + 1) * steps, step, 0, unroll=steps)


def keys_kernel(level_ref, x_hbm, mod_hbm, w_hbm, kv_ref, table_ref, x_ref, normed_ref, mod_ref, w_ref, sems):
    level = level_ref[0]
    first = pl.multiple_of(level // 8 * 8, 8)
    copy_mod = pltpu.make_async_copy(mod_hbm.at[pl.ds(first, 8)], mod_ref, sems.at[0])
    copy_k = pltpu.make_async_copy(w_hbm.at[1], w_ref.at[0], sems.at[1])
    copy_v = pltpu.make_async_copy(w_hbm.at[2], w_ref.at[1], sems.at[2])
    copy_mod.start()
    copies = load(x_hbm, x_ref, sems, 3)
    copy_k.start()
    copy_v.start()
    copy_mod.wait()
    row = pl.ds(level % 8, 1)
    normalize(copies, x_ref, mod_ref, row, normed_ref)
    table_ref[...] = mod_ref[row, :]
    copy_k.wait()
    kv_ref[0] = dot(normed_ref[...], w_ref[0]).astype(BF16)
    copy_v.wait()
    kv_ref[1] = dot(normed_ref[...], w_ref[1]).astype(BF16)


def masked(scores, limit):
    spots = lax.broadcasted_iota(jnp.int32, scores.shape, 1)
    return jnp.where(spots < limit, scores * (1.0 / math.sqrt(HD)), -jnp.inf)


def limits(place, counts_ref, mask_ref):
    places = counts_ref.shape[0]
    before = jnp.where(place > 0, counts_ref[jnp.maximum(place - 1, 0)] * mask_ref[0, place], 0)
    after = jnp.where(
        place < places - 1, counts_ref[jnp.minimum(place + 1, places - 1)] * mask_ref[1, place], 0
    )
    odd = place % 2 == 1
    return jnp.where(odd, before, after), jnp.where(odd, after, before)


def near_kernel(
    meta_ref, counts_ref, mask_ref, x_hbm, table_ref, w_hbm, kv_ref, chip_ref, q_ref, o_ref, m_ref, l_ref, *scratch
):
    x_ref, normed_ref, w_ref, sems = scratch
    rows, size = q_ref.shape
    copies = load(x_hbm, x_ref, sems, 1)
    copy_q = pltpu.make_async_copy(w_hbm.at[0], w_ref, sems.at[0])
    copy_q.start()
    normalize(copies, x_ref, table_ref, slice(0, 1), normed_ref)
    copy_q.wait()
    q_ref[...] = dot(normed_ref[...], w_ref[...]).astype(BF16)
    place = meta_ref[0]
    own = counts_ref[place]
    chip = limits(place, counts_ref, mask_ref)[0]
    for head in range(size // HD):
        at = slice(head * HD, (head + 1) * HD)
        query = q_ref[:, at]
        left = masked(dot_t(query, kv_ref[0, :, at]), own)
        right = masked(dot_t(query, chip_ref[0, :, at]), chip)
        top = jnp.max(jnp.maximum(left, right), axis=-1, keepdims=True)
        left = jnp.exp(left - top)
        right = jnp.exp(right - top)
        m_ref[:, at] = jnp.broadcast_to(top, (rows, HD))
        l_ref[:, at] = jnp.broadcast_to(jnp.sum(left + right, axis=-1, keepdims=True), (rows, HD))
        o_ref[:, at] = dot(left.astype(BF16), kv_ref[1, :, at]) + dot(right.astype(BF16), chip_ref[1, :, at])


def join_kernel(meta_ref, counts_ref, mask_ref, q_ref, o_ref, m_ref, l_ref, far_ref, w_ref, *refs):
    outs, att_ref = refs[:-1], refs[-1]
    h = meta_ref[1]
    limit = limits(meta_ref[0], counts_ref, mask_ref)[1]
    rows, size = q_ref.shape
    for head in range(size // HD):
        at = slice(head * HD, (head + 1) * HD)
        scores = masked(dot_t(q_ref[:, at], far_ref[0, :, at]), limit)
        old = m_ref[:, at][:, :1]
        top = jnp.maximum(old, jnp.max(scores, axis=-1, keepdims=True))
        expo = jnp.exp(scores - top)
        keep = jnp.exp(old - top)
        total = l_ref[:, at][:, :1] * keep + jnp.sum(expo, axis=-1, keepdims=True)
        acc = o_ref[:, at] * keep + dot(expo.astype(BF16), far_ref[1, :, at])
        att_ref[:, at] = (acc / total).astype(BF16)
    for k in range(w_ref.shape[1] // size):
        result = dot(att_ref[...], w_ref[:, columns(h ^ k, size)]).astype(BF16)
        first = 0
        for c, dims in enumerate(ORDERS):
            spot = combos(dims).index(k)
            held = outs[first].shape[0]
            outs[first + spot // held][spot % held] = result[rows_of(c)]
            first += 8 // held


def add_kernel(starts, *refs):
    total = 0.0
    for start, ref in zip(starts, refs):
        total = total + ref[start : start + 2].astype(F32)
    refs[-1][...] = total.astype(BF16)


def update_kernel(chain, meta_ref, x_ref, table_ref, keep_ref, got_ref, out_ref):
    size = out_ref.shape[2]
    n_head = x_ref.shape[1] // size
    for j in range(2):
        target = meta_ref[1] ^ combos(ORDERS[chain])[j]
        at = columns(target, size)
        total = keep_ref[j].astype(F32) + got_ref[1 - j].astype(F32)
        x = x_ref[rows_of(chain), at].astype(F32)
        out_ref[j] = (x + table_ref[:, columns(2 * n_head + target, size)] * total).astype(BF16)


def concat_kernel(a_ref, b_ref, out_ref):
    half = a_ref.shape[0]
    out_ref[:half] = a_ref[...]
    out_ref[half:] = b_ref[...]


def place_kernel(meta_ref, *refs):
    pieces, out, sems = refs[:-2], refs[-2], refs[-1]
    size = pieces[0].shape[2]
    copies = []
    first = 0
    for c, part in enumerate(ROWS):
        held = pieces[first].shape[0]
        for spot in range(8):
            piece = pieces[first + spot // held].at[spot % held]
            target = meta_ref[1] ^ combos(ORDERS[c])[spot]
            to = out.at[pl.ds(rows_of(c).start, part), columns(target, size)]
            copies.append(pltpu.make_async_copy(piece, to, sems.at[len(copies)]))
            copies[-1].start()
        first += 8 // held
    for copy in copies:
        copy.wait()


def body(latents, levels, counts, window_mask, modulation, qkv_weight, out_weight):
    rows, width = latents.shape
    size = qkv_weight.shape[2]
    weight = jnp.transpose(qkv_weight, (1, 0, 2))
    n_head = lax.axis_size("head")
    n_queue = lax.axis_size("queue")
    meta = jnp.stack([lax.axis_index("queue"), lax.axis_index("head")]).astype(jnp.int32)
    shape = jax.ShapeDtypeStruct

    def swap(array, chain, level):
        step = ORDERS[chain][level]
        return lax.ppermute(array, "head", [(i, i ^ step) for i in range(n_head)])

    kv, table = pl.pallas_call(
        keys_kernel,
        out_shape=(shape((2, rows, size), BF16), shape((1, 3 * width), F32)),
        in_specs=smem() + hbm(3),
        out_specs=vmem(2),
        scratch_shapes=[
            pltpu.VMEM((rows, width), BF16),
            pltpu.VMEM((rows, width), BF16),
            pltpu.VMEM((8, 3 * width), F32),
            pltpu.VMEM((2, width, size), BF16),
            pltpu.SemaphoreType.DMA((3 + LOADS,)),
        ],
        compiler_params=params(53),
        cost_estimate=cost(4 * rows * width * size, 4 * width * size),
    )(levels, latents, modulation, weight)

    chip = lax.ppermute(kv, "queue", [(i, i ^ 1) for i in range(n_queue)])
    route = []
    for i in range(n_queue):
        j = i - 1 + i % 2 * 2
        for k in range(n_head):
            there = j * n_head + k if 0 <= j < n_queue else i * n_head + (k ^ 1)
            route.append((i * n_head + k, there))
    cross = lax.ppermute(kv, ("queue", "head"), route)

    query, *state = pl.pallas_call(
        near_kernel,
        out_shape=(shape((rows, size), BF16),) + (shape((rows, size), F32),) * 3,
        in_specs=smem(3) + hbm() + vmem() + hbm() + vmem(2),
        out_specs=vmem(4),
        scratch_shapes=[
            pltpu.VMEM((rows, width), BF16),
            pltpu.VMEM((rows, width), BF16),
            pltpu.VMEM((width, size), BF16),
            pltpu.SemaphoreType.DMA((1 + LOADS,)),
        ],
        compiler_params=params(NEAR),
        cost_estimate=cost(1, 1),
    )(meta, counts, window_mask.T, latents, table, weight, kv, chip)

    held = [2 if half else 4 for half in HALVES]
    parts = pl.pallas_call(
        join_kernel,
        out_shape=tuple(shape((n, part, size), BF16) for n, part in zip(held, ROWS) for _ in range(8 // n)),
        in_specs=smem(3) + vmem(6),
        out_specs=(vmem()[0],) * sum(8 // n for n in held),
        scratch_shapes=[pltpu.VMEM((rows, size), BF16)],
        compiler_params=params(32),
        cost_estimate=cost(4 * rows * width * size, 2 * width * size),
    )(meta, counts, window_mask.T, query, *state, cross, out_weight)

    small = dict(compiler_params=params(16), cost_estimate=cost(4 * 96 * size, 8 * 96 * size))

    def add(part, *terms):
        return pl.pallas_call(
            functools.partial(add_kernel, [start for start, _ in terms]),
            out_shape=shape((2, part, size), BF16),
            in_specs=vmem(len(terms)),
            out_specs=vmem()[0],
            **small,
        )(*[term for _, term in terms])

    chains = range(len(ROWS))
    keep, pass_on, got, got_on = {}, {}, {}, {}
    for c in chains:
        if HALVES[c]:
            keep[c], pass_on[c], give, give_on = parts[:4]
            parts = parts[4:]
            got_on[c] = swap(give_on, c, 0)
            got[c] = swap(give, c, 0)
        else:
            keep[c], give = parts[:2]
            parts = parts[2:]
            got[c] = swap(give, c, 0)
    relayed = {}
    for c, part in enumerate(ROWS):
        if HALVES[c]:
            term = add(part, (0, pass_on[c]), (0, got_on[c]))
        else:
            term = add(part, (2, keep[c]), (2, got[c]))
        relayed[c] = swap(term, c, 1)
    mine, other = {}, {}
    for c, part in enumerate(ROWS):
        mine[c] = add(part, (0, keep[c]), (0, got[c]), (0, relayed[c]))
        other[c] = swap(mine[c], c, 2)
    moved = {}
    for c, part in enumerate(ROWS):
        fresh = pl.pallas_call(
            functools.partial(update_kernel, c),
            out_shape=shape((2, part, size), BF16),
            in_specs=smem() + vmem(4),
            out_specs=vmem()[0],
            **small,
        )(meta, latents, table, mine[c], other[c])
        moved[c] = lax.ppermute(fresh, "queue", [(i, (i - 1) % n_queue) for i in range(n_queue)])
    ready = []
    for c, part in enumerate(ROWS):
        near = swap(moved[c], c, 1)
        if GATHER[c]:
            ready += [moved[c], near, swap(moved[c], c, 0), swap(near, c, 0)]
        else:
            four = pl.pallas_call(
                concat_kernel,
                out_shape=shape((4, part, size), BF16),
                in_specs=vmem(2),
                out_specs=vmem()[0],
                **small,
            )(moved[c], near)
            ready += [four, swap(four, c, 0)]

    return pl.pallas_call(
        place_kernel,
        out_shape=shape((rows, width), BF16),
        in_specs=smem() + vmem(len(ready)),
        out_specs=hbm()[0],
        scratch_shapes=[pltpu.SemaphoreType.DMA((8 * len(ROWS),))],
        **small,
    )(meta, *ready)


def solution(mesh):
    in_specs = (P("queue", None), P("queue"), P(), P(), P(), P(None, None, "head"), P("head", None))
    out_specs = P("queue", None)
    return jax.shard_map(body, mesh=mesh, in_specs=in_specs, out_specs=out_specs, check_vma=False)
```

time: 77.8 us -> 73.5 us (0.945)
  waiting for transfers between devices: 34.6 us -> 30.4 us
  Pallas kernels: 15.8 us -> 17.5 us
  starting transfers between devices: 26.2 us -> 24.5 us
    ppermute x1, waiting for transfers between devices: 11.3 us -> 7.62 us  [body(): cross = lax.ppermute(kv, ('queue', 'head'), route)]
    pallas_call x11, Pallas kernels: 7.85 us -> 10.6 us  [the longest x1 5.14 us: body(): pl.pallas_call(near_kernel, out_shape=(shape((rows, size), BF16),) + (sha...]
    ppermute x15 -> x18, starting transfers between devices: 21.3 us -> 19.6 us  [swap(): return lax.ppermute(array, 'head', [(i, i ^ step) for i in range(n_head)])]
    ppermute x3, waiting for transfers between devices: 10.8 us -> 9.48 us  [body(): lax.ppermute(fresh, 'queue', [(i, (i - 1) % n_queue) for i in range(n_que...]
    pallas_call x1, Pallas kernels: 5.91 us -> 4.81 us  [body(): pl.pallas_call(keys_kernel, out_shape=(shape((2, rows, size), BF16), shap...]
    ppermute x15 -> x18, waiting for transfers between devices: 12.5 us -> 13.3 us  [swap(): return lax.ppermute(array, 'head', [(i, i ^ step) for i in range(n_head)])]
  transfers between devices with their start and end apart: 20 -> 23, of which waited for: 13 -> 14; matrix products, arithmetic and copies ran while one was open for 0% -> 0% of each run, Pallas kernels for 5% -> 10%
where the time goes in v3:
time: 73.5 us; the launch traced here: 73.4 us
  waiting for transfers between devices  30.4 us (41%)
  starting transfers between devices  24.5 us (33%)
  Pallas kernels  17.5 us (24%)
  between operations  1 us (1%)
    ppermute x18, starting transfers between devices, swap(): return lax.ppermute(array, 'head', [(i, i ^ step) for i in range(n_head)])  19.6 us
    ppermute x18, waiting for transfers between devices, swap(): return lax.ppermute(array, 'head', [(i, i ^ step) for i in range(n_head)])  13.3 us
    ppermute x3, waiting for transfers between devices, body(): lax.ppermute(fresh, 'queue', [(i, (i - 1) % n_queue) for i in range(n_que...  9.48 us
    ppermute x1, waiting for transfers between devices, body(): cross = lax.ppermute(kv, ('queue', 'head'), route)  7.62 us
    pallas_call x1, Pallas kernels, body(): pl.pallas_call(near_kernel, out_shape=(shape((rows, size), BF16),) + (sha...  5.14 us
    pallas_call x1, Pallas kernels, body(): pl.pallas_call(keys_kernel, out_shape=(shape((2, rows, size), BF16), shap...  4.81 us
    ppermute x1, starting transfers between devices, body(): cross = lax.ppermute(kv, ('queue', 'head'), route)  3.85 us
    pallas_call x1, Pallas kernels, body(): pl.pallas_call(join_kernel, out_shape=tuple((shape((n, part, size), BF16)...  3.36 us
  transfers between devices with their start and end apart: 23, of which 14 were waited for; matrix products, arithmetic and copies ran while one was open for 0% of the time, Pallas kernels for 10%

profile of v3, /device:TPU:89, one launch (start us, length us, event | category | flops | bytes accessed | tf_op | source)
XLA Modules:
  0.0 73.4 jit_solution(8173324129126226497)
XLA Ops:
  0.7 4.8 %shard_map.73 = (bf16[2,288,384]{2,1,0:T(8,128)(2,1)S(1)}, f32[1,9216]{1,0:T(1,128)S(1)}) custom-call(s32[1]{0:T(128)S(6)} %copy.8.level_ref, bf16[288,3072]{1,0:T(8,128)(2,1)} %x_ref.5, f32[16,9216]{1,0:T(8,128)} %mod_hbm.1, bf16[3,3072,384]{2,1,0:T(8,128)(2,1)} %bitcast.6), custom_call_target="tpu_custom_call" | custom-call | flops 1358954496 | bytes 4718592 | tf_op jit(solution)/shard_map/pallas_call | solution.py:238
  5.5 0.8 %collective-permute-start = (bf16[2,288,384]{2,1,0:T(8,128)(2,1)S(1)}, bf16[2,288,384]{2,1,0:T(8,128)(2,1)S(1)}, u32[]{:S(2)}, u32[]{:S(2)}) collective-permute-start(bf16[2,288,384]{2,1,0:T(8,128)(2,1)S(1)} %get-tuple-element.24.kv_ref), channel_id=1, source_target_pairs={{0,8},{8,0},{16,24},{24,16},{32,40},{40,32},{48,56},{56,48},{64,72... | collective-permute-start | bytes 1327112 | tf_op jit(solution)/shard_map/ppermute | solution.py:254
  6.3 3.9 %collective-permute-start.1 = (bf16[2,288,384]{2,1,0:T(8,128)(2,1)S(1)}, bf16[2,288,384]{2,1,0:T(8,128)(2,1)S(1)}, u32[]{:S(2)}, u32[]{:S(2)}) collective-permute-start(bf16[2,288,384]{2,1,0:T(8,128)(2,1)S(1)} %get-tuple-element.24.kv_ref), channel_id=1, source_target_pairs={{0,1},{1,0},{2,3},{3,2},{4,5},{5,4},{6,7},{7,6},{8,16},{9,17},{10,... | collective-permute-start | bytes 1327112 | tf_op jit(solution)/shard_map/ppermute | solution.py:261
  10.1 0.1 pad_add_fusion.meta_ref
  10.2 0.0 copy-start.3
  10.2 5.1 %shard_map.74 = (bf16[288,384]{1,0:T(8,128)(2,1)S(1)}, f32[288,384]{1,0:T(8,128)S(1)}, f32[288,384]{1,0:T(8,128)S(1)}, f32[288,384]{1,0:T(8,128)S(1)}) custom-call(s32[2]{0:T(128)S(1)} %pad_add_fusion.meta_ref, s32[32]{0:T(128)S(1)} %copy-done.2, s32[2,32]{1,0:T(2,128)S(1)} %bitcast.4, bf16[288,3072]{1,0:T(8,128)(2,1)S(1)} %copy-done, ...), custom_call_target="tpu_custom_call" | custom-call | flops 1 | bytes 1 | tf_op jit(solution)/shard_map/pallas_call | solution.py:263
  15.4 7.6 %collective-permute-done.1.far_ref = bf16[2,288,384]{2,1,0:T(8,128)(2,1)S(1)} collective-permute-done((bf16[2,288,384]{2,1,0:T(8,128)(2,1)S(1)}, bf16[2,288,384]{2,1,0:T(8,128)(2,1)S(1)}, u32[]{:S(2)}, u32[]{:S(2)}) %collective-permute-start.1) | collective-permute-done | bytes 442400 | tf_op jit(solution)/shard_map/ppermute | solution.py:261
  23.0 3.4 %shard_map.75 = (bf16[2,96,384]{2,1,0:T(8,128)(2,1)S(1)}, bf16[2,96,384]{2,1,0:T(8,128)(2,1)S(1)}, bf16[2,96,384]{2,1,0:T(8,128)(2,1)S(1)}, bf16[2,96,384]{2,1,0...) custom-call(s32[2]{0:T(128)S(1)} %pad_add_fusion.meta_ref, ...), custom_call_target="tpu_custom_call" | custom-call | flops 1358954496 | bytes 2359296 | tf_op jit(solution)/shard_map/pallas_call | solution.py:279
  26.3 2.6 %collective-permute-start.17 = (bf16[2,96,384]{2,1,0:T(8,128)(2,1)S(1)}, bf16[2,96,384]{2,1,0:T(8,128)(2,1)S(1)}, u32[]{:S(2)}, u32[]{:S(2)}) collective-permute-start(bf16[2,96,384]{2,1,0:T(8,128)(2,1)S(1)} %get-tuple-element.40), channel_id=1, source_target_pairs={{0,3},{1,2},{2,1},{3,0},{4,7},{5,6},{6,5},{7,4},{8,11},{9,10},{10,... | collective-permute-start | bytes 442376 | tf_op jit(solution)/shard_map/ppermute | solution.py:236
  29.0 0.0 collective-permute-start.3
  29.0 0.7 collective-permute-start.16
  29.7 0.8 %collective-permute-start.9 = (bf16[2,96,384]{2,1,0:T(8,128)(2,1)S(1)}, bf16[2,96,384]{2,1,0:T(8,128)(2,1)S(1)}, u32[]{:S(2)}, u32[]{:S(2)}) collective-permute-start(bf16[2,96,384]{2,1,0:T(8,128)(2,1)S(1)} %get-tuple-element.34), channel_id=1, source_target_pairs={{0,1},{1,0},{2,3},{3,2},{4,5},{5,4},{6,7},{7,6},{8,9},{9,8},{10,11... | collective-permute-start | bytes 442376 | tf_op jit(solution)/shard_map/ppermute | solution.py:236
  30.5 3.0 %collective-permute-done.17.refs_1_ = bf16[2,96,384]{2,1,0:T(8,128)(2,1)S(1)} collective-permute-done((bf16[2,96,384]{2,1,0:T(8,128)(2,1)S(1)}, bf16[2,96,384]{2,1,0:T(8,128)(2,1)S(1)}, u32[]{:S(2)}, u32[]{:S(2)}) %collective-permute-start.17) | collective-permute-done | bytes 147488 | tf_op jit(solution)/shard_map/ppermute | solution.py:236
  33.5 0.1 collective-permute-start.18
  33.6 0.5 collective-permute-done.10.refs_1_
  34.1 2.2 %collective-permute-start.11 = (bf16[2,96,384]{2,1,0:T(8,128)(2,1)S(1)}, bf16[2,96,384]{2,1,0:T(8,128)(2,1)S(1)}, u32[]{:S(2)}, u32[]{:S(2)}) collective-permute-start(bf16[2,96,384]{2,1,0:T(8,128)(2,1)S(1)} %shard_map.80), channel_id=1, source_target_pairs={{0,3},{1,2},{2,1},{3,0},{4,7},{5,6},{6,5},{7,4},{8,11},{9,10},{10,... | collective-permute-start | bytes 442376 | tf_op jit(solution)/shard_map/ppermute | solution.py:236
  36.3 1.4 %collective-permute-start.2 = (bf16[2,96,384]{2,1,0:T(8,128)(2,1)S(1)}, bf16[2,96,384]{2,1,0:T(8,128)(2,1)S(1)}, u32[]{:S(2)}, u32[]{:S(2)}) collective-permute-start(bf16[2,96,384]{2,1,0:T(8,128)(2,1)S(1)} %get-tuple-element.30), channel_id=1, source_target_pairs={{0,4},{1,5},{2,6},{3,7},{4,0},{5,1},{6,2},{7,3},{8,12},{9,13},{10,... | collective-permute-start | bytes 442376 | tf_op jit(solution)/shard_map/ppermute | solution.py:236
  37.8 0.0 collective-permute-done.16.refs_1_
  37.8 0.1 collective-permute-start.4
  37.9 0.4 collective-permute-done.18.refs_2_
  38.3 0.1 shard_map.85.keep_ref
  38.4 1.1 %collective-permute-start.19 = (bf16[2,96,384]{2,1,0:T(8,128)(2,1)S(1)}, bf16[2,96,384]{2,1,0:T(8,128)(2,1)S(1)}, u32[]{:S(2)}, u32[]{:S(2)}) collective-permute-start(bf16[2,96,384]{2,1,0:T(8,128)(2,1)S(1)} %shard_map.85.keep_ref), channel_id=1, source_target_pairs={{0,1},{1,0},{2,3},{3,2},{4,5},{5,4},{6,7},{7,6},{8,9},{9,8},{10,11... | collective-permute-start | bytes 442376 | tf_op jit(solution)/shard_map/ppermute | solution.py:236
  39.5 0.1 shard_map.81.keep_ref
  39.6 0.9 %collective-permute-start.12 = (bf16[2,96,384]{2,1,0:T(8,128)(2,1)S(1)}, bf16[2,96,384]{2,1,0:T(8,128)(2,1)S(1)}, u32[]{:S(2)}, u32[]{:S(2)}) collective-permute-start(bf16[2,96,384]{2,1,0:T(8,128)(2,1)S(1)} %shard_map.81.keep_ref), channel_id=1, source_target_pairs={{0,4},{1,5},{2,6},{3,7},{4,0},{5,1},{6,2},{7,3},{8,12},{9,13},{10,... | collective-permute-start | bytes 442376 | tf_op jit(solution)/shard_map/ppermute | solution.py:236
  40.5 0.5 collective-permute-done.2.refs_1_
  41.0 1.1 %collective-permute-done.4.refs_2_ = bf16[2,96,384]{2,1,0:T(8,128)(2,1)S(1)} collective-permute-done((bf16[2,96,384]{2,1,0:T(8,128)(2,1)S(1)}, bf16[2,96,384]{2,1,0:T(8,128)(2,1)S(1)}, u32[]{:S(2)}, u32[]{:S(2)}) %collective-permute-start.4) | collective-permute-done | bytes 147488 | tf_op jit(solution)/shard_map/ppermute | solution.py:236
  42.1 0.1 shard_map.77.keep_ref
  42.2 1.7 %collective-permute-start.5 = (bf16[2,96,384]{2,1,0:T(8,128)(2,1)S(1)}, bf16[2,96,384]{2,1,0:T(8,128)(2,1)S(1)}, u32[]{:S(2)}, u32[]{:S(2)}) collective-permute-start(bf16[2,96,384]{2,1,0:T(8,128)(2,1)S(1)} %shard_map.77.keep_ref), channel_id=1, source_target_pairs={{0,3},{1,2},{2,1},{3,0},{4,7},{5,6},{6,5},{7,4},{8,11},{9,10},{10,... | collective-permute-start | bytes 442376 | tf_op jit(solution)/shard_map/ppermute | solution.py:236
  43.9 0.6 shard_map.86
  44.5 0.1 collective-permute-start.20
  44.6 0.6 shard_map.82
  45.2 0.1 collective-permute-start.13
  45.3 2.1 %collective-permute-done.5.got_ref = bf16[2,96,384]{2,1,0:T(8,128)(2,1)S(1)} collective-permute-done((bf16[2,96,384]{2,1,0:T(8,128)(2,1)S(1)}, bf16[2,96,384]{2,1,0:T(8,128)(2,1)S(1)}, u32[]{:S(2)}, u32[]{:S(2)}) %collective-permute-start.5) | collective-permute-done | bytes 147488 | tf_op jit(solution)/shard_map/ppermute | solution.py:236
  47.5 0.6 shard_map.78
  48.1 0.1 collective-permute-start.6
  48.2 6.6 %collective-permute-done.20.a_ref = bf16[2,96,384]{2,1,0:T(8,128)(2,1)S(1)} collective-permute-done((bf16[2,96,384]{2,1,0:T(8,128)(2,1)S(1)}, bf16[2,96,384]{2,1,0:T(8,128)(2,1)S(1)}, u32[]{:S(2)}, u32[]{:S(2)}) %collective-permute-start.20) | collective-permute-done | bytes 147488 | tf_op jit(solution)/shard_map/ppermute | solution.py:332
  54.8 0.5 collective-permute-start.21
  55.3 2.0 %collective-permute-done.13.a_ref = bf16[2,96,384]{2,1,0:T(8,128)(2,1)S(1)} collective-permute-done((bf16[2,96,384]{2,1,0:T(8,128)(2,1)S(1)}, bf16[2,96,384]{2,1,0:T(8,128)(2,1)S(1)}, u32[]{:S(2)}, u32[]{:S(2)}) %collective-permute-start.13) | collective-permute-done | bytes 147488 | tf_op jit(solution)/shard_map/ppermute | solution.py:332
  57.3 1.3 %collective-permute-start.14 = (bf16[2,96,384]{2,1,0:T(8,128)(2,1)S(1)}, bf16[2,96,384]{2,1,0:T(8,128)(2,1)S(1)}, u32[]{:S(2)}, u32[]{:S(2)}) collective-permute-start(bf16[2,96,384]{2,1,0:T(8,128)(2,1)S(1)} %collective-permute-done.13.a_ref), channel_id=1, source_target_pairs={{0,3},{1,2},{2,1},{3,0},{4,7},{5,6},{6,5},{7,4},{8,11},{9,10},{10,... | collective-permute-start | bytes 442376 | tf_op jit(solution)/shard_map/ppermute | solution.py:236
  58.6 0.8 %collective-permute-done.6.a_ref = bf16[2,96,384]{2,1,0:T(8,128)(2,1)S(1)} collective-permute-done((bf16[2,96,384]{2,1,0:T(8,128)(2,1)S(1)}, bf16[2,96,384]{2,1,0:T(8,128)(2,1)S(1)}, u32[]{:S(2)}, u32[]{:S(2)}) %collective-permute-start.6) | collective-permute-done | bytes 147488 | tf_op jit(solution)/shard_map/ppermute | solution.py:332
  59.4 0.9 %collective-permute-done.21.b_ref = bf16[2,96,384]{2,1,0:T(8,128)(2,1)S(1)} collective-permute-done((bf16[2,96,384]{2,1,0:T(8,128)(2,1)S(1)}, bf16[2,96,384]{2,1,0:T(8,128)(2,1)S(1)}, u32[]{:S(2)}, u32[]{:S(2)}) %collective-permute-start.21) | collective-permute-done | bytes 147488 | tf_op jit(solution)/shard_map/ppermute | solution.py:236
  60.3 2.3 %collective-permute-start.22 = (bf16[4,96,384]{2,1,0:T(8,128)(2,1)S(1)}, bf16[4,96,384]{2,1,0:T(8,128)(2,1)S(1)}, u32[]{:S(2)}, u32[]{:S(2)}) collective-permute-start(bf16[4,96,384]{2,1,0:T(8,128)(2,1)S(1)} %shard_map.87.refs_4_), channel_id=1, source_target_pairs={{0,3},{1,2},{2,1},{3,0},{4,7},{5,6},{6,5},{7,4},{8,11},{9,10},{10,... | collective-permute-start | bytes 884744 | tf_op jit(solution)/shard_map/ppermute | solution.py:236
  62.7 0.1 collective-permute-start.15
  62.8 0.6 collective-permute-done.7.b_ref
  63.5 3.8 %collective-permute-start.8 = (bf16[4,96,384]{2,1,0:T(8,128)(2,1)S(1)}, bf16[4,96,384]{2,1,0:T(8,128)(2,1)S(1)}, u32[]{:S(2)}, u32[]{:S(2)}) collective-permute-start(bf16[4,96,384]{2,1,0:T(8,128)(2,1)S(1)} %shard_map.79.refs_0_), channel_id=1, source_target_pairs={{0,4},{1,5},{2,6},{3,7},{4,0},{5,1},{6,2},{7,3},{8,12},{9,13},{10,... | collective-permute-start | bytes 884744 | tf_op jit(solution)/shard_map/ppermute | solution.py:236
  67.2 1.1 %collective-permute-done.15.refs_3_ = bf16[4,96,384]{2,1,0:T(8,128)(2,1)S(1)} collective-permute-done((bf16[4,96,384]{2,1,0:T(8,128)(2,1)S(1)}, bf16[4,96,384]{2,1,0:T(8,128)(2,1)S(1)}, u32[]{:S(2)}, u32[]{:S(2)}) %collective-permute-start.15) | collective-permute-done | bytes 294944 | tf_op jit(solution)/shard_map/ppermute | solution.py:236
  68.3 3.0 %collective-permute-done.8.refs_1_ = bf16[4,96,384]{2,1,0:T(8,128)(2,1)S(1)} collective-permute-done((bf16[4,96,384]{2,1,0:T(8,128)(2,1)S(1)}, bf16[4,96,384]{2,1,0:T(8,128)(2,1)S(1)}, u32[]{:S(2)}, u32[]{:S(2)}) %collective-permute-start.8) | collective-permute-done | bytes 294944 | tf_op jit(solution)/shard_map/ppermute | solution.py:236
  71.3 1.9 %shard_map.88 = bf16[288,3072]{1,0:T(8,128)(2,1)} custom-call(s32[2]{0:T(128)S(1)} %pad_add_fusion.meta_ref, bf16[4,96,384]{2,1,0:T(8,128)(2,1)S(1)} %shard_map.79.refs_0_, bf16[4,96,384]{2,1,0:T(8,128)(2,1)S(1)} %collective-permute-done.8.refs_1_, bf16[4,96,384]{2,1,0:T(8,128)(2,1)S(1)} %shard_map.83.refs_2_, ...), custom_call_target="tpu_custom_call" | custom-call | flops 147456 | bytes 294912 | tf_op jit(solution)/shard_map/pallas_call | solution.py:348
  (23 shorter events, 0.2 us)
Async XLA Ops:
  0.7 9.5 %copy-start = (bf16[288,3072]{1,0:T(8,128)(2,1)S(1)}, bf16[288,3072]{1,0:T(8,128)(2,1)}, u32[]{:S(2)}) copy-start(bf16[288,3072]{1,0:T(8,128)(2,1)} %x_ref.5) | copy-start | bytes 5308420
  0.7 9.5 %copy-start.1 = (s32[32,2]{0,1:T(2,128)S(1)}, s32[32,2]{0,1:T(2,128)}, u32[]{:S(2)}) copy-start(s32[32,2]{0,1:T(2,128)} %param.10) | copy-start | bytes 772
  0.7 9.5 %copy-start.2 = (s32[32]{0:T(128)S(1)}, s32[32]{0:T(128)}, u32[]{:S(2)}) copy-start(s32[32]{0:T(128)} %counts_ref.3) | copy-start | bytes 388
  5.5 4.7 %collective-permute-start = (bf16[2,288,384]{2,1,0:T(8,128)(2,1)S(1)}, bf16[2,288,384]{2,1,0:T(8,128)(2,1)S(1)}, u32[]{:S(2)}, u32[]{:S(2)}) collective-permute-start(bf16[2,288,384]{2,1,0:T(8,128)(2,1)S(1)} %get-tuple-element.24.kv_ref), channel_id=1, source_target_pairs={{0,8},{8,0},{16,24},{24,16},{32,40},{40,32},{48,56},{56,48},{64,72... | collective-permute-start | bytes 1327112 | tf_op jit(solution)/shard_map/ppermute | solution.py:254
  6.3 16.7 %collective-permute-start.1 = (bf16[2,288,384]{2,1,0:T(8,128)(2,1)S(1)}, bf16[2,288,384]{2,1,0:T(8,128)(2,1)S(1)}, u32[]{:S(2)}, u32[]{:S(2)}) collective-permute-start(bf16[2,288,384]{2,1,0:T(8,128)(2,1)S(1)} %get-tuple-element.24.kv_ref), channel_id=1, source_target_pairs={{0,1},{1,0},{2,3},{3,2},{4,5},{5,4},{6,7},{7,6},{8,16},{9,17},{10,... | collective-permute-start | bytes 1327112 | tf_op jit(solution)/shard_map/ppermute | solution.py:261
  10.2 12.8 %copy-start.3 = (bf16[384,3072]{1,0:T(8,128)(2,1)S(1)}, bf16[384,3072]{1,0:T(8,128)(2,1)}, u32[]{:S(2)}) copy-start(bf16[384,3072]{1,0:T(8,128)(2,1)} %w_ref.1) | copy-start | bytes 7077892
  26.3 7.1 %collective-permute-start.17 = (bf16[2,96,384]{2,1,0:T(8,128)(2,1)S(1)}, bf16[2,96,384]{2,1,0:T(8,128)(2,1)S(1)}, u32[]{:S(2)}, u32[]{:S(2)}) collective-permute-start(bf16[2,96,384]{2,1,0:T(8,128)(2,1)S(1)} %get-tuple-element.40), channel_id=1, source_target_pairs={{0,3},{1,2},{2,1},{3,0},{4,7},{5,6},{6,5},{7,4},{8,11},{9,10},{10,... | collective-permute-start | bytes 442376 | tf_op jit(solution)/shard_map/ppermute | solution.py:236
  29.0 5.1 %collective-permute-start.10 = (bf16[2,96,384]{2,1,0:T(8,128)(2,1)S(1)}, bf16[2,96,384]{2,1,0:T(8,128)(2,1)S(1)}, u32[]{:S(2)}, u32[]{:S(2)}) collective-permute-start(bf16[2,96,384]{2,1,0:T(8,128)(2,1)S(1)} %get-tuple-element.36), channel_id=1, source_target_pairs={{0,1},{1,0},{2,3},{3,2},{4,5},{5,4},{6,7},{7,6},{8,9},{9,8},{10,11... | collective-permute-start | bytes 442376 | tf_op jit(solution)/shard_map/ppermute | solution.py:236
  29.0 7.3 %collective-permute-start.3 = (bf16[2,96,384]{2,1,0:T(8,128)(2,1)S(1)}, bf16[2,96,384]{2,1,0:T(8,128)(2,1)S(1)}, u32[]{:S(2)}, u32[]{:S(2)}) collective-permute-start(bf16[2,96,384]{2,1,0:T(8,128)(2,1)S(1)} %get-tuple-element.32), channel_id=1, source_target_pairs={{0,4},{1,5},{2,6},{3,7},{4,0},{5,1},{6,2},{7,3},{8,12},{9,13},{10,... | collective-permute-start | bytes 442376 | tf_op jit(solution)/shard_map/ppermute | solution.py:236
  29.0 8.8 %collective-permute-start.16 = (bf16[2,96,384]{2,1,0:T(8,128)(2,1)S(1)}, bf16[2,96,384]{2,1,0:T(8,128)(2,1)S(1)}, u32[]{:S(2)}, u32[]{:S(2)}) collective-permute-start(bf16[2,96,384]{2,1,0:T(8,128)(2,1)S(1)} %get-tuple-element.38), channel_id=1, source_target_pairs={{0,3},{1,2},{2,1},{3,0},{4,7},{5,6},{6,5},{7,4},{8,11},{9,10},{10,... | collective-permute-start | bytes 442376 | tf_op jit(solution)/shard_map/ppermute | solution.py:236
  29.7 9.8 %collective-permute-start.9 = (bf16[2,96,384]{2,1,0:T(8,128)(2,1)S(1)}, bf16[2,96,384]{2,1,0:T(8,128)(2,1)S(1)}, u32[]{:S(2)}, u32[]{:S(2)}) collective-permute-start(bf16[2,96,384]{2,1,0:T(8,128)(2,1)S(1)} %get-tuple-element.34), channel_id=1, source_target_pairs={{0,1},{1,0},{2,3},{3,2},{4,5},{5,4},{6,7},{7,6},{8,9},{9,8},{10,11... | collective-permute-start | bytes 442376 | tf_op jit(solution)/shard_map/ppermute | solution.py:236
  33.5 4.9 %collective-permute-start.18 = (bf16[2,96,384]{2,1,0:T(8,128)(2,1)S(1)}, bf16[2,96,384]{2,1,0:T(8,128)(2,1)S(1)}, u32[]{:S(2)}, u32[]{:S(2)}) collective-permute-start(bf16[2,96,384]{2,1,0:T(8,128)(2,1)S(1)} %shard_map.84), channel_id=1, source_target_pairs={{0,4},{1,5},{2,6},{3,7},{4,0},{5,1},{6,2},{7,3},{8,12},{9,13},{10,... | collective-permute-start | bytes 442376 | tf_op jit(solution)/shard_map/ppermute | solution.py:236
  34.1 5.4 %collective-permute-start.11 = (bf16[2,96,384]{2,1,0:T(8,128)(2,1)S(1)}, bf16[2,96,384]{2,1,0:T(8,128)(2,1)S(1)}, u32[]{:S(2)}, u32[]{:S(2)}) collective-permute-start(bf16[2,96,384]{2,1,0:T(8,128)(2,1)S(1)} %shard_map.80), channel_id=1, source_target_pairs={{0,3},{1,2},{2,1},{3,0},{4,7},{5,6},{6,5},{7,4},{8,11},{9,10},{10,... | collective-permute-start | bytes 442376 | tf_op jit(solution)/shard_map/ppermute | solution.py:236
  36.3 4.7 %collective-permute-start.2 = (bf16[2,96,384]{2,1,0:T(8,128)(2,1)S(1)}, bf16[2,96,384]{2,1,0:T(8,128)(2,1)S(1)}, u32[]{:S(2)}, u32[]{:S(2)}) collective-permute-start(bf16[2,96,384]{2,1,0:T(8,128)(2,1)S(1)} %get-tuple-element.30), channel_id=1, source_target_pairs={{0,4},{1,5},{2,6},{3,7},{4,0},{5,1},{6,2},{7,3},{8,12},{9,13},{10,... | collective-permute-start | bytes 442376 | tf_op jit(solution)/shard_map/ppermute | solution.py:236
  37.8 4.3 %collective-permute-start.4 = (bf16[2,96,384]{2,1,0:T(8,128)(2,1)S(1)}, bf16[2,96,384]{2,1,0:T(8,128)(2,1)S(1)}, u32[]{:S(2)}, u32[]{:S(2)}) collective-permute-start(bf16[2,96,384]{2,1,0:T(8,128)(2,1)S(1)} %shard_map.76), channel_id=1, source_target_pairs={{0,1},{1,0},{2,3},{3,2},{4,5},{5,4},{6,7},{7,6},{8,9},{9,8},{10,11... | collective-permute-start | bytes 442376 | tf_op jit(solution)/shard_map/ppermute | solution.py:236
  38.4 5.5 %collective-permute-start.19 = (bf16[2,96,384]{2,1,0:T(8,128)(2,1)S(1)}, bf16[2,96,384]{2,1,0:T(8,128)(2,1)S(1)}, u32[]{:S(2)}, u32[]{:S(2)}) collective-permute-start(bf16[2,96,384]{2,1,0:T(8,128)(2,1)S(1)} %shard_map.85.keep_ref), channel_id=1, source_target_pairs={{0,1},{1,0},{2,3},{3,2},{4,5},{5,4},{6,7},{7,6},{8,9},{9,8},{10,11... | collective-permute-start | bytes 442376 | tf_op jit(solution)/shard_map/ppermute | solution.py:236
  39.6 5.0 %collective-permute-start.12 = (bf16[2,96,384]{2,1,0:T(8,128)(2,1)S(1)}, bf16[2,96,384]{2,1,0:T(8,128)(2,1)S(1)}, u32[]{:S(2)}, u32[]{:S(2)}) collective-permute-start(bf16[2,96,384]{2,1,0:T(8,128)(2,1)S(1)} %shard_map.81.keep_ref), channel_id=1, source_target_pairs={{0,4},{1,5},{2,6},{3,7},{4,0},{5,1},{6,2},{7,3},{8,12},{9,13},{10,... | collective-permute-start | bytes 442376 | tf_op jit(solution)/shard_map/ppermute | solution.py:236
  42.2 5.3 %collective-permute-start.5 = (bf16[2,96,384]{2,1,0:T(8,128)(2,1)S(1)}, bf16[2,96,384]{2,1,0:T(8,128)(2,1)S(1)}, u32[]{:S(2)}, u32[]{:S(2)}) collective-permute-start(bf16[2,96,384]{2,1,0:T(8,128)(2,1)S(1)} %shard_map.77.keep_ref), channel_id=1, source_target_pairs={{0,3},{1,2},{2,1},{3,0},{4,7},{5,6},{6,5},{7,4},{8,11},{9,10},{10,... | collective-permute-start | bytes 442376 | tf_op jit(solution)/shard_map/ppermute | solution.py:236
  44.5 10.3 %collective-permute-start.20 = (bf16[2,96,384]{2,1,0:T(8,128)(2,1)S(1)}, bf16[2,96,384]{2,1,0:T(8,128)(2,1)S(1)}, u32[]{:S(2)}, u32[]{:S(2)}) collective-permute-start(bf16[2,96,384]{2,1,0:T(8,128)(2,1)S(1)} %shard_map.86), channel_id=1, source_target_pairs={{0,248},{8,0},{16,8},{24,16},{32,24},{40,32},{48,40},{56,48},{64,5... | collective-permute-start | bytes 442376 | tf_op jit(solution)/shard_map/ppermute | solution.py:332
  45.2 12.1 %collective-permute-start.13 = (bf16[2,96,384]{2,1,0:T(8,128)(2,1)S(1)}, bf16[2,96,384]{2,1,0:T(8,128)(2,1)S(1)}, u32[]{:S(2)}, u32[]{:S(2)}) collective-permute-start(bf16[2,96,384]{2,1,0:T(8,128)(2,1)S(1)} %shard_map.82), channel_id=1, source_target_pairs={{0,248},{8,0},{16,8},{24,16},{32,24},{40,32},{48,40},{56,48},{64,5... | collective-permute-start | bytes 442376 | tf_op jit(solution)/shard_map/ppermute | solution.py:332
  48.1 11.3 %collective-permute-start.6 = (bf16[2,96,384]{2,1,0:T(8,128)(2,1)S(1)}, bf16[2,96,384]{2,1,0:T(8,128)(2,1)S(1)}, u32[]{:S(2)}, u32[]{:S(2)}) collective-permute-start(bf16[2,96,384]{2,1,0:T(8,128)(2,1)S(1)} %shard_map.78), channel_id=1, source_target_pairs={{0,248},{8,0},{16,8},{24,16},{32,24},{40,32},{48,40},{56,48},{64,5... | collective-permute-start | bytes 442376 | tf_op jit(solution)/shard_map/ppermute | solution.py:332
  54.8 5.5 %collective-permute-start.21 = (bf16[2,96,384]{2,1,0:T(8,128)(2,1)S(1)}, bf16[2,96,384]{2,1,0:T(8,128)(2,1)S(1)}, u32[]{:S(2)}, u32[]{:S(2)}) collective-permute-start(bf16[2,96,384]{2,1,0:T(8,128)(2,1)S(1)} %collective-permute-done.20.a_ref), channel_id=1, source_target_pairs={{0,4},{1,5},{2,6},{3,7},{4,0},{5,1},{6,2},{7,3},{8,12},{9,13},{10,... | collective-permute-start | bytes 442376 | tf_op jit(solution)/shard_map/ppermute | solution.py:236
  57.3 5.3 %collective-permute-start.14 = (bf16[2,96,384]{2,1,0:T(8,128)(2,1)S(1)}, bf16[2,96,384]{2,1,0:T(8,128)(2,1)S(1)}, u32[]{:S(2)}, u32[]{:S(2)}) collective-permute-start(bf16[2,96,384]{2,1,0:T(8,128)(2,1)S(1)} %collective-permute-done.13.a_ref), channel_id=1, source_target_pairs={{0,3},{1,2},{2,1},{3,0},{4,7},{5,6},{6,5},{7,4},{8,11},{9,10},{10,... | collective-permute-start | bytes 442376 | tf_op jit(solution)/shard_map/ppermute | solution.py:236
  59.4 4.0 %collective-permute-start.7 = (bf16[2,96,384]{2,1,0:T(8,128)(2,1)S(1)}, bf16[2,96,384]{2,1,0:T(8,128)(2,1)S(1)}, u32[]{:S(2)}, u32[]{:S(2)}) collective-permute-start(bf16[2,96,384]{2,1,0:T(8,128)(2,1)S(1)} %collective-permute-done.6.a_ref), channel_id=1, source_target_pairs={{0,1},{1,0},{2,3},{3,2},{4,5},{5,4},{6,7},{7,6},{8,9},{9,8},{10,11... | collective-permute-start | bytes 442376 | tf_op jit(solution)/shard_map/ppermute | solution.py:236
  60.3 6.9 %collective-permute-start.22 = (bf16[4,96,384]{2,1,0:T(8,128)(2,1)S(1)}, bf16[4,96,384]{2,1,0:T(8,128)(2,1)S(1)}, u32[]{:S(2)}, u32[]{:S(2)}) collective-permute-start(bf16[4,96,384]{2,1,0:T(8,128)(2,1)S(1)} %shard_map.87.refs_4_), channel_id=1, source_target_pairs={{0,3},{1,2},{2,1},{3,0},{4,7},{5,6},{6,5},{7,4},{8,11},{9,10},{10,... | collective-permute-start | bytes 884744 | tf_op jit(solution)/shard_map/ppermute | solution.py:236
  62.7 5.7 %collective-permute-start.15 = (bf16[4,96,384]{2,1,0:T(8,128)(2,1)S(1)}, bf16[4,96,384]{2,1,0:T(8,128)(2,1)S(1)}, u32[]{:S(2)}, u32[]{:S(2)}) collective-permute-start(bf16[4,96,384]{2,1,0:T(8,128)(2,1)S(1)} %shard_map.83.refs_2_), channel_id=1, source_target_pairs={{0,1},{1,0},{2,3},{3,2},{4,5},{5,4},{6,7},{7,6},{8,9},{9,8},{10,11... | collective-permute-start | bytes 884744 | tf_op jit(solution)/shard_map/ppermute | solution.py:236
  63.5 7.9 %collective-permute-start.8 = (bf16[4,96,384]{2,1,0:T(8,128)(2,1)S(1)}, bf16[4,96,384]{2,1,0:T(8,128)(2,1)S(1)}, u32[]{:S(2)}, u32[]{:S(2)}) collective-permute-start(bf16[4,96,384]{2,1,0:T(8,128)(2,1)S(1)} %shard_map.79.refs_0_), channel_id=1, source_target_pairs={{0,4},{1,5},{2,6},{3,7},{4,0},{5,1},{6,2},{7,3},{8,12},{9,13},{10,... | collective-permute-start | bytes 884744 | tf_op jit(solution)/shard_map/ppermute | solution.py:236

commit v4 on v3

--- a/solution.py
+++ b/solution.py
@@ -10,7 +10,7 @@
 
 HD = 128
 ROWS = (96, 96, 96)
-ORDERS = ((4, 1, 3), (1, 3, 4), (3, 4, 1))
+ORDERS = ((1, 4, 3), (3, 1, 4), (4, 3, 1))
 HALVES = (True, True, True)
 GATHER = (False, False, False)
 CHUNK = 16
@@ -204,20 +204,16 @@
     out_ref[half:] = b_ref[...]
 
 
-def place_kernel(meta_ref, *refs):
-    pieces, out, sems = refs[:-2], refs[-2], refs[-1]
+def place_kernel(chains, meta_ref, *refs):
+    pieces, out, sems = refs[-2 - 2 * len(chains) : -2], refs[-2], refs[-1]
     size = pieces[0].shape[2]
     copies = []
-    first = 0
-    for c, part in enumerate(ROWS):
-        held = pieces[first].shape[0]
-        for spot in range(8):
-            piece = pieces[first + spot // held].at[spot % held]
-            target = meta_ref[1] ^ combos(ORDERS[c])[spot]
-            to = out.at[pl.ds(rows_of(c).start, part), columns(target, size)]
+    for i, c in enumerate(chains):
+        for spot, step in enumerate(combos(ORDERS[c])):
+            piece = pieces[2 * i + spot // 4].at[spot % 4]
+            to = out.at[pl.ds(rows_of(c).start, ROWS[c]), columns(meta_ref[1] ^ step, size)]
             copies.append(pltpu.make_async_copy(piece, to, sems.at[len(copies)]))
             copies[-1].start()
-        first += 8 // held
     for copy in copies:
         copy.wait()
 
@@ -345,14 +341,20 @@
             )(moved[c], near)
             ready += [four, swap(four, c, 0)]
 
-    return pl.pallas_call(
-        place_kernel,
-        out_shape=shape((rows, width), BF16),
-        in_specs=smem() + vmem(len(ready)),
-        out_specs=hbm()[0],
-        scratch_shapes=[pltpu.SemaphoreType.DMA((8 * len(ROWS),))],
-        **small,
-    )(meta, *ready)
+    out = []
+    for chains in ((0, 1), (2,)):
+        out = [
+            pl.pallas_call(
+                functools.partial(place_kernel, chains),
+                out_shape=shape((rows, width), BF16),
+                in_specs=smem() + hbm(len(out)) + vmem(2 * len(chains)),
+                out_specs=hbm()[0],
+                scratch_shapes=[pltpu.SemaphoreType.DMA((8 * len(chains),))],
+                input_output_aliases={1: 0} if out else {},
+                **small,
+            )(meta, *out, *ready[2 * chains[0] : 2 * chains[-1] + 2])
+        ]
+    return out[0]
 
 
 def solution(mesh):

time: 73.5 us -> 73.8 us (level)
  Pallas kernels: 17.5 us -> 18.6 us
  waiting for transfers between devices: 30.4 us -> 29.6 us
    ppermute x18, waiting for transfers between devices: 13.3 us -> 11 us  [swap(): return lax.ppermute(array, 'head', [(i, i ^ step) for i in range(n_head)])]
    ppermute x3, waiting for transfers between devices: 9.48 us -> 10.9 us  [body(): lax.ppermute(fresh, 'queue', [(i, (i - 1) % n_queue) for i in range(n_que...]
    pallas_call x1 -> x2, Pallas kernels: 1.95 us -> 3.1 us  [body(): pl.pallas_call(functools.partial(place_kernel, chains), out_shape=shape((...]
  transfers between devices with their start and end apart: 23 -> 23, of which waited for: 14 -> 15; matrix products, arithmetic and copies ran while one was open for 0% -> 0% of each run, Pallas kernels for 10% -> 12%
where the time goes in v4:
time: 73.8 us; the launch traced here: 73.7 us
  waiting for transfers between devices  29.6 us (40%)
  starting transfers between devices  24.4 us (33%)
  Pallas kernels  18.6 us (25%)
  between operations  0.99 us (1%)
    ppermute x18, starting transfers between devices, swap(): return lax.ppermute(array, 'head', [(i, i ^ step) for i in range(n_head)])  19.5 us
    ppermute x18, waiting for transfers between devices, swap(): return lax.ppermute(array, 'head', [(i, i ^ step) for i in range(n_head)])  11 us
    ppermute x3, waiting for transfers between devices, body(): lax.ppermute(fresh, 'queue', [(i, (i - 1) % n_queue) for i in range(n_que...  10.9 us
    ppermute x1, waiting for transfers between devices, body(): cross = lax.ppermute(kv, ('queue', 'head'), route)  7.62 us
    pallas_call x1, Pallas kernels, body(): pl.pallas_call(near_kernel, out_shape=(shape((rows, size), BF16),) + (sha...  5.14 us
    pallas_call x1, Pallas kernels, body(): pl.pallas_call(keys_kernel, out_shape=(shape((2, rows, size), BF16), shap...  4.83 us
    ppermute x1, starting transfers between devices, body(): cross = lax.ppermute(kv, ('queue', 'head'), route)  3.85 us
    pallas_call x1, Pallas kernels, body(): pl.pallas_call(join_kernel, out_shape=tuple((shape((n, part, size), BF16)...  3.36 us
  transfers between devices with their start and end apart: 23, of which 15 were waited for; matrix products, arithmetic and copies ran while one was open for 0% of the time, Pallas kernels for 12%

profile of v4, /device:TPU:89, one launch (start us, length us, event | category | flops | bytes accessed | tf_op | source)
XLA Modules:
  0.0 73.7 jit_solution(13592665581610129712)
XLA Ops:
  0.7 4.8 %shard_map.73 = (bf16[2,288,384]{2,1,0:T(8,128)(2,1)S(1)}, f32[1,9216]{1,0:T(1,128)S(1)}) custom-call(s32[1]{0:T(128)S(6)} %copy.10.level_ref, bf16[288,3072]{1,0:T(8,128)(2,1)} %x_ref.5, f32[16,9216]{1,0:T(8,128)} %mod_hbm.1, bf16[3,3072,384]{2,1,0:T(8,128)(2,1)} %bitcast.6), custom_call_target="tpu_custom_call" | custom-call | flops 1358954496 | bytes 4718592 | tf_op jit(solution)/shard_map/pallas_call | solution.py:234
  5.5 0.7 collective-permute-start
  6.3 3.9 %collective-permute-start.1 = (bf16[2,288,384]{2,1,0:T(8,128)(2,1)S(1)}, bf16[2,288,384]{2,1,0:T(8,128)(2,1)S(1)}, u32[]{:S(2)}, u32[]{:S(2)}) collective-permute-start(bf16[2,288,384]{2,1,0:T(8,128)(2,1)S(1)} %get-tuple-element.24.kv_ref), channel_id=1, source_target_pairs={{0,1},{1,0},{2,3},{3,2},{4,5},{5,4},{6,7},{7,6},{8,16},{9,17},{10,... | collective-permute-start | bytes 1327112 | tf_op jit(solution)/shard_map/ppermute | solution.py:257
  10.1 0.1 pad_add_fusion.meta_ref
  10.2 5.1 %shard_map.74 = (bf16[288,384]{1,0:T(8,128)(2,1)S(1)}, f32[288,384]{1,0:T(8,128)S(1)}, f32[288,384]{1,0:T(8,128)S(1)}, f32[288,384]{1,0:T(8,128)S(1)}) custom-call(s32[2]{0:T(128)S(1)} %pad_add_fusion.meta_ref, s32[32]{0:T(128)S(1)} %copy-done.2, s32[2,32]{1,0:T(2,128)S(1)} %bitcast.4, bf16[288,3072]{1,0:T(8,128)(2,1)S(1)} %copy-done, ...), custom_call_target="tpu_custom_call" | custom-call | flops 1 | bytes 1 | tf_op jit(solution)/shard_map/pallas_call | solution.py:259
  15.4 7.6 %collective-permute-done.1.far_ref = bf16[2,288,384]{2,1,0:T(8,128)(2,1)S(1)} collective-permute-done((bf16[2,288,384]{2,1,0:T(8,128)(2,1)S(1)}, bf16[2,288,384]{2,1,0:T(8,128)(2,1)S(1)}, u32[]{:S(2)}, u32[]{:S(2)}) %collective-permute-start.1) | collective-permute-done | bytes 442400 | tf_op jit(solution)/shard_map/ppermute | solution.py:257
  23.0 3.4 %shard_map.75 = (bf16[2,96,384]{2,1,0:T(8,128)(2,1)S(1)}, bf16[2,96,384]{2,1,0:T(8,128)(2,1)S(1)}, bf16[2,96,384]{2,1,0:T(8,128)(2,1)S(1)}, bf16[2,96,384]{2,1,0...) custom-call(s32[2]{0:T(128)S(1)} %pad_add_fusion.meta_ref, ...), custom_call_target="tpu_custom_call" | custom-call | flops 1358954496 | bytes 2359296 | tf_op jit(solution)/shard_map/pallas_call | solution.py:275
  26.3 2.6 %collective-permute-start.10 = (bf16[2,96,384]{2,1,0:T(8,128)(2,1)S(1)}, bf16[2,96,384]{2,1,0:T(8,128)(2,1)S(1)}, u32[]{:S(2)}, u32[]{:S(2)}) collective-permute-start(bf16[2,96,384]{2,1,0:T(8,128)(2,1)S(1)} %get-tuple-element.36), channel_id=1, source_target_pairs={{0,3},{1,2},{2,1},{3,0},{4,7},{5,6},{6,5},{7,4},{8,11},{9,10},{10,... | collective-permute-start | bytes 442376 | tf_op jit(solution)/shard_map/ppermute | solution.py:232
  29.0 0.7 collective-permute-start.9
  29.7 0.8 %collective-permute-start.2 = (bf16[2,96,384]{2,1,0:T(8,128)(2,1)S(1)}, bf16[2,96,384]{2,1,0:T(8,128)(2,1)S(1)}, u32[]{:S(2)}, u32[]{:S(2)}) collective-permute-start(bf16[2,96,384]{2,1,0:T(8,128)(2,1)S(1)} %get-tuple-element.30), channel_id=1, source_target_pairs={{0,1},{1,0},{2,3},{3,2},{4,5},{5,4},{6,7},{7,6},{8,9},{9,8},{10,11... | collective-permute-start | bytes 442376 | tf_op jit(solution)/shard_map/ppermute | solution.py:232
  30.5 1.2 %collective-permute-done.10.refs_1_ = bf16[2,96,384]{2,1,0:T(8,128)(2,1)S(1)} collective-permute-done((bf16[2,96,384]{2,1,0:T(8,128)(2,1)S(1)}, bf16[2,96,384]{2,1,0:T(8,128)(2,1)S(1)}, u32[]{:S(2)}, u32[]{:S(2)}) %collective-permute-start.10) | collective-permute-done | bytes 147488 | tf_op jit(solution)/shard_map/ppermute | solution.py:232
  31.7 0.4 collective-permute-start.11
  32.0 1.2 %collective-permute-done.3.refs_1_ = bf16[2,96,384]{2,1,0:T(8,128)(2,1)S(1)} collective-permute-done((bf16[2,96,384]{2,1,0:T(8,128)(2,1)S(1)}, bf16[2,96,384]{2,1,0:T(8,128)(2,1)S(1)}, u32[]{:S(2)}, u32[]{:S(2)}) %collective-permute-start.3) | collective-permute-done | bytes 147488 | tf_op jit(solution)/shard_map/ppermute | solution.py:232
  33.3 0.1 collective-permute-start.4
  33.4 0.4 collective-permute-done.17.refs_1_
  33.9 1.0 %collective-permute-start.16 = (bf16[2,96,384]{2,1,0:T(8,128)(2,1)S(1)}, bf16[2,96,384]{2,1,0:T(8,128)(2,1)S(1)}, u32[]{:S(2)}, u32[]{:S(2)}) collective-permute-start(bf16[2,96,384]{2,1,0:T(8,128)(2,1)S(1)} %get-tuple-element.38), channel_id=1, source_target_pairs={{0,4},{1,5},{2,6},{3,7},{4,0},{5,1},{6,2},{7,3},{8,12},{9,13},{10,... | collective-permute-start | bytes 442376 | tf_op jit(solution)/shard_map/ppermute | solution.py:232
  34.9 0.8 %collective-permute-done.9.refs_1_ = bf16[2,96,384]{2,1,0:T(8,128)(2,1)S(1)} collective-permute-done((bf16[2,96,384]{2,1,0:T(8,128)(2,1)S(1)}, bf16[2,96,384]{2,1,0:T(8,128)(2,1)S(1)}, u32[]{:S(2)}, u32[]{:S(2)}) %collective-permute-start.9) | collective-permute-done | bytes 147488 | tf_op jit(solution)/shard_map/ppermute | solution.py:232
  35.8 1.6 %collective-permute-start.18 = (bf16[2,96,384]{2,1,0:T(8,128)(2,1)S(1)}, bf16[2,96,384]{2,1,0:T(8,128)(2,1)S(1)}, u32[]{:S(2)}, u32[]{:S(2)}) collective-permute-start(bf16[2,96,384]{2,1,0:T(8,128)(2,1)S(1)} %shard_map.85), channel_id=1, source_target_pairs={{0,3},{1,2},{2,1},{3,0},{4,7},{5,6},{6,5},{7,4},{8,11},{9,10},{10,... | collective-permute-start | bytes 442376 | tf_op jit(solution)/shard_map/ppermute | solution.py:232
  37.4 0.1 shard_map.81.keep_ref
  37.5 0.4 collective-permute-start.12
  37.9 0.1 shard_map.77.keep_ref
  38.0 1.6 %collective-permute-start.5 = (bf16[2,96,384]{2,1,0:T(8,128)(2,1)S(1)}, bf16[2,96,384]{2,1,0:T(8,128)(2,1)S(1)}, u32[]{:S(2)}, u32[]{:S(2)}) collective-permute-start(bf16[2,96,384]{2,1,0:T(8,128)(2,1)S(1)} %shard_map.77.keep_ref), channel_id=1, source_target_pairs={{0,3},{1,2},{2,1},{3,0},{4,7},{5,6},{6,5},{7,4},{8,11},{9,10},{10,... | collective-permute-start | bytes 442376 | tf_op jit(solution)/shard_map/ppermute | solution.py:232
  39.6 1.4 %collective-permute-done.18.refs_2_ = bf16[2,96,384]{2,1,0:T(8,128)(2,1)S(1)} collective-permute-done((bf16[2,96,384]{2,1,0:T(8,128)(2,1)S(1)}, bf16[2,96,384]{2,1,0:T(8,128)(2,1)S(1)}, u32[]{:S(2)}, u32[]{:S(2)}) %collective-permute-start.18) | collective-permute-done | bytes 147488 | tf_op jit(solution)/shard_map/ppermute | solution.py:232
  41.0 0.1 shard_map.86.keep_ref
  41.1 0.1 collective-permute-start.19
  41.2 0.4 collective-permute-done.12.got_ref
  41.6 0.6 shard_map.82
  42.2 0.1 collective-permute-start.13
  42.3 1.0 %collective-permute-done.5.got_ref = bf16[2,96,384]{2,1,0:T(8,128)(2,1)S(1)} collective-permute-done((bf16[2,96,384]{2,1,0:T(8,128)(2,1)S(1)}, bf16[2,96,384]{2,1,0:T(8,128)(2,1)S(1)}, u32[]{:S(2)}, u32[]{:S(2)}) %collective-permute-start.5) | collective-permute-done | bytes 147488 | tf_op jit(solution)/shard_map/ppermute | solution.py:232
  43.3 0.6 shard_map.78
  43.9 0.1 collective-permute-start.6
  44.0 1.2 %collective-permute-done.19.got_ref = bf16[2,96,384]{2,1,0:T(8,128)(2,1)S(1)} collective-permute-done((bf16[2,96,384]{2,1,0:T(8,128)(2,1)S(1)}, bf16[2,96,384]{2,1,0:T(8,128)(2,1)S(1)}, u32[]{:S(2)}, u32[]{:S(2)}) %collective-permute-start.19) | collective-permute-done | bytes 147488 | tf_op jit(solution)/shard_map/ppermute | solution.py:232
  45.1 0.6 shard_map.87
  45.8 0.1 collective-permute-start.20
  45.9 6.6 %collective-permute-done.13.a_ref = bf16[2,96,384]{2,1,0:T(8,128)(2,1)S(1)} collective-permute-done((bf16[2,96,384]{2,1,0:T(8,128)(2,1)S(1)}, bf16[2,96,384]{2,1,0:T(8,128)(2,1)S(1)}, u32[]{:S(2)}, u32[]{:S(2)}) %collective-permute-start.13) | collective-permute-done | bytes 147488 | tf_op jit(solution)/shard_map/ppermute | solution.py:328
  52.5 0.5 collective-permute-start.14
  52.9 3.2 %collective-permute-done.6.a_ref = bf16[2,96,384]{2,1,0:T(8,128)(2,1)S(1)} collective-permute-done((bf16[2,96,384]{2,1,0:T(8,128)(2,1)S(1)}, bf16[2,96,384]{2,1,0:T(8,128)(2,1)S(1)}, u32[]{:S(2)}, u32[]{:S(2)}) %collective-permute-start.6) | collective-permute-done | bytes 147488 | tf_op jit(solution)/shard_map/ppermute | solution.py:328
  56.1 1.9 %collective-permute-start.7 = (bf16[2,96,384]{2,1,0:T(8,128)(2,1)S(1)}, bf16[2,96,384]{2,1,0:T(8,128)(2,1)S(1)}, u32[]{:S(2)}, u32[]{:S(2)}) collective-permute-start(bf16[2,96,384]{2,1,0:T(8,128)(2,1)S(1)} %collective-permute-done.6.a_ref), channel_id=1, source_target_pairs={{0,4},{1,5},{2,6},{3,7},{4,0},{5,1},{6,2},{7,3},{8,12},{9,13},{10,... | collective-permute-start | bytes 442376 | tf_op jit(solution)/shard_map/ppermute | solution.py:232
  58.0 1.2 %collective-permute-done.20.a_ref = bf16[2,96,384]{2,1,0:T(8,128)(2,1)S(1)} collective-permute-done((bf16[2,96,384]{2,1,0:T(8,128)(2,1)S(1)}, bf16[2,96,384]{2,1,0:T(8,128)(2,1)S(1)}, u32[]{:S(2)}, u32[]{:S(2)}) %collective-permute-start.20) | collective-permute-done | bytes 147488 | tf_op jit(solution)/shard_map/ppermute | solution.py:328
  59.1 2.3 %collective-permute-start.21 = (bf16[2,96,384]{2,1,0:T(8,128)(2,1)S(1)}, bf16[2,96,384]{2,1,0:T(8,128)(2,1)S(1)}, u32[]{:S(2)}, u32[]{:S(2)}) collective-permute-start(bf16[2,96,384]{2,1,0:T(8,128)(2,1)S(1)} %collective-permute-done.20.a_ref), channel_id=1, source_target_pairs={{0,3},{1,2},{2,1},{3,0},{4,7},{5,6},{6,5},{7,4},{8,11},{9,10},{10,... | collective-permute-start | bytes 442376 | tf_op jit(solution)/shard_map/ppermute | solution.py:232
  61.4 0.5 collective-permute-start.15
  62.0 1.4 %collective-permute-start.8 = (bf16[4,96,384]{2,1,0:T(8,128)(2,1)S(1)}, bf16[4,96,384]{2,1,0:T(8,128)(2,1)S(1)}, u32[]{:S(2)}, u32[]{:S(2)}) collective-permute-start(bf16[4,96,384]{2,1,0:T(8,128)(2,1)S(1)} %shard_map.79.refs_0_), channel_id=1, source_target_pairs={{0,1},{1,0},{2,3},{3,2},{4,5},{5,4},{6,7},{7,6},{8,9},{9,8},{10,11... | collective-permute-start | bytes 884744 | tf_op jit(solution)/shard_map/ppermute | solution.py:232
  63.4 0.9 %collective-permute-done.21.b_ref = bf16[2,96,384]{2,1,0:T(8,128)(2,1)S(1)} collective-permute-done((bf16[2,96,384]{2,1,0:T(8,128)(2,1)S(1)}, bf16[2,96,384]{2,1,0:T(8,128)(2,1)S(1)}, u32[]{:S(2)}, u32[]{:S(2)}) %collective-permute-start.21) | collective-permute-done | bytes 147488 | tf_op jit(solution)/shard_map/ppermute | solution.py:232
  64.4 3.6 %collective-permute-start.22 = (bf16[4,96,384]{2,1,0:T(8,128)(2,1)S(1)}, bf16[4,96,384]{2,1,0:T(8,128)(2,1)S(1)}, u32[]{:S(2)}, u32[]{:S(2)}) collective-permute-start(bf16[4,96,384]{2,1,0:T(8,128)(2,1)S(1)} %shard_map.88.refs_1_), channel_id=1, source_target_pairs={{0,4},{1,5},{2,6},{3,7},{4,0},{5,1},{6,2},{7,3},{8,12},{9,13},{10,... | collective-permute-start | bytes 884744 | tf_op jit(solution)/shard_map/ppermute | solution.py:232
  68.0 0.3 collective-permute-done.15.refs_3_
  68.3 1.7 %shard_map.84.refs_0_ = bf16[288,3072]{1,0:T(8,128)(2,1)} custom-call(s32[2]{0:T(128)S(1)} %pad_add_fusion.meta_ref, bf16[4,96,384]{2,1,0:T(8,128)(2,1)S(1)} %shard_map.79.refs_0_, bf16[4,96,384]{2,1,0:T(8,128)(2,1)S(1)} %collective-permute-done.8.refs_1_, bf16[4,96,384]{2,1,0:T(8,128)(2,1)S(1)} %shard_map.83.refs_2_, ...), custom_call_target="tpu_custom_call" | custom-call | flops 147456 | bytes 294912 | tf_op jit(solution)/shard_map/pallas_call | solution.py:347
  70.0 2.1 %collective-permute-done.22.refs_2_ = bf16[4,96,384]{2,1,0:T(8,128)(2,1)S(1)} collective-permute-done((bf16[4,96,384]{2,1,0:T(8,128)(2,1)S(1)}, bf16[4,96,384]{2,1,0:T(8,128)(2,1)S(1)}, u32[]{:S(2)}, u32[]{:S(2)}) %collective-permute-start.22) | collective-permute-done | bytes 294944 | tf_op jit(solution)/shard_map/ppermute | solution.py:232
  72.1 1.4 %shard_map.89 = bf16[288,3072]{1,0:T(8,128)(2,1)} custom-call(s32[2]{0:T(128)S(1)} %pad_add_fusion.meta_ref, bf16[288,3072]{1,0:T(8,128)(2,1)} %shard_map.84.refs_0_, bf16[4,96,384]{2,1,0:T(8,128)(2,1)S(1)} %shard_map.88.refs_1_, bf16[4,96,384]{2,1,0:T(8,128)(2,1)S(1)} %collective-permute-done.22.refs_2_), custom_call_target="tpu_custom_call", output_to_operand_aliasing={{}: (1, {})} | custom-call | flops 147456 | bytes 294912 | tf_op jit(solution)/shard_map/pallas_call | solution.py:347
  (24 shorter events, 0.2 us)
Async XLA Ops:
  0.7 9.5 %copy-start = (bf16[288,3072]{1,0:T(8,128)(2,1)S(1)}, bf16[288,3072]{1,0:T(8,128)(2,1)}, u32[]{:S(2)}) copy-start(bf16[288,3072]{1,0:T(8,128)(2,1)} %x_ref.5) | copy-start | bytes 5308420
  0.7 9.5 %copy-start.1 = (s32[32,2]{0,1:T(2,128)S(1)}, s32[32,2]{0,1:T(2,128)}, u32[]{:S(2)}) copy-start(s32[32,2]{0,1:T(2,128)} %param.10) | copy-start | bytes 772
  0.7 9.5 %copy-start.2 = (s32[32]{0:T(128)S(1)}, s32[32]{0:T(128)}, u32[]{:S(2)}) copy-start(s32[32]{0:T(128)} %counts_ref.3) | copy-start | bytes 388
  5.5 4.7 %collective-permute-start = (bf16[2,288,384]{2,1,0:T(8,128)(2,1)S(1)}, bf16[2,288,384]{2,1,0:T(8,128)(2,1)S(1)}, u32[]{:S(2)}, u32[]{:S(2)}) collective-permute-start(bf16[2,288,384]{2,1,0:T(8,128)(2,1)S(1)} %get-tuple-element.24.kv_ref), channel_id=1, source_target_pairs={{0,8},{8,0},{16,24},{24,16},{32,40},{40,32},{48,56},{56,48},{64,72... | collective-permute-start | bytes 1327112 | tf_op jit(solution)/shard_map/ppermute | solution.py:250
  6.3 16.7 %collective-permute-start.1 = (bf16[2,288,384]{2,1,0:T(8,128)(2,1)S(1)}, bf16[2,288,384]{2,1,0:T(8,128)(2,1)S(1)}, u32[]{:S(2)}, u32[]{:S(2)}) collective-permute-start(bf16[2,288,384]{2,1,0:T(8,128)(2,1)S(1)} %get-tuple-element.24.kv_ref), channel_id=1, source_target_pairs={{0,1},{1,0},{2,3},{3,2},{4,5},{5,4},{6,7},{7,6},{8,16},{9,17},{10,... | collective-permute-start | bytes 1327112 | tf_op jit(solution)/shard_map/ppermute | solution.py:257
  10.2 12.8 %copy-start.3 = (bf16[384,3072]{1,0:T(8,128)(2,1)S(1)}, bf16[384,3072]{1,0:T(8,128)(2,1)}, u32[]{:S(2)}) copy-start(bf16[384,3072]{1,0:T(8,128)(2,1)} %w_ref.1) | copy-start | bytes 7077892
  26.3 5.3 %collective-permute-start.10 = (bf16[2,96,384]{2,1,0:T(8,128)(2,1)S(1)}, bf16[2,96,384]{2,1,0:T(8,128)(2,1)S(1)}, u32[]{:S(2)}, u32[]{:S(2)}) collective-permute-start(bf16[2,96,384]{2,1,0:T(8,128)(2,1)S(1)} %get-tuple-element.36), channel_id=1, source_target_pairs={{0,3},{1,2},{2,1},{3,0},{4,7},{5,6},{6,5},{7,4},{8,11},{9,10},{10,... | collective-permute-start | bytes 442376 | tf_op jit(solution)/shard_map/ppermute | solution.py:232
  29.0 4.3 %collective-permute-start.3 = (bf16[2,96,384]{2,1,0:T(8,128)(2,1)S(1)}, bf16[2,96,384]{2,1,0:T(8,128)(2,1)S(1)}, u32[]{:S(2)}, u32[]{:S(2)}) collective-permute-start(bf16[2,96,384]{2,1,0:T(8,128)(2,1)S(1)} %get-tuple-element.32), channel_id=1, source_target_pairs={{0,1},{1,0},{2,3},{3,2},{4,5},{5,4},{6,7},{7,6},{8,9},{9,8},{10,11... | collective-permute-start | bytes 442376 | tf_op jit(solution)/shard_map/ppermute | solution.py:232
  29.0 4.9 %collective-permute-start.17 = (bf16[2,96,384]{2,1,0:T(8,128)(2,1)S(1)}, bf16[2,96,384]{2,1,0:T(8,128)(2,1)S(1)}, u32[]{:S(2)}, u32[]{:S(2)}) collective-permute-start(bf16[2,96,384]{2,1,0:T(8,128)(2,1)S(1)} %get-tuple-element.40), channel_id=1, source_target_pairs={{0,4},{1,5},{2,6},{3,7},{4,0},{5,1},{6,2},{7,3},{8,12},{9,13},{10,... | collective-permute-start | bytes 442376 | tf_op jit(solution)/shard_map/ppermute | solution.py:232
  29.0 6.8 %collective-permute-start.9 = (bf16[2,96,384]{2,1,0:T(8,128)(2,1)S(1)}, bf16[2,96,384]{2,1,0:T(8,128)(2,1)S(1)}, u32[]{:S(2)}, u32[]{:S(2)}) collective-permute-start(bf16[2,96,384]{2,1,0:T(8,128)(2,1)S(1)} %get-tuple-element.34), channel_id=1, source_target_pairs={{0,3},{1,2},{2,1},{3,0},{4,7},{5,6},{6,5},{7,4},{8,11},{9,10},{10,... | collective-permute-start | bytes 442376 | tf_op jit(solution)/shard_map/ppermute | solution.py:232
  29.7 8.2 %collective-permute-start.2 = (bf16[2,96,384]{2,1,0:T(8,128)(2,1)S(1)}, bf16[2,96,384]{2,1,0:T(8,128)(2,1)S(1)}, u32[]{:S(2)}, u32[]{:S(2)}) collective-permute-start(bf16[2,96,384]{2,1,0:T(8,128)(2,1)S(1)} %get-tuple-element.30), channel_id=1, source_target_pairs={{0,1},{1,0},{2,3},{3,2},{4,5},{5,4},{6,7},{7,6},{8,9},{9,8},{10,11... | collective-permute-start | bytes 442376 | tf_op jit(solution)/shard_map/ppermute | solution.py:232
  31.7 5.8 %collective-permute-start.11 = (bf16[2,96,384]{2,1,0:T(8,128)(2,1)S(1)}, bf16[2,96,384]{2,1,0:T(8,128)(2,1)S(1)}, u32[]{:S(2)}, u32[]{:S(2)}) collective-permute-start(bf16[2,96,384]{2,1,0:T(8,128)(2,1)S(1)} %shard_map.80), channel_id=1, source_target_pairs={{0,1},{1,0},{2,3},{3,2},{4,5},{5,4},{6,7},{7,6},{8,9},{9,8},{10,11... | collective-permute-start | bytes 442376 | tf_op jit(solution)/shard_map/ppermute | solution.py:232
  33.3 4.6 %collective-permute-start.4 = (bf16[2,96,384]{2,1,0:T(8,128)(2,1)S(1)}, bf16[2,96,384]{2,1,0:T(8,128)(2,1)S(1)}, u32[]{:S(2)}, u32[]{:S(2)}) collective-permute-start(bf16[2,96,384]{2,1,0:T(8,128)(2,1)S(1)} %shard_map.76), channel_id=1, source_target_pairs={{0,4},{1,5},{2,6},{3,7},{4,0},{5,1},{6,2},{7,3},{8,12},{9,13},{10,... | collective-permute-start | bytes 442376 | tf_op jit(solution)/shard_map/ppermute | solution.py:232
  33.9 5.7 %collective-permute-start.16 = (bf16[2,96,384]{2,1,0:T(8,128)(2,1)S(1)}, bf16[2,96,384]{2,1,0:T(8,128)(2,1)S(1)}, u32[]{:S(2)}, u32[]{:S(2)}) collective-permute-start(bf16[2,96,384]{2,1,0:T(8,128)(2,1)S(1)} %get-tuple-element.38), channel_id=1, source_target_pairs={{0,4},{1,5},{2,6},{3,7},{4,0},{5,1},{6,2},{7,3},{8,12},{9,13},{10,... | collective-permute-start | bytes 442376 | tf_op jit(solution)/shard_map/ppermute | solution.py:232
  35.8 5.2 %collective-permute-start.18 = (bf16[2,96,384]{2,1,0:T(8,128)(2,1)S(1)}, bf16[2,96,384]{2,1,0:T(8,128)(2,1)S(1)}, u32[]{:S(2)}, u32[]{:S(2)}) collective-permute-start(bf16[2,96,384]{2,1,0:T(8,128)(2,1)S(1)} %shard_map.85), channel_id=1, source_target_pairs={{0,3},{1,2},{2,1},{3,0},{4,7},{5,6},{6,5},{7,4},{8,11},{9,10},{10,... | collective-permute-start | bytes 442376 | tf_op jit(solution)/shard_map/ppermute | solution.py:232
  37.5 4.1 %collective-permute-start.12 = (bf16[2,96,384]{2,1,0:T(8,128)(2,1)S(1)}, bf16[2,96,384]{2,1,0:T(8,128)(2,1)S(1)}, u32[]{:S(2)}, u32[]{:S(2)}) collective-permute-start(bf16[2,96,384]{2,1,0:T(8,128)(2,1)S(1)} %shard_map.81.keep_ref), channel_id=1, source_target_pairs={{0,4},{1,5},{2,6},{3,7},{4,0},{5,1},{6,2},{7,3},{8,12},{9,13},{10,... | collective-permute-start | bytes 442376 | tf_op jit(solution)/shard_map/ppermute | solution.py:232
  38.0 5.3 %collective-permute-start.5 = (bf16[2,96,384]{2,1,0:T(8,128)(2,1)S(1)}, bf16[2,96,384]{2,1,0:T(8,128)(2,1)S(1)}, u32[]{:S(2)}, u32[]{:S(2)}) collective-permute-start(bf16[2,96,384]{2,1,0:T(8,128)(2,1)S(1)} %shard_map.77.keep_ref), channel_id=1, source_target_pairs={{0,3},{1,2},{2,1},{3,0},{4,7},{5,6},{6,5},{7,4},{8,11},{9,10},{10,... | collective-permute-start | bytes 442376 | tf_op jit(solution)/shard_map/ppermute | solution.py:232
  41.1 4.1 %collective-permute-start.19 = (bf16[2,96,384]{2,1,0:T(8,128)(2,1)S(1)}, bf16[2,96,384]{2,1,0:T(8,128)(2,1)S(1)}, u32[]{:S(2)}, u32[]{:S(2)}) collective-permute-start(bf16[2,96,384]{2,1,0:T(8,128)(2,1)S(1)} %shard_map.86.keep_ref), channel_id=1, source_target_pairs={{0,1},{1,0},{2,3},{3,2},{4,5},{5,4},{6,7},{7,6},{8,9},{9,8},{10,11... | collective-permute-start | bytes 442376 | tf_op jit(solution)/shard_map/ppermute | solution.py:232
  42.2 10.3 %collective-permute-start.13 = (bf16[2,96,384]{2,1,0:T(8,128)(2,1)S(1)}, bf16[2,96,384]{2,1,0:T(8,128)(2,1)S(1)}, u32[]{:S(2)}, u32[]{:S(2)}) collective-permute-start(bf16[2,96,384]{2,1,0:T(8,128)(2,1)S(1)} %shard_map.82), channel_id=1, source_target_pairs={{0,248},{8,0},{16,8},{24,16},{32,24},{40,32},{48,40},{56,48},{64,5... | collective-permute-start | bytes 442376 | tf_op jit(solution)/shard_map/ppermute | solution.py:328
  43.9 12.2 %collective-permute-start.6 = (bf16[2,96,384]{2,1,0:T(8,128)(2,1)S(1)}, bf16[2,96,384]{2,1,0:T(8,128)(2,1)S(1)}, u32[]{:S(2)}, u32[]{:S(2)}) collective-permute-start(bf16[2,96,384]{2,1,0:T(8,128)(2,1)S(1)} %shard_map.78), channel_id=1, source_target_pairs={{0,248},{8,0},{16,8},{24,16},{32,24},{40,32},{48,40},{56,48},{64,5... | collective-permute-start | bytes 442376 | tf_op jit(solution)/shard_map/ppermute | solution.py:328
  45.8 13.4 %collective-permute-start.20 = (bf16[2,96,384]{2,1,0:T(8,128)(2,1)S(1)}, bf16[2,96,384]{2,1,0:T(8,128)(2,1)S(1)}, u32[]{:S(2)}, u32[]{:S(2)}) collective-permute-start(bf16[2,96,384]{2,1,0:T(8,128)(2,1)S(1)} %shard_map.87), channel_id=1, source_target_pairs={{0,248},{8,0},{16,8},{24,16},{32,24},{40,32},{48,40},{56,48},{64,5... | collective-permute-start | bytes 442376 | tf_op jit(solution)/shard_map/ppermute | solution.py:328
  52.5 8.9 %collective-permute-start.14 = (bf16[2,96,384]{2,1,0:T(8,128)(2,1)S(1)}, bf16[2,96,384]{2,1,0:T(8,128)(2,1)S(1)}, u32[]{:S(2)}, u32[]{:S(2)}) collective-permute-start(bf16[2,96,384]{2,1,0:T(8,128)(2,1)S(1)} %collective-permute-done.13.a_ref), channel_id=1, source_target_pairs={{0,1},{1,0},{2,3},{3,2},{4,5},{5,4},{6,7},{7,6},{8,9},{9,8},{10,11... | collective-permute-start | bytes 442376 | tf_op jit(solution)/shard_map/ppermute | solution.py:232
  56.1 5.8 %collective-permute-start.7 = (bf16[2,96,384]{2,1,0:T(8,128)(2,1)S(1)}, bf16[2,96,384]{2,1,0:T(8,128)(2,1)S(1)}, u32[]{:S(2)}, u32[]{:S(2)}) collective-permute-start(bf16[2,96,384]{2,1,0:T(8,128)(2,1)S(1)} %collective-permute-done.6.a_ref), channel_id=1, source_target_pairs={{0,4},{1,5},{2,6},{3,7},{4,0},{5,1},{6,2},{7,3},{8,12},{9,13},{10,... | collective-permute-start | bytes 442376 | tf_op jit(solution)/shard_map/ppermute | solution.py:232
  59.1 5.2 %collective-permute-start.21 = (bf16[2,96,384]{2,1,0:T(8,128)(2,1)S(1)}, bf16[2,96,384]{2,1,0:T(8,128)(2,1)S(1)}, u32[]{:S(2)}, u32[]{:S(2)}) collective-permute-start(bf16[2,96,384]{2,1,0:T(8,128)(2,1)S(1)} %collective-permute-done.20.a_ref), channel_id=1, source_target_pairs={{0,3},{1,2},{2,1},{3,0},{4,7},{5,6},{6,5},{7,4},{8,11},{9,10},{10,... | collective-permute-start | bytes 442376 | tf_op jit(solution)/shard_map/ppermute | solution.py:232
  61.4 6.9 %collective-permute-start.15 = (bf16[4,96,384]{2,1,0:T(8,128)(2,1)S(1)}, bf16[4,96,384]{2,1,0:T(8,128)(2,1)S(1)}, u32[]{:S(2)}, u32[]{:S(2)}) collective-permute-start(bf16[4,96,384]{2,1,0:T(8,128)(2,1)S(1)} %shard_map.83.refs_2_), channel_id=1, source_target_pairs={{0,3},{1,2},{2,1},{3,0},{4,7},{5,6},{6,5},{7,4},{8,11},{9,10},{10,... | collective-permute-start | bytes 884744 | tf_op jit(solution)/shard_map/ppermute | solution.py:232
  62.0 6.3 %collective-permute-start.8 = (bf16[4,96,384]{2,1,0:T(8,128)(2,1)S(1)}, bf16[4,96,384]{2,1,0:T(8,128)(2,1)S(1)}, u32[]{:S(2)}, u32[]{:S(2)}) collective-permute-start(bf16[4,96,384]{2,1,0:T(8,128)(2,1)S(1)} %shard_map.79.refs_0_), channel_id=1, source_target_pairs={{0,1},{1,0},{2,3},{3,2},{4,5},{5,4},{6,7},{7,6},{8,9},{9,8},{10,11... | collective-permute-start | bytes 884744 | tf_op jit(solution)/shard_map/ppermute | solution.py:232
  64.4 7.7 %collective-permute-start.22 = (bf16[4,96,384]{2,1,0:T(8,128)(2,1)S(1)}, bf16[4,96,384]{2,1,0:T(8,128)(2,1)S(1)}, u32[]{:S(2)}, u32[]{:S(2)}) collective-permute-start(bf16[4,96,384]{2,1,0:T(8,128)(2,1)S(1)} %shard_map.88.refs_1_), channel_id=1, source_target_pairs={{0,4},{1,5},{2,6},{3,7},{4,0},{5,1},{6,2},{7,3},{8,12},{9,13},{10,... | collective-permute-start | bytes 884744 | tf_op jit(solution)/shard_map/ppermute | solution.py:232

commit v5 on v4

--- a/solution.py
+++ b/solution.py
@@ -204,15 +204,14 @@
     out_ref[half:] = b_ref[...]
 
 
-def place_kernel(chains, meta_ref, *refs):
-    pieces, out, sems = refs[-2 - 2 * len(chains) : -2], refs[-2], refs[-1]
+def place_kernel(half, meta_ref, *refs):
+    pieces, out, sems = refs[-2 - len(ROWS) : -2], refs[-2], refs[-1]
     size = pieces[0].shape[2]
     copies = []
-    for i, c in enumerate(chains):
-        for spot, step in enumerate(combos(ORDERS[c])):
-            piece = pieces[2 * i + spot // 4].at[spot % 4]
-            to = out.at[pl.ds(rows_of(c).start, ROWS[c]), columns(meta_ref[1] ^ step, size)]
-            copies.append(pltpu.make_async_copy(piece, to, sems.at[len(copies)]))
+    for c, (piece, part) in enumerate(zip(pieces, ROWS)):
+        for spot, step in enumerate(combos(ORDERS[c])[4 * half : 4 * half + 4]):
+            to = out.at[pl.ds(rows_of(c).start, part), columns(meta_ref[1] ^ step, size)]
+            copies.append(pltpu.make_async_copy(piece.at[spot], to, sems.at[len(copies)]))
             copies[-1].start()
     for copy in copies:
         copy.wait()
@@ -342,17 +341,17 @@
             ready += [four, swap(four, c, 0)]
 
     out = []
-    for chains in ((0, 1), (2,)):
+    for half in range(2):
         out = [
             pl.pallas_call(
-                functools.partial(place_kernel, chains),
+                functools.partial(place_kernel, half),
                 out_shape=shape((rows, width), BF16),
-                in_specs=smem() + hbm(len(out)) + vmem(2 * len(chains)),
+                in_specs=smem() + hbm(len(out)) + vmem(len(ROWS)),
                 out_specs=hbm()[0],
-                scratch_shapes=[pltpu.SemaphoreType.DMA((8 * len(chains),))],
+                scratch_shapes=[pltpu.SemaphoreType.DMA((4 * len(ROWS),))],
                 input_output_aliases={1: 0} if out else {},
                 **small,
-            )(meta, *out, *ready[2 * chains[0] : 2 * chains[-1] + 2])
+            )(meta, *out, *ready[half::2])
         ]
     return out[0]
 

time: 73.8 us -> 72.7 us (0.985)
  starting transfers between devices: 24.4 us -> 19.7 us
  waiting for transfers between devices: 29.6 us -> 33.2 us
    ppermute x18, starting transfers between devices: 19.5 us -> 14.8 us  [swap(): return lax.ppermute(array, 'head', [(i, i ^ step) for i in range(n_head)])]
    ppermute x3, waiting for transfers between devices: 10.9 us -> 14.8 us  [body(): lax.ppermute(fresh, 'queue', [(i, (i - 1) % n_queue) for i in range(n_que...]
where the time goes in v5:
time: 72.7 us; the launch traced here: 72.6 us
  waiting for transfers between devices  33.2 us (46%)
  starting transfers between devices  19.7 us (27%)
  Pallas kernels  18.6 us (26%)
  between operations  1 us (1%)
    ppermute x18, starting transfers between devices, swap(): return lax.ppermute(array, 'head', [(i, i ^ step) for i in range(n_head)])  14.8 us
    ppermute x3, waiting for transfers between devices, body(): lax.ppermute(fresh, 'queue', [(i, (i - 1) % n_queue) for i in range(n_que...  14.8 us
    ppermute x18, waiting for transfers between devices, swap(): return lax.ppermute(array, 'head', [(i, i ^ step) for i in range(n_head)])  10.7 us
    ppermute x1, waiting for transfers between devices, body(): cross = lax.ppermute(kv, ('queue', 'head'), route)  7.66 us
    pallas_call x1, Pallas kernels, body(): pl.pallas_call(near_kernel, out_shape=(shape((rows, size), BF16),) + (sha...  5.14 us
    pallas_call x1, Pallas kernels, body(): pl.pallas_call(keys_kernel, out_shape=(shape((2, rows, size), BF16), shap...  4.81 us
    ppermute x1, starting transfers between devices, body(): cross = lax.ppermute(kv, ('queue', 'head'), route)  3.88 us
    pallas_call x1, Pallas kernels, body(): pl.pallas_call(join_kernel, out_shape=tuple((shape((n, part, size), BF16)...  3.36 us
  transfers between devices with their start and end apart: 23, of which 15 were waited for; matrix products, arithmetic and copies ran while one was open for 0% of the time, Pallas kernels for 12%

profile of v5, /device:TPU:89, one launch (start us, length us, event | category | flops | bytes accessed | tf_op | source)
XLA Modules:
  0.0 72.6 jit_solution(15389720858933000350)
XLA Ops:
  0.7 4.8 %shard_map.73 = (bf16[2,288,384]{2,1,0:T(8,128)(2,1)S(1)}, f32[1,9216]{1,0:T(1,128)S(1)}) custom-call(s32[1]{0:T(128)S(6)} %copy.10.level_ref, bf16[288,3072]{1,0:T(8,128)(2,1)} %x_ref.5, f32[16,9216]{1,0:T(8,128)} %mod_hbm.1, bf16[3,3072,384]{2,1,0:T(8,128)(2,1)} %bitcast.6), custom_call_target="tpu_custom_call" | custom-call | flops 1358954496 | bytes 4718592 | tf_op jit(solution)/shard_map/pallas_call | solution.py:233
  5.5 0.8 %collective-permute-start = (bf16[2,288,384]{2,1,0:T(8,128)(2,1)S(1)}, bf16[2,288,384]{2,1,0:T(8,128)(2,1)S(1)}, u32[]{:S(2)}, u32[]{:S(2)}) collective-permute-start(bf16[2,288,384]{2,1,0:T(8,128)(2,1)S(1)} %get-tuple-element.24.kv_ref), channel_id=1, source_target_pairs={{0,8},{8,0},{16,24},{24,16},{32,40},{40,32},{48,56},{56,48},{64,72... | collective-permute-start | bytes 1327112 | tf_op jit(solution)/shard_map/ppermute | solution.py:249
  6.3 3.9 %collective-permute-start.1 = (bf16[2,288,384]{2,1,0:T(8,128)(2,1)S(1)}, bf16[2,288,384]{2,1,0:T(8,128)(2,1)S(1)}, u32[]{:S(2)}, u32[]{:S(2)}) collective-permute-start(bf16[2,288,384]{2,1,0:T(8,128)(2,1)S(1)} %get-tuple-element.24.kv_ref), channel_id=1, source_target_pairs={{0,1},{1,0},{2,3},{3,2},{4,5},{5,4},{6,7},{7,6},{8,16},{9,17},{10,... | collective-permute-start | bytes 1327112 | tf_op jit(solution)/shard_map/ppermute | solution.py:256
  10.1 0.1 pad_add_fusion.meta_ref
  10.2 5.1 %shard_map.74 = (bf16[288,384]{1,0:T(8,128)(2,1)S(1)}, f32[288,384]{1,0:T(8,128)S(1)}, f32[288,384]{1,0:T(8,128)S(1)}, f32[288,384]{1,0:T(8,128)S(1)}) custom-call(s32[2]{0:T(128)S(1)} %pad_add_fusion.meta_ref, s32[32]{0:T(128)S(1)} %copy-done.2, s32[2,32]{1,0:T(2,128)S(1)} %bitcast.4, bf16[288,3072]{1,0:T(8,128)(2,1)S(1)} %copy-done, ...), custom_call_target="tpu_custom_call" | custom-call | flops 1 | bytes 1 | tf_op jit(solution)/shard_map/pallas_call | solution.py:258
  15.4 7.7 %collective-permute-done.1.far_ref = bf16[2,288,384]{2,1,0:T(8,128)(2,1)S(1)} collective-permute-done((bf16[2,288,384]{2,1,0:T(8,128)(2,1)S(1)}, bf16[2,288,384]{2,1,0:T(8,128)(2,1)S(1)}, u32[]{:S(2)}, u32[]{:S(2)}) %collective-permute-start.1) | collective-permute-done | bytes 442400 | tf_op jit(solution)/shard_map/ppermute | solution.py:256
  23.1 3.4 %shard_map.75 = (bf16[2,96,384]{2,1,0:T(8,128)(2,1)S(1)}, bf16[2,96,384]{2,1,0:T(8,128)(2,1)S(1)}, bf16[2,96,384]{2,1,0:T(8,128)(2,1)S(1)}, bf16[2,96,384]{2,1,0...) custom-call(s32[2]{0:T(128)S(1)} %pad_add_fusion.meta_ref, ...), custom_call_target="tpu_custom_call" | custom-call | flops 1358954496 | bytes 2359296 | tf_op jit(solution)/shard_map/pallas_call | solution.py:274
  26.4 0.1 collective-permute-start.15
  26.5 2.6 %collective-permute-start.9 = (bf16[2,96,384]{2,1,0:T(8,128)(2,1)S(1)}, bf16[2,96,384]{2,1,0:T(8,128)(2,1)S(1)}, u32[]{:S(2)}, u32[]{:S(2)}) collective-permute-start(bf16[2,96,384]{2,1,0:T(8,128)(2,1)S(1)} %get-tuple-element.36), channel_id=1, source_target_pairs={{0,3},{1,2},{2,1},{3,0},{4,7},{5,6},{6,5},{7,4},{8,11},{9,10},{10,... | collective-permute-start | bytes 442376 | tf_op jit(solution)/shard_map/ppermute | solution.py:231
  29.1 1.4 %collective-permute-start.14 = (bf16[2,96,384]{2,1,0:T(8,128)(2,1)S(1)}, bf16[2,96,384]{2,1,0:T(8,128)(2,1)S(1)}, u32[]{:S(2)}, u32[]{:S(2)}) collective-permute-start(bf16[2,96,384]{2,1,0:T(8,128)(2,1)S(1)} %get-tuple-element.38), channel_id=1, source_target_pairs={{0,4},{1,5},{2,6},{3,7},{4,0},{5,1},{6,2},{7,3},{8,12},{9,13},{10,... | collective-permute-start | bytes 442376 | tf_op jit(solution)/shard_map/ppermute | solution.py:231
  30.5 0.8 %collective-permute-start.8 = (bf16[2,96,384]{2,1,0:T(8,128)(2,1)S(1)}, bf16[2,96,384]{2,1,0:T(8,128)(2,1)S(1)}, u32[]{:S(2)}, u32[]{:S(2)}) collective-permute-start(bf16[2,96,384]{2,1,0:T(8,128)(2,1)S(1)} %get-tuple-element.34), channel_id=1, source_target_pairs={{0,3},{1,2},{2,1},{3,0},{4,7},{5,6},{6,5},{7,4},{8,11},{9,10},{10,... | collective-permute-start | bytes 442376 | tf_op jit(solution)/shard_map/ppermute | solution.py:231
  31.3 2.1 %collective-permute-start.16 = (bf16[2,96,384]{2,1,0:T(8,128)(2,1)S(1)}, bf16[2,96,384]{2,1,0:T(8,128)(2,1)S(1)}, u32[]{:S(2)}, u32[]{:S(2)}) collective-permute-start(bf16[2,96,384]{2,1,0:T(8,128)(2,1)S(1)} %shard_map.84), channel_id=1, source_target_pairs={{0,3},{1,2},{2,1},{3,0},{4,7},{5,6},{6,5},{7,4},{8,11},{9,10},{10,... | collective-permute-start | bytes 442376 | tf_op jit(solution)/shard_map/ppermute | solution.py:231
  33.4 0.2 collective-permute-start.10
  33.7 0.4 collective-permute-done.3.refs_1_
  34.1 0.9 %collective-permute-start.2 = (bf16[2,96,384]{2,1,0:T(8,128)(2,1)S(1)}, bf16[2,96,384]{2,1,0:T(8,128)(2,1)S(1)}, u32[]{:S(2)}, u32[]{:S(2)}) collective-permute-start(bf16[2,96,384]{2,1,0:T(8,128)(2,1)S(1)} %get-tuple-element.30), channel_id=1, source_target_pairs={{0,1},{1,0},{2,3},{3,2},{4,5},{5,4},{6,7},{7,6},{8,9},{9,8},{10,11... | collective-permute-start | bytes 442376 | tf_op jit(solution)/shard_map/ppermute | solution.py:231
  35.1 1.1 %collective-permute-start.4 = (bf16[2,96,384]{2,1,0:T(8,128)(2,1)S(1)}, bf16[2,96,384]{2,1,0:T(8,128)(2,1)S(1)}, u32[]{:S(2)}, u32[]{:S(2)}) collective-permute-start(bf16[2,96,384]{2,1,0:T(8,128)(2,1)S(1)} %shard_map.76), channel_id=1, source_target_pairs={{0,4},{1,5},{2,6},{3,7},{4,0},{5,1},{6,2},{7,3},{8,12},{9,13},{10,... | collective-permute-start | bytes 442376 | tf_op jit(solution)/shard_map/ppermute | solution.py:231
  36.2 1.0 %collective-permute-done.16.refs_2_ = bf16[2,96,384]{2,1,0:T(8,128)(2,1)S(1)} collective-permute-done((bf16[2,96,384]{2,1,0:T(8,128)(2,1)S(1)}, bf16[2,96,384]{2,1,0:T(8,128)(2,1)S(1)}, u32[]{:S(2)}, u32[]{:S(2)}) %collective-permute-start.16) | collective-permute-done | bytes 147488 | tf_op jit(solution)/shard_map/ppermute | solution.py:231
  37.2 0.1 shard_map.85.keep_ref
  37.3 0.3 collective-permute-start.17
  37.6 0.1 shard_map.81.keep_ref
  37.7 0.9 %collective-permute-start.11 = (bf16[2,96,384]{2,1,0:T(8,128)(2,1)S(1)}, bf16[2,96,384]{2,1,0:T(8,128)(2,1)S(1)}, u32[]{:S(2)}, u32[]{:S(2)}) collective-permute-start(bf16[2,96,384]{2,1,0:T(8,128)(2,1)S(1)} %shard_map.81.keep_ref), channel_id=1, source_target_pairs={{0,4},{1,5},{2,6},{3,7},{4,0},{5,1},{6,2},{7,3},{8,12},{9,13},{10,... | collective-permute-start | bytes 442376 | tf_op jit(solution)/shard_map/ppermute | solution.py:231
  38.6 0.8 %collective-permute-done.2.refs_1_ = bf16[2,96,384]{2,1,0:T(8,128)(2,1)S(1)} collective-permute-done((bf16[2,96,384]{2,1,0:T(8,128)(2,1)S(1)}, bf16[2,96,384]{2,1,0:T(8,128)(2,1)S(1)}, u32[]{:S(2)}, u32[]{:S(2)}) %collective-permute-start.2) | collective-permute-done | bytes 147488 | tf_op jit(solution)/shard_map/ppermute | solution.py:231
  39.4 0.1 shard_map.77.keep_ref
  39.5 1.7 %collective-permute-start.5 = (bf16[2,96,384]{2,1,0:T(8,128)(2,1)S(1)}, bf16[2,96,384]{2,1,0:T(8,128)(2,1)S(1)}, u32[]{:S(2)}, u32[]{:S(2)}) collective-permute-start(bf16[2,96,384]{2,1,0:T(8,128)(2,1)S(1)} %shard_map.77.keep_ref), channel_id=1, source_target_pairs={{0,3},{1,2},{2,1},{3,0},{4,7},{5,6},{6,5},{7,4},{8,11},{9,10},{10,... | collective-permute-start | bytes 442376 | tf_op jit(solution)/shard_map/ppermute | solution.py:231
  41.2 0.2 collective-permute-done.17.got_ref
  41.4 0.6 shard_map.86
  42.0 0.1 collective-permute-start.18
  42.1 0.6 shard_map.82
  42.7 0.1 collective-permute-start.12
  42.8 2.0 %collective-permute-done.5.got_ref = bf16[2,96,384]{2,1,0:T(8,128)(2,1)S(1)} collective-permute-done((bf16[2,96,384]{2,1,0:T(8,128)(2,1)S(1)}, bf16[2,96,384]{2,1,0:T(8,128)(2,1)S(1)}, u32[]{:S(2)}, u32[]{:S(2)}) %collective-permute-start.5) | collective-permute-done | bytes 147488 | tf_op jit(solution)/shard_map/ppermute | solution.py:231
  44.8 0.6 shard_map.78
  45.4 0.1 collective-permute-start.6
  45.5 11.1 %collective-permute-done.18.a_ref = bf16[2,96,384]{2,1,0:T(8,128)(2,1)S(1)} collective-permute-done((bf16[2,96,384]{2,1,0:T(8,128)(2,1)S(1)}, bf16[2,96,384]{2,1,0:T(8,128)(2,1)S(1)}, u32[]{:S(2)}, u32[]{:S(2)}) %collective-permute-start.18) | collective-permute-done | bytes 147488 | tf_op jit(solution)/shard_map/ppermute | solution.py:327
  56.6 0.4 collective-permute-start.19
  57.0 2.6 %collective-permute-done.12.a_ref = bf16[2,96,384]{2,1,0:T(8,128)(2,1)S(1)} collective-permute-done((bf16[2,96,384]{2,1,0:T(8,128)(2,1)S(1)}, bf16[2,96,384]{2,1,0:T(8,128)(2,1)S(1)}, u32[]{:S(2)}, u32[]{:S(2)}) %collective-permute-start.12) | collective-permute-done | bytes 147488 | tf_op jit(solution)/shard_map/ppermute | solution.py:327
  59.6 0.5 collective-permute-start.13
  60.2 1.1 %collective-permute-done.6.a_ref = bf16[2,96,384]{2,1,0:T(8,128)(2,1)S(1)} collective-permute-done((bf16[2,96,384]{2,1,0:T(8,128)(2,1)S(1)}, bf16[2,96,384]{2,1,0:T(8,128)(2,1)S(1)}, u32[]{:S(2)}, u32[]{:S(2)}) %collective-permute-start.6) | collective-permute-done | bytes 147488 | tf_op jit(solution)/shard_map/ppermute | solution.py:327
  61.2 0.6 collective-permute-done.19.b_ref
  61.8 1.0 %collective-permute-start.22 = (bf16[4,96,384]{2,1,0:T(8,128)(2,1)S(1)}, bf16[4,96,384]{2,1,0:T(8,128)(2,1)S(1)}, u32[]{:S(2)}, u32[]{:S(2)}) collective-permute-start(bf16[4,96,384]{2,1,0:T(8,128)(2,1)S(1)} %shard_map.87.refs_2_), channel_id=1, source_target_pairs={{0,4},{1,5},{2,6},{3,7},{4,0},{5,1},{6,2},{7,3},{8,12},{9,13},{10,... | collective-permute-start | bytes 884744 | tf_op jit(solution)/shard_map/ppermute | solution.py:231
  62.8 0.8 %collective-permute-done.13.b_ref = bf16[2,96,384]{2,1,0:T(8,128)(2,1)S(1)} collective-permute-done((bf16[2,96,384]{2,1,0:T(8,128)(2,1)S(1)}, bf16[2,96,384]{2,1,0:T(8,128)(2,1)S(1)}, u32[]{:S(2)}, u32[]{:S(2)}) %collective-permute-start.13) | collective-permute-done | bytes 147488 | tf_op jit(solution)/shard_map/ppermute | solution.py:231
  63.7 0.1 collective-permute-start.21
  63.8 1.4 %collective-permute-done.7.b_ref = bf16[2,96,384]{2,1,0:T(8,128)(2,1)S(1)} collective-permute-done((bf16[2,96,384]{2,1,0:T(8,128)(2,1)S(1)}, bf16[2,96,384]{2,1,0:T(8,128)(2,1)S(1)}, u32[]{:S(2)}, u32[]{:S(2)}) %collective-permute-start.7) | collective-permute-done | bytes 147488 | tf_op jit(solution)/shard_map/ppermute | solution.py:231
  65.2 0.6 collective-permute-start.20
  65.9 1.5 %shard_map.88.refs_0_ = bf16[288,3072]{1,0:T(8,128)(2,1)} custom-call(s32[2]{0:T(128)S(1)} %pad_add_fusion.meta_ref, bf16[4,96,384]{2,1,0:T(8,128)(2,1)S(1)} %shard_map.79.refs_0_, bf16[4,96,384]{2,1,0:T(8,128)(2,1)S(1)} %shard_map.83.refs_1_, bf16[4,96,384]{2,1,0:T(8,128)(2,1)S(1)} %shard_map.87.refs_2_), custom_call_target="tpu_custom_call" | custom-call | flops 147456 | bytes 294912 | tf_op jit(solution)/shard_map/pallas_call | solution.py:346
  67.4 1.0 %collective-permute-done.22.refs_3_ = bf16[4,96,384]{2,1,0:T(8,128)(2,1)S(1)} collective-permute-done((bf16[4,96,384]{2,1,0:T(8,128)(2,1)S(1)}, bf16[4,96,384]{2,1,0:T(8,128)(2,1)S(1)}, u32[]{:S(2)}, u32[]{:S(2)}) %collective-permute-start.22) | collective-permute-done | bytes 294944 | tf_op jit(solution)/shard_map/ppermute | solution.py:231
  68.4 2.2 %collective-permute-done.21.refs_2_ = bf16[4,96,384]{2,1,0:T(8,128)(2,1)S(1)} collective-permute-done((bf16[4,96,384]{2,1,0:T(8,128)(2,1)S(1)}, bf16[4,96,384]{2,1,0:T(8,128)(2,1)S(1)}, u32[]{:S(2)}, u32[]{:S(2)}) %collective-permute-start.21) | collective-permute-done | bytes 294944 | tf_op jit(solution)/shard_map/ppermute | solution.py:231
  70.5 0.4 collective-permute-done.20.refs_1_
  70.9 1.6 %shard_map.89 = bf16[288,3072]{1,0:T(8,128)(2,1)} custom-call(s32[2]{0:T(128)S(1)} %pad_add_fusion.meta_ref, bf16[288,3072]{1,0:T(8,128)(2,1)} %shard_map.88.refs_0_, bf16[4,96,384]{2,1,0:T(8,128)(2,1)S(1)} %collective-permute-done.20.refs_1_, bf16[4,96,384]{2,1,0:T(8,128)(2,1)S(1)} %collective-permute-done.21.refs_2_, ...), custom_call_target="tpu_custom_call", output_to_operand_aliasing={{}: (1, {})} | custom-call | flops 147456 | bytes 294912 | tf_op jit(solution)/shard_map/pallas_call | solution.py:346
  (24 shorter events, 0.3 us)
Async XLA Ops:
  0.7 9.6 %copy-start = (bf16[288,3072]{1,0:T(8,128)(2,1)S(1)}, bf16[288,3072]{1,0:T(8,128)(2,1)}, u32[]{:S(2)}) copy-start(bf16[288,3072]{1,0:T(8,128)(2,1)} %x_ref.5) | copy-start | bytes 5308420
  0.7 9.6 %copy-start.1 = (s32[32,2]{0,1:T(2,128)S(1)}, s32[32,2]{0,1:T(2,128)}, u32[]{:S(2)}) copy-start(s32[32,2]{0,1:T(2,128)} %param.10) | copy-start | bytes 772
  0.7 9.5 %copy-start.2 = (s32[32]{0:T(128)S(1)}, s32[32]{0:T(128)}, u32[]{:S(2)}) copy-start(s32[32]{0:T(128)} %counts_ref.3) | copy-start | bytes 388
  5.5 4.7 %collective-permute-start = (bf16[2,288,384]{2,1,0:T(8,128)(2,1)S(1)}, bf16[2,288,384]{2,1,0:T(8,128)(2,1)S(1)}, u32[]{:S(2)}, u32[]{:S(2)}) collective-permute-start(bf16[2,288,384]{2,1,0:T(8,128)(2,1)S(1)} %get-tuple-element.24.kv_ref), channel_id=1, source_target_pairs={{0,8},{8,0},{16,24},{24,16},{32,40},{40,32},{48,56},{56,48},{64,72... | collective-permute-start | bytes 1327112 | tf_op jit(solution)/shard_map/ppermute | solution.py:249
  6.3 16.8 %collective-permute-start.1 = (bf16[2,288,384]{2,1,0:T(8,128)(2,1)S(1)}, bf16[2,288,384]{2,1,0:T(8,128)(2,1)S(1)}, u32[]{:S(2)}, u32[]{:S(2)}) collective-permute-start(bf16[2,288,384]{2,1,0:T(8,128)(2,1)S(1)} %get-tuple-element.24.kv_ref), channel_id=1, source_target_pairs={{0,1},{1,0},{2,3},{3,2},{4,5},{5,4},{6,7},{7,6},{8,16},{9,17},{10,... | collective-permute-start | bytes 1327112 | tf_op jit(solution)/shard_map/ppermute | solution.py:256
  10.2 12.8 %copy-start.3 = (bf16[384,3072]{1,0:T(8,128)(2,1)S(1)}, bf16[384,3072]{1,0:T(8,128)(2,1)}, u32[]{:S(2)}) copy-start(bf16[384,3072]{1,0:T(8,128)(2,1)} %w_ref.1) | copy-start | bytes 7077892
  26.4 4.8 %collective-permute-start.15 = (bf16[2,96,384]{2,1,0:T(8,128)(2,1)S(1)}, bf16[2,96,384]{2,1,0:T(8,128)(2,1)S(1)}, u32[]{:S(2)}, u32[]{:S(2)}) collective-permute-start(bf16[2,96,384]{2,1,0:T(8,128)(2,1)S(1)} %get-tuple-element.40), channel_id=1, source_target_pairs={{0,4},{1,5},{2,6},{3,7},{4,0},{5,1},{6,2},{7,3},{8,12},{9,13},{10,... | collective-permute-start | bytes 442376 | tf_op jit(solution)/shard_map/ppermute | solution.py:231
  26.5 6.9 %collective-permute-start.9 = (bf16[2,96,384]{2,1,0:T(8,128)(2,1)S(1)}, bf16[2,96,384]{2,1,0:T(8,128)(2,1)S(1)}, u32[]{:S(2)}, u32[]{:S(2)}) collective-permute-start(bf16[2,96,384]{2,1,0:T(8,128)(2,1)S(1)} %get-tuple-element.36), channel_id=1, source_target_pairs={{0,3},{1,2},{2,1},{3,0},{4,7},{5,6},{6,5},{7,4},{8,11},{9,10},{10,... | collective-permute-start | bytes 442376 | tf_op jit(solution)/shard_map/ppermute | solution.py:231
  29.1 5.0 %collective-permute-start.3 = (bf16[2,96,384]{2,1,0:T(8,128)(2,1)S(1)}, bf16[2,96,384]{2,1,0:T(8,128)(2,1)S(1)}, u32[]{:S(2)}, u32[]{:S(2)}) collective-permute-start(bf16[2,96,384]{2,1,0:T(8,128)(2,1)S(1)} %get-tuple-element.32), channel_id=1, source_target_pairs={{0,1},{1,0},{2,3},{3,2},{4,5},{5,4},{6,7},{7,6},{8,9},{9,8},{10,11... | collective-permute-start | bytes 442376 | tf_op jit(solution)/shard_map/ppermute | solution.py:231
  29.1 6.0 %collective-permute-start.14 = (bf16[2,96,384]{2,1,0:T(8,128)(2,1)S(1)}, bf16[2,96,384]{2,1,0:T(8,128)(2,1)S(1)}, u32[]{:S(2)}, u32[]{:S(2)}) collective-permute-start(bf16[2,96,384]{2,1,0:T(8,128)(2,1)S(1)} %get-tuple-element.38), channel_id=1, source_target_pairs={{0,4},{1,5},{2,6},{3,7},{4,0},{5,1},{6,2},{7,3},{8,12},{9,13},{10,... | collective-permute-start | bytes 442376 | tf_op jit(solution)/shard_map/ppermute | solution.py:231
  30.5 7.2 %collective-permute-start.8 = (bf16[2,96,384]{2,1,0:T(8,128)(2,1)S(1)}, bf16[2,96,384]{2,1,0:T(8,128)(2,1)S(1)}, u32[]{:S(2)}, u32[]{:S(2)}) collective-permute-start(bf16[2,96,384]{2,1,0:T(8,128)(2,1)S(1)} %get-tuple-element.34), channel_id=1, source_target_pairs={{0,3},{1,2},{2,1},{3,0},{4,7},{5,6},{6,5},{7,4},{8,11},{9,10},{10,... | collective-permute-start | bytes 442376 | tf_op jit(solution)/shard_map/ppermute | solution.py:231
  31.3 5.9 %collective-permute-start.16 = (bf16[2,96,384]{2,1,0:T(8,128)(2,1)S(1)}, bf16[2,96,384]{2,1,0:T(8,128)(2,1)S(1)}, u32[]{:S(2)}, u32[]{:S(2)}) collective-permute-start(bf16[2,96,384]{2,1,0:T(8,128)(2,1)S(1)} %shard_map.84), channel_id=1, source_target_pairs={{0,3},{1,2},{2,1},{3,0},{4,7},{5,6},{6,5},{7,4},{8,11},{9,10},{10,... | collective-permute-start | bytes 442376 | tf_op jit(solution)/shard_map/ppermute | solution.py:231
  33.4 4.2 %collective-permute-start.10 = (bf16[2,96,384]{2,1,0:T(8,128)(2,1)S(1)}, bf16[2,96,384]{2,1,0:T(8,128)(2,1)S(1)}, u32[]{:S(2)}, u32[]{:S(2)}) collective-permute-start(bf16[2,96,384]{2,1,0:T(8,128)(2,1)S(1)} %shard_map.80), channel_id=1, source_target_pairs={{0,1},{1,0},{2,3},{3,2},{4,5},{5,4},{6,7},{7,6},{8,9},{9,8},{10,11... | collective-permute-start | bytes 442376 | tf_op jit(solution)/shard_map/ppermute | solution.py:231
  34.1 5.3 %collective-permute-start.2 = (bf16[2,96,384]{2,1,0:T(8,128)(2,1)S(1)}, bf16[2,96,384]{2,1,0:T(8,128)(2,1)S(1)}, u32[]{:S(2)}, u32[]{:S(2)}) collective-permute-start(bf16[2,96,384]{2,1,0:T(8,128)(2,1)S(1)} %get-tuple-element.30), channel_id=1, source_target_pairs={{0,1},{1,0},{2,3},{3,2},{4,5},{5,4},{6,7},{7,6},{8,9},{9,8},{10,11... | collective-permute-start | bytes 442376 | tf_op jit(solution)/shard_map/ppermute | solution.py:231
  35.1 4.4 %collective-permute-start.4 = (bf16[2,96,384]{2,1,0:T(8,128)(2,1)S(1)}, bf16[2,96,384]{2,1,0:T(8,128)(2,1)S(1)}, u32[]{:S(2)}, u32[]{:S(2)}) collective-permute-start(bf16[2,96,384]{2,1,0:T(8,128)(2,1)S(1)} %shard_map.76), channel_id=1, source_target_pairs={{0,4},{1,5},{2,6},{3,7},{4,0},{5,1},{6,2},{7,3},{8,12},{9,13},{10,... | collective-permute-start | bytes 442376 | tf_op jit(solution)/shard_map/ppermute | solution.py:231
  37.3 4.1 %collective-permute-start.17 = (bf16[2,96,384]{2,1,0:T(8,128)(2,1)S(1)}, bf16[2,96,384]{2,1,0:T(8,128)(2,1)S(1)}, u32[]{:S(2)}, u32[]{:S(2)}) collective-permute-start(bf16[2,96,384]{2,1,0:T(8,128)(2,1)S(1)} %shard_map.85.keep_ref), channel_id=1, source_target_pairs={{0,1},{1,0},{2,3},{3,2},{4,5},{5,4},{6,7},{7,6},{8,9},{9,8},{10,11... | collective-permute-start | bytes 442376 | tf_op jit(solution)/shard_map/ppermute | solution.py:231
  37.7 4.4 %collective-permute-start.11 = (bf16[2,96,384]{2,1,0:T(8,128)(2,1)S(1)}, bf16[2,96,384]{2,1,0:T(8,128)(2,1)S(1)}, u32[]{:S(2)}, u32[]{:S(2)}) collective-permute-start(bf16[2,96,384]{2,1,0:T(8,128)(2,1)S(1)} %shard_map.81.keep_ref), channel_id=1, source_target_pairs={{0,4},{1,5},{2,6},{3,7},{4,0},{5,1},{6,2},{7,3},{8,12},{9,13},{10,... | collective-permute-start | bytes 442376 | tf_op jit(solution)/shard_map/ppermute | solution.py:231
  39.5 5.3 %collective-permute-start.5 = (bf16[2,96,384]{2,1,0:T(8,128)(2,1)S(1)}, bf16[2,96,384]{2,1,0:T(8,128)(2,1)S(1)}, u32[]{:S(2)}, u32[]{:S(2)}) collective-permute-start(bf16[2,96,384]{2,1,0:T(8,128)(2,1)S(1)} %shard_map.77.keep_ref), channel_id=1, source_target_pairs={{0,3},{1,2},{2,1},{3,0},{4,7},{5,6},{6,5},{7,4},{8,11},{9,10},{10,... | collective-permute-start | bytes 442376 | tf_op jit(solution)/shard_map/ppermute | solution.py:231
  42.0 14.6 %collective-permute-start.18 = (bf16[2,96,384]{2,1,0:T(8,128)(2,1)S(1)}, bf16[2,96,384]{2,1,0:T(8,128)(2,1)S(1)}, u32[]{:S(2)}, u32[]{:S(2)}) collective-permute-start(bf16[2,96,384]{2,1,0:T(8,128)(2,1)S(1)} %shard_map.86), channel_id=1, source_target_pairs={{0,248},{8,0},{16,8},{24,16},{32,24},{40,32},{48,40},{56,48},{64,5... | collective-permute-start | bytes 442376 | tf_op jit(solution)/shard_map/ppermute | solution.py:327
  42.7 16.9 %collective-permute-start.12 = (bf16[2,96,384]{2,1,0:T(8,128)(2,1)S(1)}, bf16[2,96,384]{2,1,0:T(8,128)(2,1)S(1)}, u32[]{:S(2)}, u32[]{:S(2)}) collective-permute-start(bf16[2,96,384]{2,1,0:T(8,128)(2,1)S(1)} %shard_map.82), channel_id=1, source_target_pairs={{0,248},{8,0},{16,8},{24,16},{32,24},{40,32},{48,40},{56,48},{64,5... | collective-permute-start | bytes 442376 | tf_op jit(solution)/shard_map/ppermute | solution.py:327
  45.4 15.8 %collective-permute-start.6 = (bf16[2,96,384]{2,1,0:T(8,128)(2,1)S(1)}, bf16[2,96,384]{2,1,0:T(8,128)(2,1)S(1)}, u32[]{:S(2)}, u32[]{:S(2)}) collective-permute-start(bf16[2,96,384]{2,1,0:T(8,128)(2,1)S(1)} %shard_map.78), channel_id=1, source_target_pairs={{0,248},{8,0},{16,8},{24,16},{32,24},{40,32},{48,40},{56,48},{64,5... | collective-permute-start | bytes 442376 | tf_op jit(solution)/shard_map/ppermute | solution.py:327
  56.6 5.2 %collective-permute-start.19 = (bf16[2,96,384]{2,1,0:T(8,128)(2,1)S(1)}, bf16[2,96,384]{2,1,0:T(8,128)(2,1)S(1)}, u32[]{:S(2)}, u32[]{:S(2)}) collective-permute-start(bf16[2,96,384]{2,1,0:T(8,128)(2,1)S(1)} %collective-permute-done.18.a_ref), channel_id=1, source_target_pairs={{0,3},{1,2},{2,1},{3,0},{4,7},{5,6},{6,5},{7,4},{8,11},{9,10},{10,... | collective-permute-start | bytes 442376 | tf_op jit(solution)/shard_map/ppermute | solution.py:231
  59.6 4.0 %collective-permute-start.13 = (bf16[2,96,384]{2,1,0:T(8,128)(2,1)S(1)}, bf16[2,96,384]{2,1,0:T(8,128)(2,1)S(1)}, u32[]{:S(2)}, u32[]{:S(2)}) collective-permute-start(bf16[2,96,384]{2,1,0:T(8,128)(2,1)S(1)} %collective-permute-done.12.a_ref), channel_id=1, source_target_pairs={{0,1},{1,0},{2,3},{3,2},{4,5},{5,4},{6,7},{7,6},{8,9},{9,8},{10,11... | collective-permute-start | bytes 442376 | tf_op jit(solution)/shard_map/ppermute | solution.py:231
  61.2 4.0 %collective-permute-start.7 = (bf16[2,96,384]{2,1,0:T(8,128)(2,1)S(1)}, bf16[2,96,384]{2,1,0:T(8,128)(2,1)S(1)}, u32[]{:S(2)}, u32[]{:S(2)}) collective-permute-start(bf16[2,96,384]{2,1,0:T(8,128)(2,1)S(1)} %collective-permute-done.6.a_ref), channel_id=1, source_target_pairs={{0,4},{1,5},{2,6},{3,7},{4,0},{5,1},{6,2},{7,3},{8,12},{9,13},{10,... | collective-permute-start | bytes 442376 | tf_op jit(solution)/shard_map/ppermute | solution.py:231
  61.8 6.5 %collective-permute-start.22 = (bf16[4,96,384]{2,1,0:T(8,128)(2,1)S(1)}, bf16[4,96,384]{2,1,0:T(8,128)(2,1)S(1)}, u32[]{:S(2)}, u32[]{:S(2)}) collective-permute-start(bf16[4,96,384]{2,1,0:T(8,128)(2,1)S(1)} %shard_map.87.refs_2_), channel_id=1, source_target_pairs={{0,4},{1,5},{2,6},{3,7},{4,0},{5,1},{6,2},{7,3},{8,12},{9,13},{10,... | collective-permute-start | bytes 884744 | tf_op jit(solution)/shard_map/ppermute | solution.py:231
  63.7 6.9 %collective-permute-start.21 = (bf16[4,96,384]{2,1,0:T(8,128)(2,1)S(1)}, bf16[4,96,384]{2,1,0:T(8,128)(2,1)S(1)}, u32[]{:S(2)}, u32[]{:S(2)}) collective-permute-start(bf16[4,96,384]{2,1,0:T(8,128)(2,1)S(1)} %shard_map.83.refs_1_), channel_id=1, source_target_pairs={{0,3},{1,2},{2,1},{3,0},{4,7},{5,6},{6,5},{7,4},{8,11},{9,10},{10,... | collective-permute-start | bytes 884744 | tf_op jit(solution)/shard_map/ppermute | solution.py:231
  65.2 5.7 %collective-permute-start.20 = (bf16[4,96,384]{2,1,0:T(8,128)(2,1)S(1)}, bf16[4,96,384]{2,1,0:T(8,128)(2,1)S(1)}, u32[]{:S(2)}, u32[]{:S(2)}) collective-permute-start(bf16[4,96,384]{2,1,0:T(8,128)(2,1)S(1)} %shard_map.79.refs_0_), channel_id=1, source_target_pairs={{0,1},{1,0},{2,3},{3,2},{4,5},{5,4},{6,7},{7,6},{8,9},{9,8},{10,11... | collective-permute-start | bytes 884744 | tf_op jit(solution)/shard_map/ppermute | solution.py:231

commit v6 on v5

--- a/solution.py
+++ b/solution.py
@@ -12,7 +12,7 @@
 ROWS = (96, 96, 96)
 ORDERS = ((1, 4, 3), (3, 1, 4), (4, 3, 1))
 HALVES = (True, True, True)
-GATHER = (False, False, False)
+GATHER = (True, False, False)
 CHUNK = 16
 LOADS = 3
 NEAR = 48
@@ -204,14 +204,15 @@
     out_ref[half:] = b_ref[...]
 
 
-def place_kernel(half, meta_ref, *refs):
-    pieces, out, sems = refs[-2 - len(ROWS) : -2], refs[-2], refs[-1]
+def place_kernel(plan, meta_ref, *refs):
+    pieces, out, sems = refs[-2 - len(plan) : -2], refs[-2], refs[-1]
     size = pieces[0].shape[2]
     copies = []
-    for c, (piece, part) in enumerate(zip(pieces, ROWS)):
-        for spot, step in enumerate(combos(ORDERS[c])[4 * half : 4 * half + 4]):
-            to = out.at[pl.ds(rows_of(c).start, part), columns(meta_ref[1] ^ step, size)]
-            copies.append(pltpu.make_async_copy(piece.at[spot], to, sems.at[len(copies)]))
+    for (c, first), piece in zip(plan, pieces):
+        for i in range(piece.shape[0]):
+            target = meta_ref[1] ^ combos(ORDERS[c])[first + i]
+            to = out.at[pl.ds(rows_of(c).start, ROWS[c]), columns(target, size)]
+            copies.append(pltpu.make_async_copy(piece.at[i], to, sems.at[len(copies)]))
             copies[-1].start()
     for copy in copies:
         copy.wait()
@@ -325,11 +326,12 @@
             **small,
         )(meta, latents, table, mine[c], other[c])
         moved[c] = lax.ppermute(fresh, "queue", [(i, (i - 1) % n_queue) for i in range(n_queue)])
-    ready = []
+    ready = [[], []]
     for c, part in enumerate(ROWS):
         near = swap(moved[c], c, 1)
         if GATHER[c]:
-            ready += [moved[c], near, swap(moved[c], c, 0), swap(near, c, 0)]
+            ready[0] += [((c, 0), moved[c]), ((c, 2), near)]
+            ready[1] += [((c, 4), swap(moved[c], c, 0)), ((c, 6), swap(near, c, 0))]
         else:
             four = pl.pallas_call(
                 concat_kernel,
@@ -338,20 +340,22 @@
                 out_specs=vmem()[0],
                 **small,
             )(moved[c], near)
-            ready += [four, swap(four, c, 0)]
+            ready[0] += [((c, 0), four)]
+            ready[1] += [((c, 4), swap(four, c, 0))]
 
     out = []
-    for half in range(2):
+    for group in ready:
+        plan, pieces = zip(*group)
         out = [
             pl.pallas_call(
-                functools.partial(place_kernel, half),
+                functools.partial(place_kernel, plan),
                 out_shape=shape((rows, width), BF16),
-                in_specs=smem() + hbm(len(out)) + vmem(len(ROWS)),
+                in_specs=smem() + hbm(len(out)) + vmem(len(pieces)),
                 out_specs=hbm()[0],
                 scratch_shapes=[pltpu.SemaphoreType.DMA((4 * len(ROWS),))],
                 input_output_aliases={1: 0} if out else {},
                 **small,
-            )(meta, *out, *ready[half::2])
+            )(meta, *out, *pieces)
         ]
     return out[0]
 

time: 72.7 us -> 71.2 us (0.979)
  waiting for transfers between devices: 33.2 us -> 28.9 us
  starting transfers between devices: 19.7 us -> 22.2 us
    ppermute x18 -> x19, waiting for transfers between devices: 10.7 us -> 6.66 us  [swap(): return lax.ppermute(array, 'head', [(i, i ^ step) for i in range(n_head)])]
    ppermute x18 -> x19, starting transfers between devices: 14.8 us -> 17.4 us  [swap(): return lax.ppermute(array, 'head', [(i, i ^ step) for i in range(n_head)])]
  transfers between devices with their start and end apart: 23 -> 24, of which waited for: 15 -> 13; matrix products, arithmetic and copies ran while one was open for 0% -> 0% of each run, Pallas kernels for 12% -> 13%
where the time goes in v6:
time: 71.2 us; the launch traced here: 70.8 us
  waiting for transfers between devices  28.9 us (41%)
  starting transfers between devices  22.2 us (31%)
  Pallas kernels  18.6 us (26%)
  between operations  1 us (1%)
    ppermute x19, starting transfers between devices, swap(): return lax.ppermute(array, 'head', [(i, i ^ step) for i in range(n_head)])  17.4 us
    ppermute x3, waiting for transfers between devices, body(): lax.ppermute(fresh, 'queue', [(i, (i - 1) % n_queue) for i in range(n_que...  14.6 us
    ppermute x1, waiting for transfers between devices, body(): cross = lax.ppermute(kv, ('queue', 'head'), route)  7.66 us
    ppermute x19, waiting for transfers between devices, swap(): return lax.ppermute(array, 'head', [(i, i ^ step) for i in range(n_head)])  6.66 us
    pallas_call x1, Pallas kernels, body(): pl.pallas_call(near_kernel, out_shape=(shape((rows, size), BF16),) + (sha...  5.14 us
    pallas_call x1, Pallas kernels, body(): pl.pallas_call(keys_kernel, out_shape=(shape((2, rows, size), BF16), shap...  4.81 us
    ppermute x1, starting transfers between devices, body(): cross = lax.ppermute(kv, ('queue', 'head'), route)  3.88 us
    pallas_call x1, Pallas kernels, body(): pl.pallas_call(join_kernel, out_shape=tuple((shape((n, part, size), BF16)...  3.36 us
  transfers between devices with their start and end apart: 24, of which 13 were waited for; matrix products, arithmetic and copies ran while one was open for 0% of the time, Pallas kernels for 13%

profile of v6, /device:TPU:89, one launch (start us, length us, event | category | flops | bytes accessed | tf_op | source)
XLA Modules:
  0.0 70.8 jit_solution(2117699491675868163)
XLA Ops:
  0.7 4.8 %shard_map.73 = (bf16[2,288,384]{2,1,0:T(8,128)(2,1)S(1)}, f32[1,9216]{1,0:T(1,128)S(1)}) custom-call(s32[1]{0:T(128)S(6)} %copy.10.level_ref, bf16[288,3072]{1,0:T(8,128)(2,1)} %x_ref.5, f32[16,9216]{1,0:T(8,128)} %mod_hbm.1, bf16[3,3072,384]{2,1,0:T(8,128)(2,1)} %bitcast.6), custom_call_target="tpu_custom_call" | custom-call | flops 1358954496 | bytes 4718592 | tf_op jit(solution)/shard_map/pallas_call | solution.py:234
  5.5 0.8 %collective-permute-start = (bf16[2,288,384]{2,1,0:T(8,128)(2,1)S(1)}, bf16[2,288,384]{2,1,0:T(8,128)(2,1)S(1)}, u32[]{:S(2)}, u32[]{:S(2)}) collective-permute-start(bf16[2,288,384]{2,1,0:T(8,128)(2,1)S(1)} %get-tuple-element.24.kv_ref), channel_id=1, source_target_pairs={{0,8},{8,0},{16,24},{24,16},{32,40},{40,32},{48,56},{56,48},{64,72... | collective-permute-start | bytes 1327112 | tf_op jit(solution)/shard_map/ppermute | solution.py:250
  6.3 3.9 %collective-permute-start.1 = (bf16[2,288,384]{2,1,0:T(8,128)(2,1)S(1)}, bf16[2,288,384]{2,1,0:T(8,128)(2,1)S(1)}, u32[]{:S(2)}, u32[]{:S(2)}) collective-permute-start(bf16[2,288,384]{2,1,0:T(8,128)(2,1)S(1)} %get-tuple-element.24.kv_ref), channel_id=1, source_target_pairs={{0,1},{1,0},{2,3},{3,2},{4,5},{5,4},{6,7},{7,6},{8,16},{9,17},{10,... | collective-permute-start | bytes 1327112 | tf_op jit(solution)/shard_map/ppermute | solution.py:257
  10.1 0.1 pad_add_fusion.meta_ref
  10.2 5.1 %shard_map.74 = (bf16[288,384]{1,0:T(8,128)(2,1)S(1)}, f32[288,384]{1,0:T(8,128)S(1)}, f32[288,384]{1,0:T(8,128)S(1)}, f32[288,384]{1,0:T(8,128)S(1)}) custom-call(s32[2]{0:T(128)S(1)} %pad_add_fusion.meta_ref, s32[32]{0:T(128)S(1)} %copy-done.2, s32[2,32]{1,0:T(2,128)S(1)} %bitcast.4, bf16[288,3072]{1,0:T(8,128)(2,1)S(1)} %copy-done, ...), custom_call_target="tpu_custom_call" | custom-call | flops 1 | bytes 1 | tf_op jit(solution)/shard_map/pallas_call | solution.py:259
  15.4 7.7 %collective-permute-done.1.far_ref = bf16[2,288,384]{2,1,0:T(8,128)(2,1)S(1)} collective-permute-done((bf16[2,288,384]{2,1,0:T(8,128)(2,1)S(1)}, bf16[2,288,384]{2,1,0:T(8,128)(2,1)S(1)}, u32[]{:S(2)}, u32[]{:S(2)}) %collective-permute-start.1) | collective-permute-done | bytes 442400 | tf_op jit(solution)/shard_map/ppermute | solution.py:257
  23.1 3.4 %shard_map.75 = (bf16[2,96,384]{2,1,0:T(8,128)(2,1)S(1)}, bf16[2,96,384]{2,1,0:T(8,128)(2,1)S(1)}, bf16[2,96,384]{2,1,0:T(8,128)(2,1)S(1)}, bf16[2,96,384]{2,1,0...) custom-call(s32[2]{0:T(128)S(1)} %pad_add_fusion.meta_ref, ...), custom_call_target="tpu_custom_call" | custom-call | flops 1358954496 | bytes 2359296 | tf_op jit(solution)/shard_map/pallas_call | solution.py:275
  26.4 0.1 collective-permute-start.15
  26.5 2.6 %collective-permute-start.9 = (bf16[2,96,384]{2,1,0:T(8,128)(2,1)S(1)}, bf16[2,96,384]{2,1,0:T(8,128)(2,1)S(1)}, u32[]{:S(2)}, u32[]{:S(2)}) collective-permute-start(bf16[2,96,384]{2,1,0:T(8,128)(2,1)S(1)} %get-tuple-element.36), channel_id=1, source_target_pairs={{0,3},{1,2},{2,1},{3,0},{4,7},{5,6},{6,5},{7,4},{8,11},{9,10},{10,... | collective-permute-start | bytes 442376 | tf_op jit(solution)/shard_map/ppermute | solution.py:232
  29.1 1.4 %collective-permute-start.14 = (bf16[2,96,384]{2,1,0:T(8,128)(2,1)S(1)}, bf16[2,96,384]{2,1,0:T(8,128)(2,1)S(1)}, u32[]{:S(2)}, u32[]{:S(2)}) collective-permute-start(bf16[2,96,384]{2,1,0:T(8,128)(2,1)S(1)} %get-tuple-element.38), channel_id=1, source_target_pairs={{0,4},{1,5},{2,6},{3,7},{4,0},{5,1},{6,2},{7,3},{8,12},{9,13},{10,... | collective-permute-start | bytes 442376 | tf_op jit(solution)/shard_map/ppermute | solution.py:232
  30.5 0.3 collective-permute-done.15.refs_1_
  30.8 2.6 %collective-permute-start.16 = (bf16[2,96,384]{2,1,0:T(8,128)(2,1)S(1)}, bf16[2,96,384]{2,1,0:T(8,128)(2,1)S(1)}, u32[]{:S(2)}, u32[]{:S(2)}) collective-permute-start(bf16[2,96,384]{2,1,0:T(8,128)(2,1)S(1)} %shard_map.83), channel_id=1, source_target_pairs={{0,3},{1,2},{2,1},{3,0},{4,7},{5,6},{6,5},{7,4},{8,11},{9,10},{10,... | collective-permute-start | bytes 442376 | tf_op jit(solution)/shard_map/ppermute | solution.py:232
  33.4 0.2 collective-permute-start.8
  33.6 0.1 collective-permute-start.10
  33.7 0.8 %collective-permute-done.3.refs_1_ = bf16[2,96,384]{2,1,0:T(8,128)(2,1)S(1)} collective-permute-done((bf16[2,96,384]{2,1,0:T(8,128)(2,1)S(1)}, bf16[2,96,384]{2,1,0:T(8,128)(2,1)S(1)}, u32[]{:S(2)}, u32[]{:S(2)}) %collective-permute-start.3) | collective-permute-done | bytes 147488 | tf_op jit(solution)/shard_map/ppermute | solution.py:232
  34.5 0.7 collective-permute-start.2
  35.3 1.3 %collective-permute-start.4 = (bf16[2,96,384]{2,1,0:T(8,128)(2,1)S(1)}, bf16[2,96,384]{2,1,0:T(8,128)(2,1)S(1)}, u32[]{:S(2)}, u32[]{:S(2)}) collective-permute-start(bf16[2,96,384]{2,1,0:T(8,128)(2,1)S(1)} %shard_map.76), channel_id=1, source_target_pairs={{0,4},{1,5},{2,6},{3,7},{4,0},{5,1},{6,2},{7,3},{8,12},{9,13},{10,... | collective-permute-start | bytes 442376 | tf_op jit(solution)/shard_map/ppermute | solution.py:232
  36.5 0.1 shard_map.84.keep_ref
  36.6 1.5 %collective-permute-start.17 = (bf16[2,96,384]{2,1,0:T(8,128)(2,1)S(1)}, bf16[2,96,384]{2,1,0:T(8,128)(2,1)S(1)}, u32[]{:S(2)}, u32[]{:S(2)}) collective-permute-start(bf16[2,96,384]{2,1,0:T(8,128)(2,1)S(1)} %shard_map.84.keep_ref), channel_id=1, source_target_pairs={{0,1},{1,0},{2,3},{3,2},{4,5},{5,4},{6,7},{7,6},{8,9},{9,8},{10,11... | collective-permute-start | bytes 442376 | tf_op jit(solution)/shard_map/ppermute | solution.py:232
  38.1 0.5 collective-permute-done.8.refs_1_
  38.6 0.1 shard_map.80.keep_ref
  38.7 0.4 collective-permute-start.11
  39.0 0.3 collective-permute-done.2.refs_1_
  39.3 0.0 collective-permute-done.4.refs_2_
  39.3 0.1 shard_map.77.keep_ref
  39.4 2.9 %collective-permute-start.5 = (bf16[2,96,384]{2,1,0:T(8,128)(2,1)S(1)}, bf16[2,96,384]{2,1,0:T(8,128)(2,1)S(1)}, u32[]{:S(2)}, u32[]{:S(2)}) collective-permute-start(bf16[2,96,384]{2,1,0:T(8,128)(2,1)S(1)} %shard_map.77.keep_ref), channel_id=1, source_target_pairs={{0,3},{1,2},{2,1},{3,0},{4,7},{5,6},{6,5},{7,4},{8,11},{9,10},{10,... | collective-permute-start | bytes 442376 | tf_op jit(solution)/shard_map/ppermute | solution.py:232
  42.3 0.6 shard_map.85
  42.9 0.1 collective-permute-start.18
  43.0 0.6 shard_map.81
  43.6 0.1 collective-permute-start.12
  43.7 1.1 %collective-permute-done.5.got_ref = bf16[2,96,384]{2,1,0:T(8,128)(2,1)S(1)} collective-permute-done((bf16[2,96,384]{2,1,0:T(8,128)(2,1)S(1)}, bf16[2,96,384]{2,1,0:T(8,128)(2,1)S(1)}, u32[]{:S(2)}, u32[]{:S(2)}) %collective-permute-start.5) | collective-permute-done | bytes 147488 | tf_op jit(solution)/shard_map/ppermute | solution.py:232
  44.8 0.6 shard_map.78
  45.4 0.1 collective-permute-start.6
  45.5 10.1 %collective-permute-done.18.a_ref = bf16[2,96,384]{2,1,0:T(8,128)(2,1)S(1)} collective-permute-done((bf16[2,96,384]{2,1,0:T(8,128)(2,1)S(1)}, bf16[2,96,384]{2,1,0:T(8,128)(2,1)S(1)}, u32[]{:S(2)}, u32[]{:S(2)}) %collective-permute-start.18) | collective-permute-done | bytes 147488 | tf_op jit(solution)/shard_map/ppermute | solution.py:328
  55.7 2.2 %collective-permute-done.12.a_ref = bf16[2,96,384]{2,1,0:T(8,128)(2,1)S(1)} collective-permute-done((bf16[2,96,384]{2,1,0:T(8,128)(2,1)S(1)}, bf16[2,96,384]{2,1,0:T(8,128)(2,1)S(1)}, u32[]{:S(2)}, u32[]{:S(2)}) %collective-permute-start.12) | collective-permute-done | bytes 147488 | tf_op jit(solution)/shard_map/ppermute | solution.py:328
  57.9 0.5 collective-permute-start.13
  58.4 2.2 %collective-permute-done.6.refs_0_ = bf16[2,96,384]{2,1,0:T(8,128)(2,1)S(1)} collective-permute-done((bf16[2,96,384]{2,1,0:T(8,128)(2,1)S(1)}, bf16[2,96,384]{2,1,0:T(8,128)(2,1)S(1)}, u32[]{:S(2)}, u32[]{:S(2)}) %collective-permute-start.6) | collective-permute-done | bytes 147488 | tf_op jit(solution)/shard_map/ppermute | solution.py:328
  60.6 1.4 %collective-permute-start.7 = (bf16[2,96,384]{2,1,0:T(8,128)(2,1)S(1)}, bf16[2,96,384]{2,1,0:T(8,128)(2,1)S(1)}, u32[]{:S(2)}, u32[]{:S(2)}) collective-permute-start(bf16[2,96,384]{2,1,0:T(8,128)(2,1)S(1)} %collective-permute-done.6.refs_0_), channel_id=1, source_target_pairs={{0,4},{1,5},{2,6},{3,7},{4,0},{5,1},{6,2},{7,3},{8,12},{9,13},{10,... | collective-permute-start | bytes 442376 | tf_op jit(solution)/shard_map/ppermute | solution.py:232
  62.1 0.1 collective-permute-start.23
  62.3 0.9 %collective-permute-start.22 = (bf16[4,96,384]{2,1,0:T(8,128)(2,1)S(1)}, bf16[4,96,384]{2,1,0:T(8,128)(2,1)S(1)}, u32[]{:S(2)}, u32[]{:S(2)}) collective-permute-start(bf16[4,96,384]{2,1,0:T(8,128)(2,1)S(1)} %shard_map.82.refs_2_), channel_id=1, source_target_pairs={{0,3},{1,2},{2,1},{3,0},{4,7},{5,6},{6,5},{7,4},{8,11},{9,10},{10,... | collective-permute-start | bytes 884744 | tf_op jit(solution)/shard_map/ppermute | solution.py:232
  63.2 0.3 collective-permute-start.20
  63.5 1.2 %collective-permute-done.7.refs_1_ = bf16[2,96,384]{2,1,0:T(8,128)(2,1)S(1)} collective-permute-done((bf16[2,96,384]{2,1,0:T(8,128)(2,1)S(1)}, bf16[2,96,384]{2,1,0:T(8,128)(2,1)S(1)}, u32[]{:S(2)}, u32[]{:S(2)}) %collective-permute-start.7) | collective-permute-done | bytes 147488 | tf_op jit(solution)/shard_map/ppermute | solution.py:232
  64.6 0.4 collective-permute-start.21
  65.1 1.5 %shard_map.87.refs_0_ = bf16[288,3072]{1,0:T(8,128)(2,1)} custom-call(s32[2]{0:T(128)S(1)} %pad_add_fusion.meta_ref, bf16[2,96,384]{2,1,0:T(8,128)(2,1)S(1)} %collective-permute-done.6.refs_0_, bf16[2,96,384]{2,1,0:T(8,128)(2,1)S(1)} %collective-permute-done.7.refs_1_, bf16[4,96,384]{2,1,0:T(8,128)(2,1)S(1)} %shard_map.82.refs_2_, ...), custom_call_target="tpu_custom_call" | custom-call | flops 147456 | bytes 294912 | tf_op jit(solution)/shard_map/pallas_call | solution.py:350
  66.6 0.6 collective-permute-done.20.refs_1_
  67.2 1.6 %collective-permute-done.21.refs_2_ = bf16[2,96,384]{2,1,0:T(8,128)(2,1)S(1)} collective-permute-done((bf16[2,96,384]{2,1,0:T(8,128)(2,1)S(1)}, bf16[2,96,384]{2,1,0:T(8,128)(2,1)S(1)}, u32[]{:S(2)}, u32[]{:S(2)}) %collective-permute-start.21) | collective-permute-done | bytes 147488 | tf_op jit(solution)/shard_map/ppermute | solution.py:232
  68.7 0.4 collective-permute-done.22.refs_3_
  69.1 1.6 %shard_map.88 = bf16[288,3072]{1,0:T(8,128)(2,1)} custom-call(s32[2]{0:T(128)S(1)} %pad_add_fusion.meta_ref, bf16[288,3072]{1,0:T(8,128)(2,1)} %shard_map.87.refs_0_, bf16[2,96,384]{2,1,0:T(8,128)(2,1)S(1)} %collective-permute-done.20.refs_1_, bf16[2,96,384]{2,1,0:T(8,128)(2,1)S(1)} %collective-permute-done.21.refs_2_, ...), custom_call_target="tpu_custom_call", output_to_operand_aliasing={{}: (1, {})} | custom-call | flops 147456 | bytes 294912 | tf_op jit(solution)/shard_map/pallas_call | solution.py:350
  (25 shorter events, 0.2 us)
Async XLA Ops:
  0.7 9.6 %copy-start = (bf16[288,3072]{1,0:T(8,128)(2,1)S(1)}, bf16[288,3072]{1,0:T(8,128)(2,1)}, u32[]{:S(2)}) copy-start(bf16[288,3072]{1,0:T(8,128)(2,1)} %x_ref.5) | copy-start | bytes 5308420
  0.7 9.6 %copy-start.1 = (s32[32,2]{0,1:T(2,128)S(1)}, s32[32,2]{0,1:T(2,128)}, u32[]{:S(2)}) copy-start(s32[32,2]{0,1:T(2,128)} %param.10) | copy-start | bytes 772
  0.7 9.5 %copy-start.2 = (s32[32]{0:T(128)S(1)}, s32[32]{0:T(128)}, u32[]{:S(2)}) copy-start(s32[32]{0:T(128)} %counts_ref.3) | copy-start | bytes 388
  5.5 4.7 %collective-permute-start = (bf16[2,288,384]{2,1,0:T(8,128)(2,1)S(1)}, bf16[2,288,384]{2,1,0:T(8,128)(2,1)S(1)}, u32[]{:S(2)}, u32[]{:S(2)}) collective-permute-start(bf16[2,288,384]{2,1,0:T(8,128)(2,1)S(1)} %get-tuple-element.24.kv_ref), channel_id=1, source_target_pairs={{0,8},{8,0},{16,24},{24,16},{32,40},{40,32},{48,56},{56,48},{64,72... | collective-permute-start | bytes 1327112 | tf_op jit(solution)/shard_map/ppermute | solution.py:250
  6.3 16.8 %collective-permute-start.1 = (bf16[2,288,384]{2,1,0:T(8,128)(2,1)S(1)}, bf16[2,288,384]{2,1,0:T(8,128)(2,1)S(1)}, u32[]{:S(2)}, u32[]{:S(2)}) collective-permute-start(bf16[2,288,384]{2,1,0:T(8,128)(2,1)S(1)} %get-tuple-element.24.kv_ref), channel_id=1, source_target_pairs={{0,1},{1,0},{2,3},{3,2},{4,5},{5,4},{6,7},{7,6},{8,16},{9,17},{10,... | collective-permute-start | bytes 1327112 | tf_op jit(solution)/shard_map/ppermute | solution.py:257
  10.2 12.8 %copy-start.3 = (bf16[384,3072]{1,0:T(8,128)(2,1)S(1)}, bf16[384,3072]{1,0:T(8,128)(2,1)}, u32[]{:S(2)}) copy-start(bf16[384,3072]{1,0:T(8,128)(2,1)} %w_ref.1) | copy-start | bytes 7077892
  26.4 4.4 %collective-permute-start.15 = (bf16[2,96,384]{2,1,0:T(8,128)(2,1)S(1)}, bf16[2,96,384]{2,1,0:T(8,128)(2,1)S(1)}, u32[]{:S(2)}, u32[]{:S(2)}) collective-permute-start(bf16[2,96,384]{2,1,0:T(8,128)(2,1)S(1)} %get-tuple-element.40), channel_id=1, source_target_pairs={{0,4},{1,5},{2,6},{3,7},{4,0},{5,1},{6,2},{7,3},{8,12},{9,13},{10,... | collective-permute-start | bytes 442376 | tf_op jit(solution)/shard_map/ppermute | solution.py:232
  26.5 7.1 %collective-permute-start.9 = (bf16[2,96,384]{2,1,0:T(8,128)(2,1)S(1)}, bf16[2,96,384]{2,1,0:T(8,128)(2,1)S(1)}, u32[]{:S(2)}, u32[]{:S(2)}) collective-permute-start(bf16[2,96,384]{2,1,0:T(8,128)(2,1)S(1)} %get-tuple-element.36), channel_id=1, source_target_pairs={{0,3},{1,2},{2,1},{3,0},{4,7},{5,6},{6,5},{7,4},{8,11},{9,10},{10,... | collective-permute-start | bytes 442376 | tf_op jit(solution)/shard_map/ppermute | solution.py:232
  29.1 5.4 %collective-permute-start.3 = (bf16[2,96,384]{2,1,0:T(8,128)(2,1)S(1)}, bf16[2,96,384]{2,1,0:T(8,128)(2,1)S(1)}, u32[]{:S(2)}, u32[]{:S(2)}) collective-permute-start(bf16[2,96,384]{2,1,0:T(8,128)(2,1)S(1)} %get-tuple-element.32), channel_id=1, source_target_pairs={{0,1},{1,0},{2,3},{3,2},{4,5},{5,4},{6,7},{7,6},{8,9},{9,8},{10,11... | collective-permute-start | bytes 442376 | tf_op jit(solution)/shard_map/ppermute | solution.py:232
  29.1 6.2 %collective-permute-start.14 = (bf16[2,96,384]{2,1,0:T(8,128)(2,1)S(1)}, bf16[2,96,384]{2,1,0:T(8,128)(2,1)S(1)}, u32[]{:S(2)}, u32[]{:S(2)}) collective-permute-start(bf16[2,96,384]{2,1,0:T(8,128)(2,1)S(1)} %get-tuple-element.38), channel_id=1, source_target_pairs={{0,4},{1,5},{2,6},{3,7},{4,0},{5,1},{6,2},{7,3},{8,12},{9,13},{10,... | collective-permute-start | bytes 442376 | tf_op jit(solution)/shard_map/ppermute | solution.py:232
  30.8 5.7 %collective-permute-start.16 = (bf16[2,96,384]{2,1,0:T(8,128)(2,1)S(1)}, bf16[2,96,384]{2,1,0:T(8,128)(2,1)S(1)}, u32[]{:S(2)}, u32[]{:S(2)}) collective-permute-start(bf16[2,96,384]{2,1,0:T(8,128)(2,1)S(1)} %shard_map.83), channel_id=1, source_target_pairs={{0,3},{1,2},{2,1},{3,0},{4,7},{5,6},{6,5},{7,4},{8,11},{9,10},{10,... | collective-permute-start | bytes 442376 | tf_op jit(solution)/shard_map/ppermute | solution.py:232
  33.4 5.2 %collective-permute-start.8 = (bf16[2,96,384]{2,1,0:T(8,128)(2,1)S(1)}, bf16[2,96,384]{2,1,0:T(8,128)(2,1)S(1)}, u32[]{:S(2)}, u32[]{:S(2)}) collective-permute-start(bf16[2,96,384]{2,1,0:T(8,128)(2,1)S(1)} %get-tuple-element.34), channel_id=1, source_target_pairs={{0,3},{1,2},{2,1},{3,0},{4,7},{5,6},{6,5},{7,4},{8,11},{9,10},{10,... | collective-permute-start | bytes 442376 | tf_op jit(solution)/shard_map/ppermute | solution.py:232
  33.6 5.0 %collective-permute-start.10 = (bf16[2,96,384]{2,1,0:T(8,128)(2,1)S(1)}, bf16[2,96,384]{2,1,0:T(8,128)(2,1)S(1)}, u32[]{:S(2)}, u32[]{:S(2)}) collective-permute-start(bf16[2,96,384]{2,1,0:T(8,128)(2,1)S(1)} %shard_map.79), channel_id=1, source_target_pairs={{0,1},{1,0},{2,3},{3,2},{4,5},{5,4},{6,7},{7,6},{8,9},{9,8},{10,11... | collective-permute-start | bytes 442376 | tf_op jit(solution)/shard_map/ppermute | solution.py:232
  34.5 4.8 %collective-permute-start.2 = (bf16[2,96,384]{2,1,0:T(8,128)(2,1)S(1)}, bf16[2,96,384]{2,1,0:T(8,128)(2,1)S(1)}, u32[]{:S(2)}, u32[]{:S(2)}) collective-permute-start(bf16[2,96,384]{2,1,0:T(8,128)(2,1)S(1)} %get-tuple-element.30), channel_id=1, source_target_pairs={{0,1},{1,0},{2,3},{3,2},{4,5},{5,4},{6,7},{7,6},{8,9},{9,8},{10,11... | collective-permute-start | bytes 442376 | tf_op jit(solution)/shard_map/ppermute | solution.py:232
  35.3 4.1 %collective-permute-start.4 = (bf16[2,96,384]{2,1,0:T(8,128)(2,1)S(1)}, bf16[2,96,384]{2,1,0:T(8,128)(2,1)S(1)}, u32[]{:S(2)}, u32[]{:S(2)}) collective-permute-start(bf16[2,96,384]{2,1,0:T(8,128)(2,1)S(1)} %shard_map.76), channel_id=1, source_target_pairs={{0,4},{1,5},{2,6},{3,7},{4,0},{5,1},{6,2},{7,3},{8,12},{9,13},{10,... | collective-permute-start | bytes 442376 | tf_op jit(solution)/shard_map/ppermute | solution.py:232
  36.6 5.7 %collective-permute-start.17 = (bf16[2,96,384]{2,1,0:T(8,128)(2,1)S(1)}, bf16[2,96,384]{2,1,0:T(8,128)(2,1)S(1)}, u32[]{:S(2)}, u32[]{:S(2)}) collective-permute-start(bf16[2,96,384]{2,1,0:T(8,128)(2,1)S(1)} %shard_map.84.keep_ref), channel_id=1, source_target_pairs={{0,1},{1,0},{2,3},{3,2},{4,5},{5,4},{6,7},{7,6},{8,9},{9,8},{10,11... | collective-permute-start | bytes 442376 | tf_op jit(solution)/shard_map/ppermute | solution.py:232
  38.7 4.3 %collective-permute-start.11 = (bf16[2,96,384]{2,1,0:T(8,128)(2,1)S(1)}, bf16[2,96,384]{2,1,0:T(8,128)(2,1)S(1)}, u32[]{:S(2)}, u32[]{:S(2)}) collective-permute-start(bf16[2,96,384]{2,1,0:T(8,128)(2,1)S(1)} %shard_map.80.keep_ref), channel_id=1, source_target_pairs={{0,4},{1,5},{2,6},{3,7},{4,0},{5,1},{6,2},{7,3},{8,12},{9,13},{10,... | collective-permute-start | bytes 442376 | tf_op jit(solution)/shard_map/ppermute | solution.py:232
  39.4 5.4 %collective-permute-start.5 = (bf16[2,96,384]{2,1,0:T(8,128)(2,1)S(1)}, bf16[2,96,384]{2,1,0:T(8,128)(2,1)S(1)}, u32[]{:S(2)}, u32[]{:S(2)}) collective-permute-start(bf16[2,96,384]{2,1,0:T(8,128)(2,1)S(1)} %shard_map.77.keep_ref), channel_id=1, source_target_pairs={{0,3},{1,2},{2,1},{3,0},{4,7},{5,6},{6,5},{7,4},{8,11},{9,10},{10,... | collective-permute-start | bytes 442376 | tf_op jit(solution)/shard_map/ppermute | solution.py:232
  42.9 12.8 %collective-permute-start.18 = (bf16[2,96,384]{2,1,0:T(8,128)(2,1)S(1)}, bf16[2,96,384]{2,1,0:T(8,128)(2,1)S(1)}, u32[]{:S(2)}, u32[]{:S(2)}) collective-permute-start(bf16[2,96,384]{2,1,0:T(8,128)(2,1)S(1)} %shard_map.85), channel_id=1, source_target_pairs={{0,248},{8,0},{16,8},{24,16},{32,24},{40,32},{48,40},{56,48},{64,5... | collective-permute-start | bytes 442376 | tf_op jit(solution)/shard_map/ppermute | solution.py:328
  43.6 14.2 %collective-permute-start.12 = (bf16[2,96,384]{2,1,0:T(8,128)(2,1)S(1)}, bf16[2,96,384]{2,1,0:T(8,128)(2,1)S(1)}, u32[]{:S(2)}, u32[]{:S(2)}) collective-permute-start(bf16[2,96,384]{2,1,0:T(8,128)(2,1)S(1)} %shard_map.81), channel_id=1, source_target_pairs={{0,248},{8,0},{16,8},{24,16},{32,24},{40,32},{48,40},{56,48},{64,5... | collective-permute-start | bytes 442376 | tf_op jit(solution)/shard_map/ppermute | solution.py:328
  45.4 15.2 %collective-permute-start.6 = (bf16[2,96,384]{2,1,0:T(8,128)(2,1)S(1)}, bf16[2,96,384]{2,1,0:T(8,128)(2,1)S(1)}, u32[]{:S(2)}, u32[]{:S(2)}) collective-permute-start(bf16[2,96,384]{2,1,0:T(8,128)(2,1)S(1)} %shard_map.78), channel_id=1, source_target_pairs={{0,248},{8,0},{16,8},{24,16},{32,24},{40,32},{48,40},{56,48},{64,5... | collective-permute-start | bytes 442376 | tf_op jit(solution)/shard_map/ppermute | solution.py:328
  55.6 6.4 %collective-permute-start.19 = (bf16[2,96,384]{2,1,0:T(8,128)(2,1)S(1)}, bf16[2,96,384]{2,1,0:T(8,128)(2,1)S(1)}, u32[]{:S(2)}, u32[]{:S(2)}) collective-permute-start(bf16[2,96,384]{2,1,0:T(8,128)(2,1)S(1)} %collective-permute-done.18.a_ref), channel_id=1, source_target_pairs={{0,3},{1,2},{2,1},{3,0},{4,7},{5,6},{6,5},{7,4},{8,11},{9,10},{10,... | collective-permute-start | bytes 442376 | tf_op jit(solution)/shard_map/ppermute | solution.py:232
  57.9 4.4 %collective-permute-start.13 = (bf16[2,96,384]{2,1,0:T(8,128)(2,1)S(1)}, bf16[2,96,384]{2,1,0:T(8,128)(2,1)S(1)}, u32[]{:S(2)}, u32[]{:S(2)}) collective-permute-start(bf16[2,96,384]{2,1,0:T(8,128)(2,1)S(1)} %collective-permute-done.12.a_ref), channel_id=1, source_target_pairs={{0,1},{1,0},{2,3},{3,2},{4,5},{5,4},{6,7},{7,6},{8,9},{9,8},{10,11... | collective-permute-start | bytes 442376 | tf_op jit(solution)/shard_map/ppermute | solution.py:232
  60.6 4.0 %collective-permute-start.7 = (bf16[2,96,384]{2,1,0:T(8,128)(2,1)S(1)}, bf16[2,96,384]{2,1,0:T(8,128)(2,1)S(1)}, u32[]{:S(2)}, u32[]{:S(2)}) collective-permute-start(bf16[2,96,384]{2,1,0:T(8,128)(2,1)S(1)} %collective-permute-done.6.refs_0_), channel_id=1, source_target_pairs={{0,4},{1,5},{2,6},{3,7},{4,0},{5,1},{6,2},{7,3},{8,12},{9,13},{10,... | collective-permute-start | bytes 442376 | tf_op jit(solution)/shard_map/ppermute | solution.py:232
  62.1 6.6 %collective-permute-start.23 = (bf16[4,96,384]{2,1,0:T(8,128)(2,1)S(1)}, bf16[4,96,384]{2,1,0:T(8,128)(2,1)S(1)}, u32[]{:S(2)}, u32[]{:S(2)}) collective-permute-start(bf16[4,96,384]{2,1,0:T(8,128)(2,1)S(1)} %shard_map.86.refs_3_), channel_id=1, source_target_pairs={{0,4},{1,5},{2,6},{3,7},{4,0},{5,1},{6,2},{7,3},{8,12},{9,13},{10,... | collective-permute-start | bytes 884744 | tf_op jit(solution)/shard_map/ppermute | solution.py:232
  62.3 6.9 %collective-permute-start.22 = (bf16[4,96,384]{2,1,0:T(8,128)(2,1)S(1)}, bf16[4,96,384]{2,1,0:T(8,128)(2,1)S(1)}, u32[]{:S(2)}, u32[]{:S(2)}) collective-permute-start(bf16[4,96,384]{2,1,0:T(8,128)(2,1)S(1)} %shard_map.82.refs_2_), channel_id=1, source_target_pairs={{0,3},{1,2},{2,1},{3,0},{4,7},{5,6},{6,5},{7,4},{8,11},{9,10},{10,... | collective-permute-start | bytes 884744 | tf_op jit(solution)/shard_map/ppermute | solution.py:232
  63.2 4.0 %collective-permute-start.20 = (bf16[2,96,384]{2,1,0:T(8,128)(2,1)S(1)}, bf16[2,96,384]{2,1,0:T(8,128)(2,1)S(1)}, u32[]{:S(2)}, u32[]{:S(2)}) collective-permute-start(bf16[2,96,384]{2,1,0:T(8,128)(2,1)S(1)} %collective-permute-done.6.refs_0_), channel_id=1, source_target_pairs={{0,1},{1,0},{2,3},{3,2},{4,5},{5,4},{6,7},{7,6},{8,9},{9,8},{10,11... | collective-permute-start | bytes 442376 | tf_op jit(solution)/shard_map/ppermute | solution.py:232
  64.6 4.1 %collective-permute-start.21 = (bf16[2,96,384]{2,1,0:T(8,128)(2,1)S(1)}, bf16[2,96,384]{2,1,0:T(8,128)(2,1)S(1)}, u32[]{:S(2)}, u32[]{:S(2)}) collective-permute-start(bf16[2,96,384]{2,1,0:T(8,128)(2,1)S(1)} %collective-permute-done.7.refs_1_), channel_id=1, source_target_pairs={{0,1},{1,0},{2,3},{3,2},{4,5},{5,4},{6,7},{7,6},{8,9},{9,8},{10,11... | collective-permute-start | bytes 442376 | tf_op jit(solution)/shard_map/ppermute | solution.py:232
